TPU v7x, 32 devices: a whole 2x2x4 slice. The times are simulated.
32 devices in a mesh: dp: 8 (over y, x, core), tensor: 4 (over z).
Axes of the slice: x: 2, y: 2, z: 4, core: 2. Of those that a mesh axis runs over, the one named last changes fastest.
Arguments:
- codes: int32 [16, 1024], P('dp'), may hold values from 0 to 1023
- doc_lengths: int32 [16, 3], P('dp'), may hold values from 1 to 896, 1024 in all within a row
- loss_mask: int32 [16, 1024], P('dp'), may hold values from 0 to 1
- qkv_master: float32 [1024, 3, 1024], P('dp', None, 'tensor'), may hold values from -0.1875 to 0.1875
- qkv_first: float32 [1024, 3, 1024], P('dp', None, 'tensor'), may hold values from -3.33786e-06 to 3.33786e-06
- qkv_second: float32 [1024, 3, 1024], P('dp', None, 'tensor'), may hold values from 2.7238338e-13 to 1.0895335e-12
- out_master: float32 [1024, 1024], P('tensor', 'dp'), may hold values from -1.5 to 1.5
- out_first: float32 [1024, 1024], P('tensor', 'dp'), may hold values from -3.33786e-06 to 3.33786e-06
- out_second: float32 [1024, 1024], P('tensor', 'dp'), may hold values from 2.7238338e-13 to 1.0895335e-12
- up_master: float32 [1024, 4096], P('dp', 'tensor'), may hold values from -0.1875 to 0.1875
- up_first: float32 [1024, 4096], P('dp', 'tensor'), may hold values from -3.33786e-06 to 3.33786e-06
- up_second: float32 [1024, 4096], P('dp', 'tensor'), may hold values from 2.7238338e-13 to 1.0895335e-12
- down_master: float32 [4096, 1024], P('tensor', 'dp'), may hold values from -0.09375 to 0.09375
- down_first: float32 [4096, 1024], P('tensor', 'dp'), may hold values from -3.33786e-06 to 3.33786e-06
- down_second: float32 [4096, 1024], P('tensor', 'dp'), may hold values from 2.7238338e-13 to 1.0895335e-12
- table_master: float32 [2, 1025, 1024], P(None, None, ('dp', 'tensor')), may hold values from -0.375 to 0.375
- table_first: float32 [2, 1025, 1024], P(None, None, ('dp', 'tensor')), may hold values from -3.33786e-06 to 3.33786e-06
- table_second: float32 [2, 1025, 1024], P(None, None, ('dp', 'tensor')), may hold values from 2.7238338e-13 to 1.0895335e-12
- gain_master: float32 [3, 1024], P(None, ('dp', 'tensor')), may hold values from 0.3 to 2.1, as said below
- gain_first: float32 [3, 1024], P(None, ('dp', 'tensor')), may hold values from -3.0517578e-05 to 3.0517578e-05
- gain_second: float32 [3, 1024], P(None, ('dp', 'tensor')), may hold values from 2.7238338e-11 to 1.0895335e-10
Outputs:
- qkv_new: float32 [1024, 3, 1024], P('dp', None, 'tensor')
- qkv_first_new: float32 [1024, 3, 1024], P('dp', None, 'tensor')
- qkv_second_new: float32 [1024, 3, 1024], P('dp', None, 'tensor')
- qkv_copy: bfloat16 [1024, 3, 1024], P('dp', None, 'tensor')
- out_new: float32 [1024, 1024], P('tensor', 'dp')
- out_first_new: float32 [1024, 1024], P('tensor', 'dp')
- out_second_new: float32 [1024, 1024], P('tensor', 'dp')
- out_copy: bfloat16 [1024, 1024], P('tensor', 'dp')
- up_new: float32 [1024, 4096], P('dp', 'tensor')
- up_first_new: float32 [1024, 4096], P('dp', 'tensor')
- up_second_new: float32 [1024, 4096], P('dp', 'tensor')
- up_copy: bfloat16 [1024, 4096], P('dp', 'tensor')
- down_new: float32 [4096, 1024], P('tensor', 'dp')
- down_first_new: float32 [4096, 1024], P('tensor', 'dp')
- down_second_new: float32 [4096, 1024], P('tensor', 'dp')
- down_copy: bfloat16 [4096, 1024], P('tensor', 'dp')
- table_new: float32 [2, 1025, 1024], P(None, None, ('dp', 'tensor'))
- table_first_new: float32 [2, 1025, 1024], P(None, None, ('dp', 'tensor'))
- table_second_new: float32 [2, 1025, 1024], P(None, None, ('dp', 'tensor'))
- table_copy: bfloat16 [2, 1025, 1024], P(None, None, ('dp', 'tensor'))
- gain_new: float32 [3, 1024], P(None, ('dp', 'tensor'))
- gain_first_new: float32 [3, 1024], P(None, ('dp', 'tensor'))
- gain_second_new: float32 [3, 1024], P(None, ('dp', 'tensor'))
- gain_copy: bfloat16 [3, 1024], P(None, ('dp', 'tensor'))
- loss_total: float32 [], replicated
- count_total: float32 [], replicated
- grad_norm: float32 [], replicated
Inputs may be any that keep to these rules, and one draw needn't show every extreme that they name: `gain_master`: positive gains.
All inputs are finite; a program needn't handle non-finite values.
Results may differ from a plain program's by a relative error of at most 0.0086.
Values may be sent and summed in bfloat16 or wider, within the bound.
No kernel may reach another device: no remote copies, remote signals or barrier semaphores. Data moves between devices by JAX's collectives and lax.ppermute only.
A program may use at most 192 MiB of HBM per device.

v0:
```python
from functools import partial
import math

import jax
import jax.numpy as jnp
from jax import lax
from jax.sharding import PartitionSpec as P

HEAD = 64
STEP = 5


RATE_MATRIX = 0.03
RATE_GAIN = 0.25
DECAY_RATE = 0.01
CLIP_NORM = 0.002
NORM_EPS = 1e-05
ADAM_EPS = 1e-08


def layer_norm(values, gain_vec):
    mean_val = jnp.mean(values, -1, keepdims=True)
    centered = values - mean_val
    inverse = lax.rsqrt(jnp.mean(centered * centered, -1, keepdims=True) + NORM_EPS)
    normed = centered * inverse
    return (normed * gain_vec, normed, inverse)


def norm_back(grad_out, normed, inverse, gain_vec):
    grad_normed = grad_out * gain_vec
    grad_in = inverse * (
        grad_normed
        - jnp.mean(grad_normed, -1, keepdims=True)
        - normed * jnp.mean(grad_normed * normed, -1, keepdims=True)
    )
    return (grad_in, jnp.sum(grad_out * normed, 0))


def doc_layout(lengths_row, total_rows):
    places = jnp.arange(total_rows, dtype=jnp.int32)
    bound_one = lengths_row[0]
    bound_two = lengths_row[0] + lengths_row[1]
    doc_ids = (places >= bound_one).astype(jnp.int32) + (places >= bound_two).astype(jnp.int32)
    starts = jnp.where(doc_ids == 0, 0, jnp.where(doc_ids == 1, bound_one, bound_two))
    return (doc_ids, places - starts)


def next_codes(codes_row, doc_ids, end_code):
    later = jnp.concatenate([codes_row[1:], jnp.full((1,), end_code, jnp.int32)])
    later_doc = jnp.concatenate([doc_ids[1:], jnp.full((1,), -1, jnp.int32)])
    return jnp.where(later_doc == doc_ids, later, end_code)


def position_code(local_pos, width):
    halves = jnp.arange(width // 2).astype(jnp.float32)
    freqs = jnp.exp(halves * (-2.0 * math.log(10000.0) / width))
    angles = local_pos.astype(jnp.float32)[:, None] * freqs[None, :]
    return jnp.stack([jnp.sin(angles), jnp.cos(angles)], -1).reshape(local_pos.shape[0], width)


def allowed_block(doc_ids, first_row, block_rows):
    total_rows = doc_ids.shape[0]
    row_pos = first_row + jnp.arange(block_rows, dtype=jnp.int32)
    col_pos = jnp.arange(total_rows, dtype=jnp.int32)
    row_doc = lax.dynamic_slice_in_dim(doc_ids, first_row, block_rows, 0)
    return (col_pos[None, :] <= row_pos[:, None]) & (doc_ids[None, :] == row_doc[:, None])


def block_scores(q_block, keys, allowed):
    scores = jnp.einsum(
        "bhe,khe->hbk", q_block, keys, preferred_element_type=jnp.float32
    ) * q_block.shape[-1] ** (-0.5)
    return jnp.where(allowed[None], scores, -1e30)


def attend(query, keys, values, doc_ids, block_rows):

    def one_block(block_index):
        first_row = block_index * block_rows
        q_block = lax.dynamic_slice_in_dim(query, first_row, block_rows, 0)
        scores = block_scores(q_block, keys, allowed_block(doc_ids, first_row, block_rows))
        top_score = jnp.max(scores, -1, keepdims=True)
        expo = jnp.exp(scores - top_score)
        totals = jnp.sum(expo, -1, keepdims=True)
        probs = (expo / totals).astype(jnp.bfloat16)
        mixed = jnp.einsum("hbk,khe->bhe", probs, values, preferred_element_type=jnp.float32)
        return (mixed.astype(jnp.bfloat16), (top_score + jnp.log(totals))[..., 0])

    mixed, logsum = lax.map(one_block, jnp.arange(query.shape[0] // block_rows, dtype=jnp.int32))
    return (mixed.reshape(query.shape), logsum)


def attend_back(query, keys, values, grad_mixed, logsum, doc_ids, block_rows):
    scale_factor = query.shape[-1] ** (-0.5)

    def one_block(carry, block_index):
        grad_keys, grad_values = carry
        first_row = block_index * block_rows
        q_block = lax.dynamic_slice_in_dim(query, first_row, block_rows, 0)
        g_block = lax.dynamic_slice_in_dim(grad_mixed, first_row, block_rows, 0)
        scores = block_scores(q_block, keys, allowed_block(doc_ids, first_row, block_rows))
        probs = jnp.exp(scores - logsum[block_index][..., None])
        grad_probs = jnp.einsum("bhe,khe->hbk", g_block, values, preferred_element_type=jnp.float32)
        inner = jnp.sum(grad_probs * probs, -1, keepdims=True)
        grad_scores = (probs * (grad_probs - inner)).astype(jnp.bfloat16)
        grad_query = (
            jnp.einsum("hbk,khe->bhe", grad_scores, keys, preferred_element_type=jnp.float32)
            * scale_factor
        )
        grad_keys = (
            grad_keys
            + jnp.einsum("hbk,bhe->khe", grad_scores, q_block, preferred_element_type=jnp.float32)
            * scale_factor
        )
        grad_values = grad_values + jnp.einsum(
            "hbk,bhe->khe", probs.astype(jnp.bfloat16), g_block, preferred_element_type=jnp.float32
        )
        return ((grad_keys, grad_values), grad_query)

    zeros_kv = jnp.zeros(keys.shape, jnp.float32)
    (grad_keys, grad_values), grad_query = lax.scan(
        one_block, (zeros_kv, zeros_kv), jnp.arange(query.shape[0] // block_rows, dtype=jnp.int32)
    )
    return (grad_query.reshape(query.shape), grad_keys, grad_values)


def gather_rows(values):
    return lax.all_gather(values, "tensor", axis=0, tiled=True)


def gather_grads(values):
    return lax.all_gather(values, "tensor", axis=0, tiled=True)


def branch_rows(left, right):
    return lax.psum_scatter(
        jnp.dot(left, right, preferred_element_type=jnp.float32).astype(jnp.bfloat16),
        "tensor",
        scatter_dimension=0,
        tiled=True,
    ).astype(jnp.float32)


def back_rows(left, right):
    return lax.psum_scatter(
        lax.dot_general(
            left, right, (((1,), (1,)), ((), ())), preferred_element_type=jnp.float32
        ).astype(jnp.bfloat16),
        "tensor",
        scatter_dimension=0,
        tiled=True,
    ).astype(jnp.float32)


def head_loss(features, table_out, targets, weights_row):
    logits = lax.dot_general(
        features, table_out, (((1,), (1,)), ((), ())), preferred_element_type=jnp.float32
    )
    top_score = jnp.max(logits, -1, keepdims=True)
    expo = jnp.exp(logits - top_score)
    totals = jnp.sum(expo, -1, keepdims=True)
    target_hit = jnp.arange(table_out.shape[0], dtype=jnp.int32)[None, :] == targets[:, None]
    picked = jnp.sum(jnp.where(target_hit, logits, 0.0), -1)
    loss_value = jnp.sum(weights_row * (top_score[:, 0] + jnp.log(totals[:, 0]) - picked))
    grad_logits = ((expo / totals - target_hit.astype(jnp.float32)) * weights_row[:, None]).astype(
        jnp.bfloat16
    )
    return (loss_value, grad_logits)


def layer_forward(codes_row, lengths_row, mask_row, weights, part_index, row_count):
    qkv_w, out_w, up_w, down_w, table_w, gain_w = weights
    total_rows = codes_row.shape[0]
    width = table_w.shape[2]
    doc_ids, local_pos = doc_layout(lengths_row, total_rows)
    targets = next_codes(codes_row, doc_ids, table_w.shape[1] - 1)
    first_row = part_index * row_count
    my_codes = lax.dynamic_slice_in_dim(codes_row, first_row, row_count, 0)
    my_local = lax.dynamic_slice_in_dim(local_pos, first_row, row_count, 0)
    my_targets = lax.dynamic_slice_in_dim(targets, first_row, row_count, 0)
    gains = gain_w.astype(jnp.float32)
    start = jnp.take(table_w[0], my_codes, axis=0).astype(jnp.float32) * math.sqrt(
        width
    ) + position_code(my_local, width)
    norm_one = layer_norm(start, gains[0])
    attn_in = gather_rows(norm_one[0].astype(jnp.bfloat16))
    joined = jnp.dot(attn_in, qkv_w.reshape(width, -1), preferred_element_type=jnp.float32).astype(
        jnp.bfloat16
    )
    joined = joined.reshape(total_rows, 3, -1, HEAD)
    block_rows = min(512, total_rows)
    mixed, logsum = attend(joined[:, 0], joined[:, 1], joined[:, 2], doc_ids, block_rows)
    mixed_flat = mixed.reshape(total_rows, -1)
    middle = start + branch_rows(mixed_flat, out_w)
    norm_two = layer_norm(middle, gains[1])
    ffn_in = gather_rows(norm_two[0].astype(jnp.bfloat16))
    up_val = jnp.dot(ffn_in, up_w, preferred_element_type=jnp.float32)
    hidden = jax.nn.gelu(up_val, approximate=False).astype(jnp.bfloat16)
    final = middle + branch_rows(hidden, down_w)
    norm_three = layer_norm(final, gains[2])
    features = norm_three[0].astype(jnp.bfloat16)
    loss_value, grad_logits = head_loss(features, table_w[1], my_targets, mask_row)
    kept = (
        my_codes,
        doc_ids,
        norm_one,
        attn_in,
        joined,
        mixed_flat,
        logsum,
        norm_two,
        ffn_in,
        up_val,
        hidden,
        norm_three,
        features,
        grad_logits,
    )
    return (kept, loss_value)


def layer_backward(kept, weights):
    qkv_w, out_w, up_w, down_w, table_w, gain_w = weights
    (
        my_codes,
        doc_ids,
        norm_one,
        attn_in,
        joined,
        mixed_flat,
        logsum,
        norm_two,
        ffn_in,
        up_val,
        hidden,
        norm_three,
        features,
        grad_logits,
    ) = kept
    total_rows = attn_in.shape[0]
    width = table_w.shape[2]
    gains = gain_w.astype(jnp.float32)
    contract_rows = (((0,), (0,)), ((), ()))
    contract_cols = (((1,), (1,)), ((), ()))
    head_grad = lax.dot_general(
        grad_logits, features, contract_rows, preferred_element_type=jnp.float32
    )
    grad_feat = jnp.dot(grad_logits, table_w[1], preferred_element_type=jnp.float32)
    grad_final, gain_three = norm_back(grad_feat, norm_three[1], norm_three[2], gains[2])
    grad_down_in = gather_grads(grad_final.astype(jnp.bfloat16))
    down_grad = lax.dot_general(
        hidden, grad_down_in, contract_rows, preferred_element_type=jnp.float32
    )
    grad_hidden = lax.dot_general(
        grad_down_in, down_w, contract_cols, preferred_element_type=jnp.float32
    )
    gelu_out, gelu_pull = jax.vjp(partial(jax.nn.gelu, approximate=False), up_val)
    grad_up = gelu_pull(grad_hidden)[0].astype(jnp.bfloat16)
    up_grad = lax.dot_general(ffn_in, grad_up, contract_rows, preferred_element_type=jnp.float32)
    grad_mid, gain_two = norm_back(back_rows(grad_up, up_w), norm_two[1], norm_two[2], gains[1])
    grad_mid = grad_mid + grad_final
    grad_out_in = gather_grads(grad_mid.astype(jnp.bfloat16))
    out_grad = lax.dot_general(
        mixed_flat, grad_out_in, contract_rows, preferred_element_type=jnp.float32
    )
    grad_mixed = lax.dot_general(
        grad_out_in, out_w, contract_cols, preferred_element_type=jnp.float32
    ).astype(jnp.bfloat16)
    grad_mixed = grad_mixed.reshape(total_rows, -1, HEAD)
    block_rows = min(512, total_rows)
    grad_query, grad_keys, grad_values = attend_back(
        joined[:, 0], joined[:, 1], joined[:, 2], grad_mixed, logsum, doc_ids, block_rows
    )
    grad_joined = (
        jnp.stack([grad_query, grad_keys, grad_values], 1)
        .reshape(total_rows, -1)
        .astype(jnp.bfloat16)
    )
    qkv_grad = lax.dot_general(
        attn_in, grad_joined, contract_rows, preferred_element_type=jnp.float32
    ).reshape(width, 3, -1)
    grad_start, gain_one = norm_back(
        back_rows(grad_joined, qkv_w.reshape(width, -1)), norm_one[1], norm_one[2], gains[0]
    )
    grad_start = grad_start + grad_mid
    embed_grad = jax.ops.segment_sum(
        grad_start * math.sqrt(width), my_codes, num_segments=table_w.shape[1]
    )
    table_grad = jnp.stack([embed_grad, head_grad])
    gain_grad = jnp.stack([gain_one, gain_two, gain_three])
    return (qkv_grad, out_grad, up_grad, down_grad, table_grad, gain_grad)


def adam_update(master, first, second, grad, step_rate, decay_rate):
    first_new = 0.5 * first + 0.5 * grad
    second_new = 0.5 * second + 0.5 * grad * grad
    correct = 1.0 - 0.5**STEP
    master_new = master - step_rate * (
        first_new / correct / (jnp.sqrt(second_new / correct) + ADAM_EPS) + decay_rate * master
    )
    return (master_new, first_new, second_new, master_new.astype(jnp.bfloat16))


def body(
    codes,
    doc_lengths,
    loss_mask,
    qkv_master,
    qkv_first,
    qkv_second,
    out_master,
    out_first,
    out_second,
    up_master,
    up_first,
    up_second,
    down_master,
    down_first,
    down_second,
    table_master,
    table_first,
    table_second,
    gain_master,
    gain_first,
    gain_second,
):
    qkv_w, out_w, up_w, down_w = (
        lax.all_gather(qkv_master.astype(jnp.bfloat16), "dp", axis=0, tiled=True),
        lax.all_gather(out_master.astype(jnp.bfloat16), "dp", axis=1, tiled=True),
        lax.all_gather(up_master.astype(jnp.bfloat16), "dp", axis=0, tiled=True),
        lax.all_gather(down_master.astype(jnp.bfloat16), "dp", axis=1, tiled=True),
    )
    table_w, gain_w = (
        lax.all_gather(table_master.astype(jnp.bfloat16), ("dp", "tensor"), axis=2, tiled=True),
        lax.all_gather(gain_master.astype(jnp.bfloat16), ("dp", "tensor"), axis=1, tiled=True),
    )
    weights = (qkv_w, out_w, up_w, down_w, table_w, gain_w)
    part_index = lax.axis_index("tensor")
    row_count = codes.shape[1] // lax.axis_size("tensor")
    my_mask = lax.dynamic_slice_in_dim(loss_mask, part_index * row_count, row_count, 1).astype(
        jnp.float32
    )
    count_local = jnp.sum(my_mask)
    count_all = lax.psum(count_local, ("dp", "tensor"))
    loss_local = jnp.zeros((), jnp.float32)
    summed = None
    for micro_index in range(codes.shape[0]):
        kept, loss_value = layer_forward(
            codes[micro_index],
            doc_lengths[micro_index],
            my_mask[micro_index],
            weights,
            part_index,
            row_count,
        )
        grads = layer_backward(kept, weights)
        loss_local = loss_local + loss_value
        summed = grads if summed is None else jax.tree.map(jnp.add, summed, grads)
    layer_part = (
        lax.psum_scatter(summed[0], "dp", scatter_dimension=0, tiled=True),
        lax.psum_scatter(summed[1], "dp", scatter_dimension=1, tiled=True),
        lax.psum_scatter(summed[2], "dp", scatter_dimension=0, tiled=True),
        lax.psum_scatter(summed[3], "dp", scatter_dimension=1, tiled=True),
    )
    shared_part = (
        lax.psum_scatter(summed[4], ("dp", "tensor"), scatter_dimension=2, tiled=True),
        lax.psum_scatter(summed[5], ("dp", "tensor"), scatter_dimension=1, tiled=True),
    )
    summed = tuple(layer_part) + tuple(shared_part)
    squares = sum((jnp.sum(grad_piece * grad_piece) for grad_piece in summed))
    loss_all, square_all = lax.psum(
        (loss_local, squares / (count_all * count_all)), ("dp", "tensor")
    )
    norm_all = jnp.sqrt(square_all)
    factor = jnp.minimum(1.0, CLIP_NORM / (norm_all + 1e-06))
    masters = (qkv_master, out_master, up_master, down_master, table_master, gain_master)
    firsts = (qkv_first, out_first, up_first, down_first, table_first, gain_first)
    seconds = (qkv_second, out_second, up_second, down_second, table_second, gain_second)
    results = []
    for weight_index in range(6):
        step_rate = RATE_GAIN if weight_index == 5 else RATE_MATRIX
        decay_rate = 0.0 if weight_index == 5 else DECAY_RATE
        clipped = summed[weight_index] / count_all * factor
        results.extend(
            adam_update(
                masters[weight_index],
                firsts[weight_index],
                seconds[weight_index],
                clipped,
                step_rate,
                decay_rate,
            )
        )
    return tuple(results) + (loss_all, count_all, norm_all)


def solution(mesh):
    in_specs = (
        P("dp", None),
        P("dp", None),
        P("dp", None),
        P("dp", None, "tensor"),
        P("dp", None, "tensor"),
        P("dp", None, "tensor"),
        P("tensor", "dp"),
        P("tensor", "dp"),
        P("tensor", "dp"),
        P("dp", "tensor"),
        P("dp", "tensor"),
        P("dp", "tensor"),
        P("tensor", "dp"),
        P("tensor", "dp"),
        P("tensor", "dp"),
        P(None, None, ("dp", "tensor")),
        P(None, None, ("dp", "tensor")),
        P(None, None, ("dp", "tensor")),
        P(None, ("dp", "tensor")),
        P(None, ("dp", "tensor")),
        P(None, ("dp", "tensor")),
    )
    out_specs = (
        P("dp", None, "tensor"),
        P("dp", None, "tensor"),
        P("dp", None, "tensor"),
        P("dp", None, "tensor"),
        P("tensor", "dp"),
        P("tensor", "dp"),
        P("tensor", "dp"),
        P("tensor", "dp"),
        P("dp", "tensor"),
        P("dp", "tensor"),
        P("dp", "tensor"),
        P("dp", "tensor"),
        P("tensor", "dp"),
        P("tensor", "dp"),
        P("tensor", "dp"),
        P("tensor", "dp"),
        P(None, None, ("dp", "tensor")),
        P(None, None, ("dp", "tensor")),
        P(None, None, ("dp", "tensor")),
        P(None, None, ("dp", "tensor")),
        P(None, ("dp", "tensor")),
        P(None, ("dp", "tensor")),
        P(None, ("dp", "tensor")),
        P(None, ("dp", "tensor")),
        P(),
        P(),
        P(),
    )
    return jax.shard_map(body, mesh=mesh, in_specs=in_specs, out_specs=out_specs, check_vma=False)
```

profile of v0, /device:TPU:0, one launch (start us, length us, event | category | flops | bytes accessed | tf_op | source)
XLA Modules:
  0.0 1630.6 jit_solution(13657850151706750479)
XLA Ops:
  18.5 69.9 %all-gather = bf16[32,32,3]{1,2,0:T(4,128)(2,1)S(1)} all-gather(bf16[1,32,3]{1,2,0:T(4,128)(2,1)S(1)} %convert_bitcast_fusion), channel_id=1, replica_groups=mesh['dp'=8,'tensor'=4] {'dp','tensor'}, dimensions={0}, use_global_device_ids=true | all-gather | bytes 6336 | tf_op jit(solution)/shard_map/all_gather | solution.py:335
  99.6 10.7 fusion.197
  110.3 11.1 copy.148
  131.3 9.4 all_gather.46
  140.7 32.2 %all-gather.16.cloned.1.call-done = bf16[1024,1024]{1,0:T(8,128)(2,1)} async-done(((bf16[256,1024]{1,0:T(8,128)(2,1)}), bf16[1024,1024]{1,0:T(8,128)(2,1)}) %all-gather.16.cloned.1.call-update) | async-done | bytes 2097168 | tf_op jit(solution)/shard_map/all_gather | solution.py:128
  177.9 21.0 %while.54 = (s32[]{:T(128)}, bf16[2,512,4,64]{1,3,2,0:T(8,128)(2,1)S(1)}, f32[2,4,512]{2,1,0:T(4,128)S(1)}, s32[2]{0:T(128)S(1)}, s32[1024]{0:T(1024)S(1)}, /*in...) while((s32[]{:T(128)}, ...), condition=%wide.region_5.7_spmd, body=%wide.region_2.6_spmd.sunk | while | flops 563739136 | bytes 28915916 | solution.py:89
  203.6 40.8 %reduce-scatter.16.cloned.1.call-done = bf16[256,1024]{1,0:T(8,128)(2,1)} async-done(((bf16[1024,1024]{1,0:T(8,128)(2,1)}), bf16[256,1024]{1,0:T(8,128)(2,1)}) %reduce-scatter.16.cloned.1.call-update) | async-done | bytes 524304 | tf_op jit(solution)/shard_map/reduce_scatter | solution.py:136
  248.7 25.4 %all-gather.22.cloned.1.call-done = bf16[1024,1024]{1,0:T(8,128)(2,1)} async-done(((bf16[128,1024]{1,0:T(8,128)(2,1)}), bf16[1024,1024]{1,0:T(8,128)(2,1)}) %all-gather.22.cloned.1.call-update) | async-done | bytes 2097168 | tf_op jit(solution)/shard_map/all_gather | solution.py:330
  274.1 48.0 %all-gather.20.cloned.1.call-done = bf16[1024,1024]{1,0:T(8,128)(2,1)} async-done(((bf16[256,1024]{1,0:T(8,128)(2,1)}), bf16[1024,1024]{1,0:T(8,128)(2,1)}) %all-gather.20.cloned.1.call-update) | async-done | bytes 2097168 | tf_op jit(solution)/shard_map/all_gather | solution.py:128
  322.2 14.8 multiply_convert_fusion.3
  337.0 14.7 all-gather.24.cloned.1.call-done
  351.7 5.9 convolution_convert_fusion.4
  361.3 11.0 copy.149
  372.3 27.6 %all-gather.30.cloned.1.call-done = bf16[1024,1024]{1,0:T(8,128)(2,1)} async-done(((bf16[256,1024]{1,0:T(8,128)(2,1)}), bf16[1024,1024]{1,0:T(8,128)(2,1)}) %all-gather.30.cloned.1.call-update) | async-done | bytes 2097168 | tf_op jit(solution)/shard_map/all_gather | solution.py:128
  403.5 41.5 %reduce-scatter.18.cloned.1.call-done = bf16[256,1024]{1,0:T(8,128)(2,1)} async-done(((bf16[1024,1024]{1,0:T(8,128)(2,1)}), bf16[256,1024]{1,0:T(8,128)(2,1)}) %reduce-scatter.18.cloned.1.call-update) | async-done | bytes 524304 | tf_op jit(solution)/shard_map/reduce_scatter | solution.py:136
  454.8 19.4 %while.55 = (s32[]{:T(128)}, bf16[2,512,4,64]{1,3,2,0:T(8,128)(2,1)}, f32[2,4,512]{2,1,0:T(4,128)S(1)}, s32[2]{0:T(128)S(1)}, s32[1024]{0:T(1024)S(1)}, /*index=...) while((s32[]{:T(128)}, ...), condition=%wide.region_27.29_spmd, body=%wide.region_24.28_spmd.sunk | while | flops 563739136 | bytes 33110276 | solution.py:89
  479.3 19.9 %all-gather.26.cloned.1.call-done = bf16[1024,1024]{1,0:T(8,128)(2,1)} async-done(((bf16[256,1024]{1,0:T(8,128)(2,1)}), bf16[1024,1024]{1,0:T(8,128)(2,1)}) %all-gather.26.cloned.1.call-update) | async-done | bytes 2097168 | tf_op jit(solution)/shard_map/all_gather | solution.py:132
  499.2 8.2 add_convert_fusion.1
  512.6 31.5 %reduce-scatter.22.cloned.1.call-done = bf16[256,1024]{1,0:T(8,128)(2,1)} async-done(((bf16[1024,1024]{1,0:T(8,128)(2,1)}), bf16[256,1024]{1,0:T(8,128)(2,1)}) %reduce-scatter.22.cloned.1.call-update) | async-done | bytes 524304 | tf_op jit(solution)/shard_map/reduce_scatter | solution.py:136
  545.7 44.0 %reduce-scatter.20.cloned.1.call-done = bf16[256,1024]{1,0:T(8,128)(2,1)} async-done(((bf16[1024,1024]{1,0:T(8,128)(2,1)}), bf16[256,1024]{1,0:T(8,128)(2,1)}) %reduce-scatter.20.cloned.1.call-update) | async-done | bytes 524304 | tf_op jit(solution)/shard_map/reduce_scatter | solution.py:145
  595.2 45.2 %all-gather.32.cloned.1.call-done = bf16[1024,1024]{1,0:T(8,128)(2,1)} async-done(((bf16[256,1024]{1,0:T(8,128)(2,1)}), bf16[1024,1024]{1,0:T(8,128)(2,1)}) %all-gather.32.cloned.1.call-update) | async-done | bytes 2097168 | tf_op jit(solution)/shard_map/all_gather | solution.py:128
  640.3 14.6 multiply_convert_fusion.2
  656.3 5.2 convolution_convert_fusion.1
  662.5 41.8 %reduce-scatter.24.cloned.1.call-done = bf16[256,1024]{1,0:T(8,128)(2,1)} async-done(((bf16[1024,1024]{1,0:T(8,128)(2,1)}), bf16[256,1024]{1,0:T(8,128)(2,1)}) %reduce-scatter.24.cloned.1.call-update) | async-done | bytes 524304 | tf_op jit(solution)/shard_map/reduce_scatter | solution.py:136
  713.5 44.8 %all-gather.34.cloned.1.call-done = bf16[1024,1024]{1,0:T(8,128)(2,1)} async-done(((bf16[256,1024]{1,0:T(8,128)(2,1)}), bf16[1024,1024]{1,0:T(8,128)(2,1)}) %all-gather.34.cloned.1.call-update) | async-done | bytes 2097168 | tf_op jit(solution)/shard_map/all_gather | solution.py:132
  758.3 7.6 add_convert_fusion
  771.1 33.9 %all-gather.28.cloned.1.call-done = bf16[1024,1024]{1,0:T(8,128)(2,1)} async-done(((bf16[256,1024]{1,0:T(8,128)(2,1)}), bf16[1024,1024]{1,0:T(8,128)(2,1)}) %all-gather.28.cloned.1.call-update) | async-done | bytes 2097168 | tf_op jit(solution)/shard_map/all_gather | solution.py:132
  808.1 41.8 %reduce-scatter.26.cloned.1.call-done = bf16[256,1024]{1,0:T(8,128)(2,1)} async-done(((bf16[1024,1024]{1,0:T(8,128)(2,1)}), bf16[256,1024]{1,0:T(8,128)(2,1)}) %reduce-scatter.26.cloned.1.call-update) | async-done | bytes 524304 | tf_op jit(solution)/shard_map/reduce_scatter | solution.py:145
  857.2 60.6 %while.56 = (s32[]{:T(128)}, f32[1024,4,64]{0,2,1:T(8,128)S(1)}, f32[1024,4,64]{0,2,1:T(8,128)}, bf16[2,512,4,64]{1,0,3,2:T(2,128)(2,1)}, s32[2]{0:T(128)S(1)}, ...) while((s32[]{:T(128)}, f32[1024,4,64]{0,2,1:T(8,128)S(1)}, ...), condition=%wide.region_21.23_spmd.clone, body=%wide.region_19.22_spmd.clone.sunk | while | flops 1376778752 | bytes 81598808 | solution.py:121
  877.7 9.8 dynamic_update_slice.37
  908.0 9.8 dynamic_update_slice.37
  929.7 54.7 %while.57 = (s32[]{:T(128)}, f32[1024,4,64]{0,2,1:T(8,128)S(1)}, f32[1024,4,64]{0,2,1:T(8,128)}, bf16[2,512,4,64]{1,0,3,2:T(2,128)(2,1)}, s32[2]{0:T(128)S(1)}, ...) while((s32[]{:T(128)}, f32[1024,4,64]{0,2,1:T(8,128)S(1)}, ...), condition=%wide.region_43.45_spmd.clone, body=%wide.region_41.44_spmd.clone.sunk | while | flops 1376778752 | bytes 75307320 | solution.py:121
  946.8 9.8 dynamic_update_slice.38
  974.6 9.8 dynamic_update_slice.38
  1017.0 5.8 fusion.100
  1022.8 12.4 reduce-scatter.38.cloned.1.call-done
  1038.7 6.6 fusion.104
  1053.0 5.9 scatter_custom_fusion
  1059.0 6.5 scatter_custom_fusion.1
  1065.5 10.1 maximum_add_fusion
  1075.5 14.5 copy.136
  1090.1 39.8 %psum.21 = f32[]{:T(128)} all-reduce(f32[]{:T(128)} %get-tuple-element.546), channel_id=1, replica_groups=mesh['dp'=8,'tensor'=4] {'dp','tensor'}, use_global_device_ids=true, to_apply=%region_46.48 | all-reduce | flops 1 | bytes 8 | tf_op jit(solution)/shard_map/psum | solution.py:344
  1135.6 9.4 reduce-scatter.34.cloned.1.call-done
  1146.8 37.4 %reduce-scatter.30.cloned.1.call-done = f32[256,128]{1,0:T(8,128)} async-done(((f32[256,1024]{1,0:T(8,128)}), f32[256,128]{1,0:T(8,128)}) %reduce-scatter.30.cloned.1.call-update) | async-done | bytes 131088 | tf_op jit(solution)/shard_map/reduce_scatter | solution.py:361
  1185.7 135.2 %reduce-scatter.40.cloned.1.call-done = f32[32,3]{1,0:T(8,128)} async-done(((f32[1024,3]{1,0:T(8,128)}), f32[32,3]{1,0:T(8,128)}) %reduce-scatter.40.cloned.1.call-update) | async-done | bytes 400
  1322.3 45.4 %reduce-scatter.28.cloned.1.call-done = f32[128,3,256]{2,0,1:T(8,128)} async-done(((f32[1024,3,256]{2,0,1:T(8,128)}), f32[128,3,256]{2,0,1:T(8,128)}) %reduce-scatter.28.cloned.1.call-update) | async-done | bytes 393232 | tf_op jit(solution)/shard_map/reduce_scatter | solution.py:360
  1372.0 192.1 %all-reduce.4.cloned.1.call-done = f32[2,1025,1024]{1,0,2:T(2,128)} async-done(((f32[2,1025,1024]{1,0,2:T(2,128)}), f32[2,1025,1024]{1,0,2:T(2,128)}) %all-reduce.4.cloned.1.call-update) | async-done | bytes 8396816
  1567.4 40.2 %all-reduce.1 = (f32[]{:T(128)}, f32[]{:T(128)}) all-reduce(f32[]{:T(128)S(6)} %div.230, f32[]{:T(128)S(6)} %add.461), channel_id=1, replica_groups=mesh['dp'=8,'tensor'=4] {'dp','tensor'}, use_global_device_ids=true, to_apply=%region_72.74 | all-reduce | flops 2 | bytes 16 | tf_op jit(solution)/shard_map/psum | solution.py:371
  (544 shorter events, 288.1 us)
Async XLA Ops:
  7.2 92.4 %all-gather.14.cloned.1.call-start = ((), (), s32[]{:S(2)}) async-start(), calls=%async_computation.13 | async-start | bytes 4866048 | tf_op jit(solution)/shard_map/all_gather | solution.py:334
  9.1 131.5 %all-gather.18.cloned.1.call-start = ((), (), s32[]{:S(2)}) async-start(), calls=%async_computation.15 | async-start | bytes 1769472 | tf_op jit(solution)/shard_map/all_gather | solution.py:328
  11.0 161.8 %all-gather.16.cloned.1.call-start = ((), (), s32[]{:S(2)}) async-start(), calls=%async_computation.14 | async-start | bytes 2621440 | tf_op jit(solution)/shard_map/all_gather | solution.py:128
  128.9 115.6 %copy-start.9 = (f32[256,1024]{1,0:T(8,128)}, f32[256,1024]{1,0:T(8,128)S(1)}, u32[]{:S(2)}) copy-start(f32[256,1024]{1,0:T(8,128)S(1)} %get-tuple-element.561) | copy-start | bytes 3145732
  128.9 47.8 %copy-start.74 = (f32[256]{0:T(256)}, f32[256]{0:T(256)S(1)}, u32[]{:S(2)}) copy-start(f32[256]{0:T(256)S(1)} %broadcast_multiply_fusion.17) | copy-start | bytes 3076
  129.1 47.6 %copy-start.76 = (f32[256]{0:T(256)}, f32[256]{0:T(256)S(1)}, u32[]{:S(2)}) copy-start(f32[256]{0:T(256)S(1)} %add_rsqrt_fusion.2) | copy-start | bytes 3076
  129.2 47.6 %copy-start.78 = (f32[256]{0:T(256)}, f32[256]{0:T(256)S(1)}, u32[]{:S(2)}) copy-start(f32[256]{0:T(256)S(1)} %add_rsqrt_fusion.5) | copy-start | bytes 3076
  130.6 113.9 %reduce-scatter.16.cloned.1.call-start = ((), (), s32[]{:S(2)}) async-start(), calls=%async_computation.16 | async-start | bytes 2621440 | tf_op jit(solution)/shard_map/reduce_scatter | solution.py:136
  140.7 335.7 %copy-start.24 = (bf16[256,1024]{1,0:T(8,128)(2,1)}, bf16[256,1024]{1,0:T(8,128)(2,1)S(1)}, u32[]{:S(2)}) copy-start(bf16[256,1024]{1,0:T(8,128)(2,1)S(1)} %all_gather.46) | copy-start | bytes 1572868
  198.9 158.7 %copy-start.45 = (s32[1024]{0:T(1024)}, s32[1024]{0:T(1024)S(1)}, u32[]{:S(2)}) copy-start(s32[1024]{0:T(1024)S(1)} %get-tuple-element.1129) | copy-start | bytes 12292
  201.7 72.5 %all-gather.22.cloned.1.call-start = ((), (), s32[]{:S(2)}) async-start(), calls=%async_computation.18 | async-start | bytes 2359296 | tf_op jit(solution)/shard_map/all_gather | solution.py:330
  203.6 118.6 %all-gather.20.cloned.1.call-start = ((), (), s32[]{:S(2)}) async-start(), calls=%async_computation.17 | async-start | bytes 2621440 | tf_op jit(solution)/shard_map/all_gather | solution.py:128
  247.0 104.8 %all-gather.24.cloned.1.call-start = ((), (), s32[]{:S(2)}) async-start(), calls=%async_computation.19 | async-start | bytes 2359296 | tf_op jit(solution)/shard_map/all_gather | solution.py:331
  247.8 152.1 %all-gather.30.cloned.1.call-start = ((), (), s32[]{:S(2)}) async-start(), calls=%async_computation.24 | async-start | bytes 2621440 | tf_op jit(solution)/shard_map/all_gather | solution.py:128
  248.5 196.4 %reduce-scatter.18.cloned.1.call-start = ((), (), s32[]{:S(2)}) async-start(), calls=%async_computation.20 | async-start | bytes 2621440 | tf_op jit(solution)/shard_map/reduce_scatter | solution.py:136
  357.6 141.6 %all-gather.26.cloned.1.call-start = ((), (), s32[]{:S(2)}) async-start(), calls=%async_computation.21 | async-start | bytes 2621440 | tf_op jit(solution)/shard_map/all_gather | solution.py:132
  358.8 91.3 %copy-start.95 = (s32[256]{0:T(256)}, s32[256]{0:T(256)S(1)}, u32[]{:S(2)}) copy-start(s32[256]{0:T(256)S(1)} %dynamic_slice.77) | copy-start | bytes 3076
  361.3 88.8 %copy-start.93 = (f32[1,256]{1,0:T(1,128)}, f32[1,256]{1,0:T(1,128)S(1)}, u32[]{:S(2)}) copy-start(f32[1,256]{1,0:T(1,128)S(1)} %get-tuple-element.607) | copy-start | bytes 3076
  453.5 90.6 %reduce-scatter.22.cloned.1.call-start = ((), (), s32[]{:S(2)}) async-start(), calls=%async_computation.25 | async-start | bytes 2621440 | tf_op jit(solution)/shard_map/reduce_scatter | solution.py:136
  479.2 110.4 %reduce-scatter.20.cloned.1.call-start = ((), (), s32[]{:S(2)}) async-start(), calls=%async_computation.22 | async-start | bytes 2621440 | tf_op jit(solution)/shard_map/reduce_scatter | solution.py:145
  512.6 127.8 %all-gather.32.cloned.1.call-start = ((), (), s32[]{:S(2)}) async-start(), calls=%async_computation.26 | async-start | bytes 2621440 | tf_op jit(solution)/shard_map/all_gather | solution.py:128
  545.4 158.9 %copy-start.11 = (f32[256,1024]{1,0:T(8,128)}, f32[256,1024]{1,0:T(8,128)S(1)}, u32[]{:S(2)}) copy-start(f32[256,1024]{1,0:T(8,128)S(1)} %get-tuple-element.571) | copy-start | bytes 3145732
  594.9 109.4 %reduce-scatter.24.cloned.1.call-start = ((), (), s32[]{:S(2)}) async-start(), calls=%async_computation.27 | async-start | bytes 2621440 | tf_op jit(solution)/shard_map/reduce_scatter | solution.py:136
  661.5 96.7 %all-gather.34.cloned.1.call-start = ((), (), s32[]{:S(2)}) async-start(), calls=%async_computation.28 | async-start | bytes 2621440 | tf_op jit(solution)/shard_map/all_gather | solution.py:132
  712.9 92.1 %all-gather.28.cloned.1.call-start = ((), (), s32[]{:S(2)}) async-start(), calls=%async_computation.23 | async-start | bytes 2621440 | tf_op jit(solution)/shard_map/all_gather | solution.py:132
  713.5 136.4 %reduce-scatter.26.cloned.1.call-start = ((), (), s32[]{:S(2)}) async-start(), calls=%async_computation.29 | async-start | bytes 2621440 | tf_op jit(solution)/shard_map/reduce_scatter | solution.py:145
  771.0 154.4 %all-gather.36.cloned.1.call-start = ((), (), s32[]{:S(2)}) async-start(), calls=%async_computation.30 | async-start | bytes 2621440 | tf_op jit(solution)/shard_map/all_gather | solution.py:132
  808.1 49.0 %copy-start.1 = (bf16[1024,4,64]{0,2,1:T(8,128)(2,1)S(1)}, bf16[1024,4,64]{0,2,1:T(8,128)(2,1)}, u32[]{:S(2)}) copy-start(bf16[1024,4,64]{0,2,1:T(8,128)(2,1)} %copy-done) | copy-start | bytes 1572868
  808.1 49.0 %copy-start.46 = (s32[1024]{0:T(1024)S(1)}, s32[1024]{0:T(1024)}, u32[]{:S(2)}) copy-start(s32[1024]{0:T(1024)} %copy-done.45) | copy-start | bytes 12292
  808.1 49.0 %copy-start.60 = (f32[2,4,512]{2,1,0:T(4,128)S(1)}, f32[2,4,512]{2,1,0:T(4,128)}, u32[]{:S(2)}) copy-start(f32[2,4,512]{2,1,0:T(4,128)} %copy-done.59) | copy-start | bytes 49156
  855.6 167.2 %reduce-scatter.36.cloned.1.call-start = ((), (), s32[]{:S(2)}) async-start(), calls=%async_computation.35 | async-start | bytes 2621440 | tf_op jit(solution)/shard_map/reduce_scatter | solution.py:145
  925.3 109.9 %reduce-scatter.38.cloned.1.call-start = ((), (), s32[]{:S(2)}) async-start(), calls=%async_computation.36 | async-start | bytes 2621440 | tf_op jit(solution)/shard_map/reduce_scatter | solution.py:145
  991.9 141.9 %reduce-scatter.32.cloned.1.call-start = ((), (), s32[]{:S(2)}) async-start(), calls=%async_computation.33 | async-start | bytes 4718592 | tf_op jit(solution)/shard_map/reduce_scatter | solution.py:362
  1001.0 143.9 %reduce-scatter.34.cloned.1.call-start = ((), (), s32[]{:S(2)}) async-start(), calls=%async_computation.34 | async-start | bytes 4718592 | tf_op jit(solution)/shard_map/reduce_scatter | solution.py:363
  1011.3 172.9 %reduce-scatter.30.cloned.1.call-start = ((), (), s32[]{:S(2)}) async-start(), calls=%async_computation.32 | async-start | bytes 1179648 | tf_op jit(solution)/shard_map/reduce_scatter | solution.py:361
  1016.4 304.5 %reduce-scatter.40.cloned.1.call-start = ((), (), s32[]{:S(2)}) async-start(), calls=%async_computation.37 | async-start | bytes 540672
  1038.5 329.1 %reduce-scatter.28.cloned.1.call-start = ((), (), s32[]{:S(2)}) async-start(), calls=%async_computation.31 | async-start | bytes 3538944 | tf_op jit(solution)/shard_map/reduce_scatter | solution.py:360
  1045.4 518.7 %all-reduce.4.cloned.1.call-start = ((), (), s32[]{:S(2)}) async-start(), calls=%async_computation.38 | async-start | bytes 18874368
  1090.0 518.4 %copy-start.88 = (f32[3,32]{1,0:T(4,128)S(1)}, f32[3,32]{1,0:T(4,128)}, u32[]{:S(2)}) copy-start(f32[3,32]{1,0:T(4,128)} %param.49) | copy-start | bytes 1156
  1090.0 518.4 %copy-start.105 = (f32[3,32]{1,0:T(4,128)S(1)}, f32[3,32]{1,0:T(4,128)}, u32[]{:S(2)}) copy-start(f32[3,32]{1,0:T(4,128)} %param.50) | copy-start | bytes 1156
  1090.0 518.4 %copy-start.106 = (f32[3,32]{1,0:T(4,128)S(1)}, f32[3,32]{1,0:T(4,128)}, u32[]{:S(2)}) copy-start(f32[3,32]{1,0:T(4,128)} %param.51) | copy-start | bytes 1156
  1090.0 519.6 %copy-start.47 = (f32[2,1025,32]{1,2,0:T(8,128)S(1)}, f32[2,1025,32]{1,2,0:T(8,128)}, u32[]{:S(2)}) copy-start(f32[2,1025,32]{1,2,0:T(8,128)} %param.46) | copy-start | bytes 787204
  1090.0 525.2 %copy-start.43 = (f32[128,3,256]{2,0,1:T(8,128)S(1)}, f32[128,3,256]{2,0,1:T(8,128)}, u32[]{:S(2)}) copy-start(f32[128,3,256]{2,0,1:T(8,128)} %param.34) | copy-start | bytes 1179652
  1131.8 486.5 %copy-start.34 = (f32[1024,128]{1,0:T(8,128)S(1)}, f32[1024,128]{1,0:T(8,128)}, u32[]{:S(2)}) copy-start(f32[1024,128]{1,0:T(8,128)} %param.43) | copy-start | bytes 1572868
  1131.8 486.5 %copy-start.50 = (f32[1024,128]{1,0:T(8,128)S(1)}, f32[1024,128]{1,0:T(8,128)}, u32[]{:S(2)}) copy-start(f32[1024,128]{1,0:T(8,128)} %param.44) | copy-start | bytes 1572868
  1131.8 486.5 %copy-start.51 = (f32[1024,128]{1,0:T(8,128)S(1)}, f32[1024,128]{1,0:T(8,128)}, u32[]{:S(2)}) copy-start(f32[1024,128]{1,0:T(8,128)} %param.45) | copy-start | bytes 1572868
  1144.9 473.4 %copy-start.37 = (f32[1024,128]{1,0:T(8,128)S(1)}, f32[1024,128]{1,0:T(8,128)}, u32[]{:S(2)}) copy-start(f32[1024,128]{1,0:T(8,128)} %reduce-scatter.34.cloned.1.call-done) | copy-start | bytes 1572868
  1367.6 247.6 %copy-start.44 = (f32[128,3,256]{2,0,1:T(8,128)S(1)}, f32[128,3,256]{2,0,1:T(8,128)}, u32[]{:S(2)}) copy-start(f32[128,3,256]{2,0,1:T(8,128)} %reduce-scatter.28.cloned.1.call-done) | copy-start | bytes 1179652
  (105 other events, 1121.8 us)
Sparse Core Ops, SparseCore 0:
  11.4 66.4 all-gather.13
  80.4 24.6 all-gather.17
  130.7 42.1 all-gather.15
  201.8 42.5 reduce-scatter.15
  246.9 27.1 all-gather.21
  276.2 45.9 all-gather.19
  324.8 26.9 all-gather.23
  353.9 45.9 all-gather.29
  402.3 42.5 reduce-scatter.17
  453.6 45.5 all-gather.25
  501.5 42.6 reduce-scatter.21
  546.4 43.1 reduce-scatter.19
  595.1 45.2 all-gather.31
  661.7 42.5 reduce-scatter.23
  713.0 45.2 all-gather.33
  760.4 44.5 all-gather.27
  807.2 42.6 reduce-scatter.25
  855.7 45.2 all-gather.35
  925.4 43.1 reduce-scatter.35
  992.0 43.1 reduce-scatter.37
  1038.6 50.6 reduce-scatter.31
  1093.0 51.8 reduce-scatter.33
  1148.1 36.0 reduce-scatter.29
  1186.8 133.9 reduce-scatter.39
  1324.6 42.9 reduce-scatter.27
  1373.3 190.8 all-reduce.3
where the time goes:
time: 1640 us; the launch traced here: 1630 us
  waiting for transfers between devices  967 us (59%)
  matrix products  208 us (13%)
  blocking collectives  159 us (10%)
  local copies, waits for them, and re-layouts  134 us (8%)
  other arithmetic  119 us (7%)
  between operations  26.9 us (2%)
    unnamed x28, waiting for transfers between devices  329 us
    reduce_scatter x4, waiting for transfers between devices, branch_rows(): lax.psum_scatter(jnp.dot(left, right, preferred_element_type=jnp.float32)...  156 us
    all_gather x4, waiting for transfers between devices, gather_rows(): return lax.all_gather(values, 'tensor', axis=0, tiled=True)  153 us
    all_gather x4, waiting for transfers between devices, gather_grads(): return lax.all_gather(values, 'tensor', axis=0, tiled=True)  98.6 us
    reduce_scatter x4, waiting for transfers between devices, back_rows(): lax.psum_scatter(lax.dot_general(left, right, (((1,), (1,)), ((), ())), p...  98.1 us
    all_gather x1, blocking collectives, body(): lax.all_gather(gain_master.astype(jnp.bfloat16), ('dp', 'tensor'), axis=1...  69.9 us
    reduce_scatter x1, waiting for transfers between devices, body(): lax.psum_scatter(summed[0], 'dp', scatter_dimension=0, tiled=True)  45.4 us
    dynamic_update_slice x8, local copies, waits for them, and re-layouts, attend_back(): lax.scan(one_block, (zeros_kv, zeros_kv), jnp.arange(query.shape[0] // bl...  40.8 us
  transfers between devices with their start and end apart: 26, of which 21 were waited for; matrix products, arithmetic and copies ran while one was open for 22% of the time, Pallas kernels for 0%

commit v1 on v0

v1 whole, which is shorter than its diff:
```python
import functools
import math

import jax
import jax.numpy as jnp
from jax import lax
from jax.experimental import pallas as pl
from jax.experimental.pallas import tpu as pltpu
from jax.sharding import PartitionSpec as P

HEAD = 64
STEP = 5

RATE_MATRIX = 0.03
RATE_GAIN = 0.25
DECAY_RATE = 0.01
CLIP_NORM = 0.002
NORM_EPS = 1e-05
ADAM_EPS = 1e-08

BF = jnp.bfloat16
F32 = jnp.float32
LOG2E = math.log2(math.e)
NN = (((1,), (0,)), ((), ()))
NT = (((1,), (1,)), ((), ()))
TN = (((0,), (0,)), ((), ()))
VMEM_BYTES = 48 * 1024 * 1024


def dot(left, right, dims=NN):
    return lax.dot_general(left, right, dims, preferred_element_type=F32)


def barrier(*values):
    return lax.optimization_barrier(values)


class Place:
    def __init__(self):
        self.dp = lax.axis_size("dp")
        self.nz = lax.axis_size("tensor")
        self.ny = self.dp // 4
        index = lax.axis_index("dp")
        self.z = lax.axis_index("tensor")
        self.c = index % 2
        self.x = (index // 2) % 2
        self.y = index // 4
        self.blocks = [(0, 0), (0, 1)]
        self.blocks += [(k, 1) for k in range(1, self.ny)]
        self.blocks += [(k, 0) for k in range(1, self.ny)]

    def at(self, ky, kx):
        return self.blocks.index((ky, kx))

    def swap_c(self, value):
        return lax.ppermute(value, "dp", [(i, i ^ 1) for i in range(self.dp)])

    def swap_x(self, value):
        return lax.ppermute(value, "dp", [(i, i ^ 2) for i in range(self.dp)])

    def from_y(self, value, k):
        n = self.dp
        return lax.ppermute(value, "dp", [((i + 4 * k) % n, i) for i in range(n)])

    def to_y(self, value, k):
        n = self.dp
        return lax.ppermute(value, "dp", [(i, (i + 4 * k) % n) for i in range(n)])

    def from_z(self, value, k):
        n = self.nz
        return lax.ppermute(value, "tensor", [((i + k) % n, i) for i in range(n)])

    def to_z(self, value, k):
        n = self.nz
        return lax.ppermute(value, "tensor", [(i, (i + k) % n) for i in range(n)])

    def total(self, value):
        value = value + self.swap_c(value)
        value = value + self.swap_x(value)
        value = value + sum(self.from_y(value, k) for k in range(1, self.ny))
        return value + sum(self.from_z(value, k) for k in range(1, self.nz))

    def in_order(self, mine, other, axis):
        first = jnp.where(self.c == 0, mine, other)
        last = jnp.where(self.c == 0, other, mine)
        return jnp.concatenate([first, last], axis)


def gather_z(place, piece):
    return [piece] + [place.from_z(piece, k) for k in range(1, place.nz)]


def join_z(parts, axis):
    half = len(parts) // 2
    return jnp.stack([jnp.concatenate(parts[:half], axis), jnp.concatenate(parts[half:], axis)])


def gather_xy_one(place, both):
    return place.swap_x(both), [place.from_y(both, k) for k in range(1, place.ny)]


def gather_xy_two(place, by_x, by_y):
    first = [place.swap_x(v[0]) for v in by_y]
    second = [place.from_y(by_x[1], k) for k in range(1, place.ny)]
    return first, second


def gathered(place, both, by_x, by_y, far_a, far_b):
    out = []
    for half, far in ((0, far_a), (1, far_b)):
        out.append([both[half], by_x[half]] + far + [v[half] for v in by_y])
    return out


def sum_xy_one(place, send_a, send_b):
    return place.swap_x(send_a), [place.to_y(v, k + 1) for k, v in enumerate(send_b)]


def sum_xy_two(place, pass_a, pass_b):
    return [place.to_y(v, k + 1) for k, v in enumerate(pass_a)], place.swap_x(pass_b)


def forward_kernel(c_ref, start_ref, qkv_ref, o_ref, lse_ref, k_s, v_s):
    c = c_ref[0]
    half = qkv_ref.shape[1]
    total = 2 * half
    block = min(256, half)
    per_half = half // block
    scale = HEAD ** (-0.5) * LOG2E
    for b in range(2):
        k_s[b * half : (b + 1) * half] = qkv_ref[b ^ c, :, 128:256]
        v_s[b * half : (b + 1) * half] = qkv_ref[b ^ c, :, 256:384]
    lane = lax.broadcasted_iota(jnp.int32, (block, 128), 1)
    for qb in range(total // block):
        rel = (qb // per_half) ^ c
        r0 = (qb % per_half) * block
        n = (qb + 1) * block
        q = qkv_ref[rel, r0 : r0 + block, 0:128]
        row = qb * block + lax.broadcasted_iota(jnp.int32, (block, n), 0)
        col = lax.broadcasted_iota(jnp.int32, (block, n), 1)
        start = start_ref[qb * block : (qb + 1) * block, 0:1]
        allowed = (col >= start) & (col <= row)
        outs = []
        for h in range(2):
            qh = jnp.where((lane >= 64) == (h == 1), q, jnp.zeros_like(q))
            s = dot(qh, k_s[0:n], NT)
            s = jnp.where(allowed, s, -1e30)
            top = jnp.max(s, -1, keepdims=True)
            p = jnp.exp2((s - top) * scale)
            total_p = jnp.sum(p, -1, keepdims=True)
            outs.append(dot(p.astype(BF), v_s[0:n]) / total_p)
            lse = top * scale + jnp.log2(total_p)
            lse_ref[0, qb * block : (qb + 1) * block, h * 64 : (h + 1) * 64] = jnp.broadcast_to(
                lse, (block, 64)
            )
        o_ref[rel, r0 : r0 + block, :] = jnp.where(lane < 64, outs[0], outs[1]).astype(BF)


def backward_kernel(c_ref, start_ref, qkv_ref, o_ref, go_ref, lse_ref, out_ref, k_s, v_s, gk_s, gv_s):
    c = c_ref[0]
    half = qkv_ref.shape[1]
    total = 2 * half
    block = min(256, half)
    per_half = half // block
    scale = HEAD ** (-0.5)
    for b in range(2):
        k_s[b * half : (b + 1) * half] = qkv_ref[b ^ c, :, 128:256]
        v_s[b * half : (b + 1) * half] = qkv_ref[b ^ c, :, 256:384]
    lane = lax.broadcasted_iota(jnp.int32, (block, 128), 1)
    for step, qb in enumerate(reversed(range(total // block))):
        rel = (qb // per_half) ^ c
        r0 = (qb % per_half) * block
        n = (qb + 1) * block
        q = qkv_ref[rel, r0 : r0 + block, 0:128]
        go = go_ref[rel, r0 : r0 + block, :]
        o = o_ref[rel, r0 : r0 + block, :]
        row = qb * block + lax.broadcasted_iota(jnp.int32, (block, n), 0)
        col = lax.broadcasted_iota(jnp.int32, (block, n), 1)
        start = start_ref[qb * block : (qb + 1) * block, 0:1]
        allowed = (col >= start) & (col <= row)
        both = go.astype(F32) * o.astype(F32)
        gq = None
        for h in range(2):
            mine = (lane >= 64) == (h == 1)
            qh = jnp.where(mine, q, jnp.zeros_like(q))
            gh = jnp.where(mine, go, jnp.zeros_like(go))
            s = dot(qh, k_s[0:n], NT)
            lse = lse_ref[0, qb * block : (qb + 1) * block, h * 64 : h * 64 + 1]
            p = jnp.where(allowed, jnp.exp2(jnp.minimum(s * (scale * LOG2E) - lse, 1.0)), 0.0)
            gp = dot(gh, v_s[0:n], NT)
            inner = jnp.sum(jnp.where(mine, both, 0.0), -1, keepdims=True)
            gs = (p * (gp - inner)).astype(BF)
            pb = p.astype(BF)
            gqh = dot(gs, k_s[0:n])
            gq = gqh if gq is None else jnp.where(lane < 64, gq, gqh)
            gk = dot(gs, qh, TN)
            gv = dot(pb, gh, TN)
            if step == 0 and h == 0:
                gk_s[0:n] = gk
                gv_s[0:n] = gv
            else:
                gk_s[0:n] += gk
                gv_s[0:n] += gv
        out_ref[rel, r0 : r0 + block, 0:128] = (gq * scale).astype(BF)
    for b in range(2):
        out_ref[b ^ c, :, 128:256] = (gk_s[b * half : (b + 1) * half] * scale).astype(BF)
        out_ref[b ^ c, :, 256:384] = gv_s[b * half : (b + 1) * half].astype(BF)


def attention(c_index, starts, qkv):
    rows, cols = qkv.shape
    half, pairs = rows // 2, cols // 384
    smem = pl.BlockSpec(memory_space=pltpu.SMEM)
    out, lse = pl.pallas_call(
        forward_kernel,
        grid=(pairs,),
        in_specs=[
            smem,
            pl.BlockSpec((rows, 1), lambda j: (0, 0)),
            pl.BlockSpec((2, half, 384), lambda j: (0, 0, j)),
        ],
        out_specs=[
            pl.BlockSpec((2, half, 128), lambda j: (0, 0, j)),
            pl.BlockSpec((1, rows, 128), lambda j: (j, 0, 0)),
        ],
        out_shape=[
            jax.ShapeDtypeStruct((2, half, pairs * 128), BF),
            jax.ShapeDtypeStruct((pairs, rows, 128), F32),
        ],
        scratch_shapes=[pltpu.VMEM((rows, 128), BF), pltpu.VMEM((rows, 128), BF)],
        compiler_params=pltpu.CompilerParams(vmem_limit_bytes=VMEM_BYTES),
        cost_estimate=pl.CostEstimate(
            flops=4 * pairs * 2 * rows * rows * 128, bytes_accessed=2 * rows * cols * 3, transcendentals=0
        ),
        name="attend",
    )(c_index, starts, qkv.reshape(2, half, cols))
    return out.reshape(rows, pairs * 128), lse


def attention_back(c_index, starts, qkv, out, grad, lse):
    rows, cols = qkv.shape
    half, pairs = rows // 2, cols // 384
    smem = pl.BlockSpec(memory_space=pltpu.SMEM)
    wide = pl.BlockSpec((2, half, 384), lambda j: (0, 0, j))
    thin = pl.BlockSpec((2, half, 128), lambda j: (0, 0, j))
    result = pl.pallas_call(
        backward_kernel,
        grid=(pairs,),
        in_specs=[
            smem,
            pl.BlockSpec((rows, 1), lambda j: (0, 0)),
            wide,
            thin,
            thin,
            pl.BlockSpec((1, rows, 128), lambda j: (j, 0, 0)),
        ],
        out_specs=wide,
        out_shape=jax.ShapeDtypeStruct((2, half, cols), BF),
        scratch_shapes=[
            pltpu.VMEM((rows, 128), BF),
            pltpu.VMEM((rows, 128), BF),
            pltpu.VMEM((rows, 128), F32),
            pltpu.VMEM((rows, 128), F32),
        ],
        compiler_params=pltpu.CompilerParams(vmem_limit_bytes=VMEM_BYTES),
        cost_estimate=pl.CostEstimate(
            flops=10 * pairs * 2 * rows * rows * 128, bytes_accessed=2 * rows * cols * 4, transcendentals=0
        ),
        name="attend_back",
    )(
        c_index,
        starts,
        qkv.reshape(2, half, cols),
        out.reshape(2, half, pairs * 128),
        grad.reshape(2, half, pairs * 128),
        lse,
    )
    return result.reshape(rows, cols)


def layer_norm(values, gain_vec):
    mean_val = jnp.mean(values, -1, keepdims=True)
    centered = values - mean_val
    inverse = lax.rsqrt(jnp.mean(centered * centered, -1, keepdims=True) + NORM_EPS)
    normed = centered * inverse
    return ((normed * gain_vec).astype(BF), normed, inverse)


def norm_back(grad_out, normed, inverse, gain_vec):
    grad_normed = grad_out * gain_vec
    grad_in = inverse * (
        grad_normed
        - jnp.mean(grad_normed, -1, keepdims=True)
        - normed * jnp.mean(grad_normed * normed, -1, keepdims=True)
    )
    return (grad_in, jnp.sum(grad_out * normed, 0))


def doc_layout(lengths_row, total_rows):
    places = jnp.arange(total_rows, dtype=jnp.int32)
    bound_one = lengths_row[0]
    bound_two = lengths_row[0] + lengths_row[1]
    doc_ids = (places >= bound_one).astype(jnp.int32) + (places >= bound_two).astype(jnp.int32)
    starts = jnp.where(doc_ids == 0, 0, jnp.where(doc_ids == 1, bound_one, bound_two))
    return (doc_ids, starts, places - starts)


def next_codes(codes_row, doc_ids, end_code):
    later = jnp.concatenate([codes_row[1:], jnp.full((1,), end_code, jnp.int32)])
    later_doc = jnp.concatenate([doc_ids[1:], jnp.full((1,), -1, jnp.int32)])
    return jnp.where(later_doc == doc_ids, later, end_code)


def head_loss(logits, targets, weights_row):
    top_score = jnp.max(logits, -1, keepdims=True)
    expo = jnp.exp(logits - top_score)
    totals = jnp.sum(expo, -1, keepdims=True)
    target_hit = jnp.arange(logits.shape[1], dtype=jnp.int32)[None, :] == targets[:, None]
    picked = jnp.sum(jnp.where(target_hit, logits, 0.0), -1)
    loss_value = jnp.sum(weights_row * (top_score[:, 0] + jnp.log(totals[:, 0]) - picked))
    grad_logits = ((expo / totals - target_hit.astype(F32)) * weights_row[:, None]).astype(BF)
    return (loss_value, grad_logits)


def adam_update(master, first, second, grad, step_rate, decay_rate):
    first_new = 0.5 * first + 0.5 * grad
    second_new = 0.5 * second + 0.5 * grad * grad
    correct = 1.0 - 0.5**STEP
    master_new = master - step_rate * (
        first_new / correct / (jnp.sqrt(second_new / correct) + ADAM_EPS) + decay_rate * master
    )
    return (master_new, first_new, second_new, master_new.astype(BF))


def gelu_both(value):
    phi = 0.5 * (1.0 + lax.erf(value * (0.5**0.5)))
    slope = phi + value * (jnp.exp(-0.5 * value * value) * (1.0 / math.sqrt(2.0 * math.pi)))
    return (value * phi).astype(BF), slope.astype(BF)


def body(
    codes,
    doc_lengths,
    loss_mask,
    qkv_master,
    qkv_first,
    qkv_second,
    out_master,
    out_first,
    out_second,
    up_master,
    up_first,
    up_second,
    down_master,
    down_first,
    down_second,
    table_master,
    table_first,
    table_second,
    gain_master,
    gain_first,
    gain_second,
):
    place = Place()
    nz, ny, nb = place.nz, place.ny, len(place.blocks)
    c, z = place.c, place.z
    feat = qkv_master.shape[0]
    width = feat * place.dp
    total_rows = codes.shape[1]
    half_rows = total_rows // 2
    vocab = table_master.shape[1]
    thin = table_master.shape[2]

    joined = jnp.concatenate([codes, loss_mask, doc_lengths], 1)
    other = place.swap_c(joined)
    four = place.in_order(joined, other, 0)
    row = lax.dynamic_index_in_dim(four, z, 0, keepdims=False)
    codes_row = row[:total_rows]
    mask_row = row[total_rows : 2 * total_rows]
    lengths_row = row[2 * total_rows :]
    doc_ids, starts, local_pos = doc_layout(lengths_row, total_rows)
    targets = next_codes(codes_row, doc_ids, vocab - 1)
    first_row = c * half_rows
    my_codes = lax.dynamic_slice_in_dim(codes_row, first_row, half_rows, 0)
    my_local = lax.dynamic_slice_in_dim(local_pos, first_row, half_rows, 0)
    my_targets = lax.dynamic_slice_in_dim(targets, first_row, half_rows, 0)
    my_mask = lax.dynamic_slice_in_dim(mask_row, first_row, half_rows, 0).astype(F32)
    c_index = jnp.reshape(c, (1,)).astype(jnp.int32)
    starts_col = starts.reshape(total_rows, 1)

    def halves(matrix, axis):
        size = matrix.shape[axis] // 2
        keep = lax.dynamic_slice_in_dim(matrix, c * size, size, axis)
        send = lax.dynamic_slice_in_dim(matrix, (1 - c) * size, size, axis)
        return keep, send

    qkv_b, out_b, up_b, down_b = (
        v.astype(BF) for v in (qkv_master, out_master, up_master, down_master)
    )
    qkv_k, qkv_s = (v.reshape(feat, -1) for v in halves(qkv_b, 2))
    out_k, out_s = (v.T for v in halves(out_b, 0))
    up_k, up_s = halves(up_b, 1)
    down_k, down_s = (v.T for v in halves(down_b, 0))
    units = [v.shape[1] for v in (qkv_k, out_k, up_k, down_k)]
    keep = jnp.concatenate([qkv_k, out_k, up_k, down_k], 1)
    send = jnp.concatenate([qkv_s, out_s, up_s, down_s], 1)
    table_t = jnp.swapaxes(table_master.astype(BF), 1, 2)
    embed_p = jnp.concatenate([table_t[0], gain_master.astype(BF).T], 1)
    head_p = table_t[1]

    recv = place.swap_c(send)
    chip = place.in_order(keep, recv, 0)
    edges = [sum(units[:i]) for i in range(5)]
    qkv_p, out_p, up_p, down_p = (chip[:, edges[i] : edges[i + 1]] for i in range(4))

    pieces = [(embed_p, 0), (qkv_p, 1), (out_p, 1), (up_p, 1), (down_p, 1), (head_p, 0)]
    plan = [
        [("z", 0), ("z", 1)],
        [("one", 0), ("one", 1), ("z", 2), ("z", 3)],
        [("two", 0), ("two", 1), ("one", 2), ("one", 3)],
        [("two", 2), ("two", 3), ("z", 4), ("z", 5)],
        [("one", 4), ("one", 5)],
        [("two", 4), ("two", 5)],
    ]
    stage = [dict(own=v[0]) for v in pieces]
    full = {}
    for slot in plan:
        live = [s for i, s in enumerate(stage) if i not in full]
        order = [i for i in range(len(stage)) if i not in full]
        (live,) = barrier(live)
        for i, s in zip(order, live):
            stage[i] = dict(s)
        for kind, i in slot:
            s = stage[i]
            if kind == "z":
                s["parts"] = gather_z(place, s["own"])
            elif kind == "one":
                s["both"] = join_z(s["parts"], pieces[i][1])
                s["by_x"], s["by_y"] = gather_xy_one(place, s["both"])
            else:
                s["far_a"], s["far_b"] = gather_xy_two(place, s["by_x"], s["by_y"])
        (stage_out,) = barrier([stage[i] for i in order])
        for i, s in zip(order, stage_out):
            stage[i] = dict(s)
        for kind, i in slot:
            if kind == "two":
                s = stage[i]
                full[i] = gathered(
                    place, s["both"], s["by_x"], s["by_y"], s["far_a"], s["far_b"]
                )

    def weight(i):
        return [jnp.concatenate(v, 0) for v in full[i]]

    def table(i):
        a, b = (jnp.stack(v) for v in full[i])
        cols = a.shape[-1]
        rel = jnp.concatenate([a, b], 1).reshape(nb, nz, thin, cols)
        mine = jnp.roll(rel, z, 1).reshape(nb, 1, nz * thin, cols)
        got = place.swap_c(mine)
        return place.in_order(mine, got, 1).reshape(width, cols)

    embed_t = table(0)
    gains = embed_t[:, vocab:].astype(F32).T
    wqkv, wout, wup, wdown = weight(1), weight(2), weight(3), weight(4)
    head_t = table(5)

    block = jnp.asarray([k for k, _ in place.blocks], jnp.int32)
    block_x = jnp.asarray([k for _, k in place.blocks], jnp.int32)
    chip_at = ((place.y + block) % ny) * 2 + (place.x ^ block_x)
    feature = (
        chip_at[:, None] * (2 * feat) + jnp.arange(2 * feat, dtype=jnp.int32)[None, :]
    ).reshape(width)
    freqs = jnp.exp((feature // 2).astype(F32) * (-2.0 * math.log(10000.0) / width))
    angles = my_local.astype(F32)[:, None] * freqs[None, :]
    coded = jnp.where((feature % 2 == 0)[None, :], jnp.sin(angles), jnp.cos(angles))
    one_hot = (
        my_codes[:, None] == jnp.arange(embed_t.shape[1], dtype=jnp.int32)[None, :]
    ).astype(BF)
    start = dot(one_hot, embed_t, NT) * math.sqrt(width) + coded
    attn_m, normed_one, inverse_one = layer_norm(start, gains[0])

    def pair(mine):
        return jnp.concatenate([mine, place.swap_c(mine)], 0)

    def branch(lefts, rights, dims):
        theirs = sum(dot(v[half_rows:], w, dims) for v, w in zip(lefts, rights)).astype(BF)
        got = place.swap_c(theirs)
        mine = sum(dot(v[:half_rows], w, dims) for v, w in zip(lefts, rights))
        return mine + got.astype(F32)

    attn_in = pair(attn_m)
    qkv = [dot(attn_in, w).astype(BF) for w in wqkv]
    mixed, lse = [], []
    for v in qkv:
        o, ls = attention(c_index, starts_col, v)
        mixed.append(o)
        lse.append(ls)
    middle = start + branch(mixed, wout, NT)
    ffn_m, normed_two, inverse_two = layer_norm(middle, gains[1])
    ffn_in = pair(ffn_m)
    hidden, slope = zip(*(gelu_both(dot(ffn_in, w)) for w in wup))
    final = middle + branch(hidden, wdown, NT)
    features, normed_three, inverse_three = layer_norm(final, gains[2])
    logits = dot(features, head_t)
    loss_local, grad_logits = head_loss(logits, my_targets, my_mask)

    cut = 2 * feat

    def weight_grad(left, rights):
        def piece(lo, hi, right):
            return dot(left[:, lo * cut : hi * cut], right, TN)

        a, b = rights
        send_a = piece(1, 1 + ny, a).astype(BF)
        if ny == 2:
            send_b = [piece(2, 4, b).astype(BF)]
        else:
            send_b = [
                jnp.concatenate(
                    [piece(place.at(k, 1), place.at(k, 1) + 1, b), piece(place.at(k, 0), place.at(k, 0) + 1, b)]
                ).astype(BF)
                for k in range(1, ny)
            ]
        got_a, got_b = sum_xy_one(place, send_a, send_b)
        pass_a = [
            (piece(place.at(k, 0), place.at(k, 0) + 1, a) + got_a[k * cut : (k + 1) * cut].astype(F32)).astype(BF)
            for k in range(1, ny)
        ]
        pass_b = (piece(1, 2, b) + sum(v[:cut].astype(F32) for v in got_b)).astype(BF)
        far_a, far_b = sum_xy_two(place, pass_a, pass_b)
        own_a = piece(0, 1, a) + got_a[:cut].astype(F32) + sum(v.astype(F32) for v in far_a)
        own_b = piece(0, 1, b) + sum(v[cut:].astype(F32) for v in got_b) + far_b.astype(F32)
        return own_a, own_b

    def sum_z(own_a, own_b, axis):
        chunks = jnp.split(own_a, nz // 2, axis) + jnp.split(own_b, nz // 2, axis)
        return chunks[0] + sum(
            place.to_z(chunks[k].astype(BF), k).astype(F32) for k in range(1, nz)
        )

    def table_grad(partial):
        cols = partial.shape[1]
        cut_t = partial.reshape(nb, 2, nz * thin, cols)
        keep_t = lax.dynamic_index_in_dim(cut_t, c, 1, keepdims=False)
        send_t = lax.dynamic_index_in_dim(cut_t, 1 - c, 1, keepdims=False)
        chip_t = keep_t.astype(F32) + place.swap_c(send_t.astype(BF)).astype(F32)
        rel = jnp.roll(chip_t.reshape(nb, nz, thin, cols), -z, 1)
        a = rel[:, : nz // 2]
        b = rel[:, nz // 2 :]
        send_a = a[1 : 1 + ny].astype(BF)
        send_b = [
            jnp.stack([b[place.at(k, 1)], b[place.at(k, 0)]]).astype(BF) for k in range(1, ny)
        ]
        got_a, got_b = sum_xy_one(place, send_a, send_b)
        pass_a = [(a[place.at(k, 0)] + got_a[k].astype(F32)).astype(BF) for k in range(1, ny)]
        pass_b = (b[1] + sum(v[0].astype(F32) for v in got_b)).astype(BF)
        far_a, far_b = sum_xy_two(place, pass_a, pass_b)
        own_a = a[0] + got_a[0].astype(F32) + sum(v.astype(F32) for v in far_a)
        own_b = b[0] + sum(v[1].astype(F32) for v in got_b) + far_b.astype(F32)
        return sum_z(own_a, own_b, 0)[0]

    head_grad = dot(features, grad_logits, TN)
    head_sum = table_grad(head_grad)
    grad_feat = dot(grad_logits, head_t, NT)
    grad_final, gain_three = norm_back(grad_feat, normed_three, inverse_three, gains[2])
    grad_down = pair(grad_final.astype(BF))
    down_own = weight_grad(grad_down, hidden)
    grad_up = [(dot(grad_down, w) * s.astype(F32)).astype(BF) for w, s in zip(wdown, slope)]
    up_own = weight_grad(ffn_in, grad_up)
    grad_mid, gain_two = norm_back(branch(grad_up, wup, NT), normed_two, inverse_two, gains[1])
    grad_mid = grad_mid + grad_final
    grad_out = pair(grad_mid.astype(BF))
    out_own = weight_grad(grad_out, mixed)
    grad_mixed = [dot(grad_out, w).astype(BF) for w in wout]
    grad_qkv = [
        attention_back(c_index, starts_col, q, o, g, ls)
        for q, o, g, ls in zip(qkv, mixed, grad_mixed, lse)
    ]
    qkv_own = weight_grad(attn_in, grad_qkv)
    grad_start, gain_one = norm_back(
        branch(grad_qkv, wqkv, NT), normed_one, inverse_one, gains[0]
    )
    grad_start = grad_start + grad_mid
    embed_grad = dot((grad_start * math.sqrt(width)).astype(BF), one_hot[:, :vocab], TN)
    gain_grad = jnp.stack([gain_one, gain_two, gain_three], 1)
    embed_sum = table_grad(jnp.concatenate([embed_grad, gain_grad], 1))

    sums = jnp.concatenate(
        [sum_z(*v, 1) for v in (qkv_own, out_own, up_own, down_own)], 1
    )
    keep_g, send_g = halves(sums, 0)
    got_g = place.swap_c(send_g)
    chunks_k = [keep_g[:, edges[i] : edges[i + 1]] for i in range(4)]
    chunks_g = [got_g[:, edges[i] : edges[i + 1]] for i in range(4)]
    qkv_g = place.in_order(
        chunks_k[0].reshape(feat, 3, -1), chunks_g[0].reshape(feat, 3, -1), 2
    )
    out_g = place.in_order(chunks_k[1].T, chunks_g[1].T, 0)
    up_g = place.in_order(chunks_k[2], chunks_g[2], 1)
    down_g = place.in_order(chunks_k[3].T, chunks_g[3].T, 0)
    table_g = jnp.stack([embed_sum[:, :vocab].T, head_sum.T])
    gain_g = embed_sum[:, vocab:].T
    summed = (qkv_g, out_g, up_g, down_g, table_g, gain_g)

    stats = place.total(jnp.stack([loss_local, jnp.sum(my_mask)]))
    loss_all, count_all = stats[0], stats[1]
    squares = (
        jnp.sum(sums * sums) + jnp.sum(embed_sum * embed_sum) + jnp.sum(head_sum * head_sum)
    )
    square_all = place.total(squares.reshape(1))[0] / (count_all * count_all)
    norm_all = jnp.sqrt(square_all)
    factor = jnp.minimum(1.0, CLIP_NORM / (norm_all + 1e-06))
    masters = (qkv_master, out_master, up_master, down_master, table_master, gain_master)
    firsts = (qkv_first, out_first, up_first, down_first, table_first, gain_first)
    seconds = (qkv_second, out_second, up_second, down_second, table_second, gain_second)
    results = []
    for i in range(6):
        step_rate = RATE_GAIN if i == 5 else RATE_MATRIX
        decay_rate = 0.0 if i == 5 else DECAY_RATE
        clipped = summed[i] / count_all * factor
        results.extend(
            adam_update(masters[i], firsts[i], seconds[i], clipped, step_rate, decay_rate)
        )
    return tuple(results) + (loss_all, count_all, norm_all)


def solution(mesh):
    rows, cols = P("dp", None, "tensor"), P("tensor", "dp")
    plain, both, gain = P("dp", "tensor"), P(None, None, ("dp", "tensor")), P(None, ("dp", "tensor"))
    kinds = (rows, cols, plain, cols, both, gain)
    in_specs = (P("dp", None),) * 3 + tuple(k for k in kinds for _ in range(3))
    out_specs = tuple(k for k in kinds for _ in range(4)) + (P(),) * 3
    return jax.shard_map(body, mesh=mesh, in_specs=in_specs, out_specs=out_specs, check_vma=False)
```

time: 1640 us -> 776 us (0.47)
  waiting for transfers between devices: 967 us -> 210 us
  blocking collectives: 159 us -> 0 us
  starting transfers between devices: 2.86 us -> 127 us
  matrix products: 208 us -> 125 us
  local copies, waits for them, and re-layouts: 134 us -> 182 us
  other arithmetic: 119 us -> 71.1 us
  Pallas kernels: 0 us -> 36.3 us
    reduce_scatter x12 -> x0, waiting for transfers between devices: 346 us -> none  [the longest x4 156 us: branch_rows(): lax.psum_scatter(jnp.dot(left, right, preferred_element_type=jnp.float32)...]
    unnamed x28 -> x0, waiting for transfers between devices: 329 us -> none
    all_gather x12 -> x0, waiting for transfers between devices: 292 us -> none  [the longest x4 153 us: gather_rows(): return lax.all_gather(values, 'tensor', axis=0, tiled=True)]
    ppermute x0 -> x111, waiting for transfers between devices: none -> 210 us  [the longest x18 67.2 us: to_z(): return lax.ppermute(value, 'tensor', [(i, (i + k) % n) for i in range(n)])]
    ppermute x0 -> x111, starting transfers between devices: none -> 127 us  [the longest x24 45.1 us: from_z(): return lax.ppermute(value, 'tensor', [((i + k) % n, i) for i in range(n)])]
    dot_general x58 -> x53, matrix products: 208 us -> 125 us  [dot(): return lax.dot_general(left, right, dims, preferred_element_type=F32)]
    psum x2 -> x0, blocking collectives: 80.1 us -> none  [the longest x1 40.2 us: body(): lax.psum((loss_local, squares / (count_all * count_all)), ('dp', 'tensor'))]
    all_gather x2 -> x0, blocking collectives: 79.3 us -> none  [the longest x1 69.9 us: body(): lax.all_gather(gain_master.astype(jnp.bfloat16), ('dp', 'tensor'), axis=1...]
  transfers between devices with their start and end apart: 26 -> 111, of which waited for: 21 -> 40; matrix products, arithmetic and copies ran while one was open for 22% -> 37% of each run, Pallas kernels for 0% -> 1%
where the time goes in v1:
time: 776 us; the launch traced here: 764 us
  waiting for transfers between devices  210 us (27%)
  local copies, waits for them, and re-layouts  182 us (23%)
  starting transfers between devices  127 us (16%)
  matrix products  125 us (16%)
  other arithmetic  71.1 us (9%)
  Pallas kernels  36.3 us (5%)
  between operations  14 us (2%)
    dot_general x53, matrix products, dot(): return lax.dot_general(left, right, dims, preferred_element_type=F32)  125 us
    ppermute x18, waiting for transfers between devices, to_z(): return lax.ppermute(value, 'tensor', [(i, (i + k) % n) for i in range(n)])  67.2 us
    ppermute x26, waiting for transfers between devices, swap_x(): return lax.ppermute(value, 'dp', [(i, i ^ 2) for i in range(self.dp)])  64.1 us
    ppermute x24, waiting for transfers between devices, from_z(): return lax.ppermute(value, 'tensor', [((i + k) % n, i) for i in range(n)])  49.9 us
    ppermute x24, starting transfers between devices, from_z(): return lax.ppermute(value, 'tensor', [((i + k) % n, i) for i in range(n)])  45.1 us
    unnamed x437, local copies, waits for them, and re-layouts  42.8 us
    ppermute x26, starting transfers between devices, swap_x(): return lax.ppermute(value, 'dp', [(i, i ^ 2) for i in range(self.dp)])  29.9 us
    concatenate x3, local copies, waits for them, and re-layouts, body(): embed_sum = table_grad(jnp.concatenate([embed_grad, gain_grad], 1))  23.5 us
  transfers between devices with their start and end apart: 111, of which 40 were waited for; matrix products, arithmetic and copies ran while one was open for 37% of the time, Pallas kernels for 1%

profile of v1, /device:TPU:0, one launch (start us, length us, event | category | flops | bytes accessed | tf_op | source)
XLA Modules:
  0.0 764.4 jit_solution(15431030754267543609)
XLA Ops:
  22.1 5.0 collective-permute-start.5
  32.8 9.6 %collective-permute-done.2 = bf16[32,1028]{1,0:T(8,128)(2,1)S(1)} collective-permute-done((bf16[32,1028]{1,0:T(8,128)(2,1)S(1)}, bf16[32,1028]{1,0:T(8,128)(2,1)S(1)}, u32[]{:S(2)}, u32[]{:S(2)}) %collective-permute-start.2) | collective-permute-done | bytes 65824 | tf_op jit(solution)/shard_map/ppermute | solution.py:71
  42.4 7.7 %collective-permute-start.4 = (bf16[32,1028]{1,0:T(8,128)(2,1)S(1)}, bf16[32,1028]{1,0:T(8,128)(2,1)S(1)}, u32[]{:S(2)}, u32[]{:S(2)}) collective-permute-start(bf16[32,1028]{1,0:T(8,128)(2,1)S(1)} %copy-done.151), channel_id=1, source_target_pairs={{3,0},{0,1},{1,2},{2,3},{7,4},{4,5},{5,6},{6,7},{11,8},{8,9},{9,10... | collective-permute-start | bytes 197384 | tf_op jit(solution)/shard_map/ppermute | solution.py:71
  60.7 5.6 collective-permute-done.13
  66.3 4.6 collective-permute-start.14
  71.0 5.1 collective-permute-done.14
  80.5 7.4 collective-permute-done.17
  94.2 23.3 %collective-permute-done.18 = bf16[64,1028]{1,0:T(8,128)(2,1)S(1)} collective-permute-done((bf16[64,1028]{1,0:T(8,128)(2,1)S(1)}, bf16[64,1028]{1,0:T(8,128)(2,1)S(1)}, u32[]{:S(2)}, u32[]{:S(2)}) %collective-permute-start.18) | collective-permute-done | bytes 131616 | tf_op jit(solution)/shard_map/ppermute | solution.py:59
  126.8 4.3 collective-permute-done.23
  153.5 10.0 %collective-permute-done.33 = bf16[256,512]{0,1:T(8,128)(2,1)} collective-permute-done((bf16[256,512]{0,1:T(8,128)(2,1)}, bf16[256,512]{0,1:T(8,128)(2,1)}, u32[]{:S(2)}, u32[]{:S(2)}) %collective-permute-start.33) | collective-permute-done | bytes 262176 | tf_op jit(solution)/shard_map/ppermute | solution.py:71
  178.3 4.5 copy.391
  182.8 5.4 reshape.335
  188.3 8.8 %fusion.239 = (f32[512]{0:T(512)S(1)}, f32[512,1024]{1,0:T(8,128)S(1)}) fusion(f32[1024]{0:T(1024)S(1)} %fusion.152, f32[512]{0:T(512)S(1)} %copy-done.178, pred[1024]{0:T(1024)(128)(4,1)S(1)} %copy-done.181, bf16[1024,1028]{0,1:T(8,128)(2,1)S(1)} %reshape.335, s32[512]{0:T(512)S(1)} %bitcast.340), kind=kOutput, calls=%fused_computation.536 | convolution fusion | flops 1081083392 | bytes 4213760 | tf_op jit(solution)/shard_map/dot_general | solution.py:31
  207.8 9.8 %collective-permute-done.46 = bf16[64,1025]{1,0:T(8,128)(2,1)S(1)} collective-permute-done((bf16[64,1025]{1,0:T(8,128)(2,1)S(1)}, bf16[64,1025]{1,0:T(8,128)(2,1)S(1)}, u32[]{:S(2)}, u32[]{:S(2)}) %collective-permute-start.46) | collective-permute-done | bytes 131232 | tf_op jit(solution)/shard_map/ppermute | solution.py:59
  224.0 7.9 %attend.2 = (bf16[2,512,256]{2,1,0:T(8,128)(2,1)S(1)}, f32[2,1024,128]{2,1,0:T(8,128)S(1)}) custom-call(s32[1]{0:T(128)} %bitcast.31.c_ref, s32[1024,1]{1,0:T(8,128)S(1)} %select_select_fusion.start_ref, bf16[2,512,768]{2,1,0:T(8,128)(2,1)S(1)} %bitcast.307), custom_call_target="tpu_custom_call" | custom-call | flops 2147483648 | bytes 4718592 | tf_op jit(solution)/shard_map/attend/pallas_call | solution.py:214
  233.8 7.7 %attend.3 = (bf16[2,512,256]{2,1,0:T(8,128)(2,1)S(1)}, f32[2,1024,128]{2,1,0:T(8,128)S(1)}) custom-call(s32[1]{0:T(128)} %bitcast.31.c_ref, s32[1024,1]{1,0:T(8,128)S(1)} %select_select_fusion.start_ref, bf16[2,512,768]{2,1,0:T(8,128)(2,1)S(1)} %bitcast.305), custom_call_target="tpu_custom_call" | custom-call | flops 2147483648 | bytes 4718592 | tf_op jit(solution)/shard_map/attend/pallas_call | solution.py:214
  265.6 5.9 multiply_convert_fusion.2
  273.7 6.1 multiply_convert_fusion.3
  284.6 6.6 copy.395
  291.2 6.3 reshape.341
  316.1 6.6 reshape.349
  322.7 5.2 constant_dynamic-slice_fusion.1
  331.1 6.3 copy.419
  339.2 4.8 copy.421
  357.3 3.8 collective-permute-start.85
  367.5 4.3 convolution_convert_fusion.3
  372.7 3.5 convolution_convert_fusion.2
  376.8 5.0 multiply_convert_fusion.1
  381.9 5.6 multiply_convert_fusion
  393.6 3.5 copy.422
  431.2 13.1 %collective-permute-done.67 = bf16[512,1024]{1,0:T(8,128)(2,1)S(1)} collective-permute-done((bf16[512,1024]{1,0:T(8,128)(2,1)S(1)}, bf16[512,1024]{1,0:T(8,128)(2,1)S(1)}, u32[]{:S(2)}, u32[]{:S(2)}) %collective-permute-start.67) | collective-permute-done | bytes 1048608 | tf_op jit(solution)/shard_map/ppermute | solution.py:59
  464.5 3.5 collective-permute-start.73
  470.3 22.0 %collective-permute-done.79 = bf16[256,512]{1,0:T(8,128)(2,1)S(1)} collective-permute-done((bf16[256,512]{1,0:T(8,128)(2,1)S(1)}, bf16[256,512]{1,0:T(8,128)(2,1)S(1)}, u32[]{:S(2)}, u32[]{:S(2)}) %collective-permute-start.79) | collective-permute-done | bytes 262176 | tf_op jit(solution)/shard_map/ppermute | solution.py:75
  493.2 12.7 %collective-permute-done.72 = bf16[256,512]{1,0:T(8,128)(2,1)S(1)} collective-permute-done((bf16[256,512]{1,0:T(8,128)(2,1)S(1)}, bf16[256,512]{1,0:T(8,128)(2,1)S(1)}, u32[]{:S(2)}, u32[]{:S(2)}) %collective-permute-start.72) | collective-permute-done | bytes 262176 | tf_op jit(solution)/shard_map/ppermute | solution.py:75
  508.5 10.3 %attend_back.2 = bf16[2,512,768]{2,1,0:T(8,128)(2,1)S(1)} custom-call(s32[1]{0:T(128)} %bitcast.31.c_ref, s32[1024,1]{1,0:T(8,128)S(1)} %select_select_fusion.start_ref, bf16[2,512,768]{2,1,0:T(8,128)(2,1)S(1)} %bitcast.308, bf16[2,512,256]{2,1,0:T(8,128)(2,1)S(1)} %get-tuple-element.274.o_ref, bf16[2,512,256]{2,1,0:T(8,128)(2,1)S(1)} %bitcast.310, ...), custom_call_target="tpu_custom_call" | custom-call | flops 5368709120 | bytes 6291456 | tf_op jit(solution)/shard_map/attend_back/pallas_call | solution.py:246
  532.1 10.4 %attend_back.3 = bf16[2,512,768]{2,1,0:T(8,128)(2,1)S(1)} custom-call(s32[1]{0:T(128)} %bitcast.31.c_ref, s32[1024,1]{1,0:T(8,128)S(1)} %copy-done.5, bf16[2,512,768]{2,1,0:T(8,128)(2,1)S(1)} %bitcast.306, bf16[2,512,256]{2,1,0:T(8,128)(2,1)S(1)} %copy-done.3, bf16[2,512,256]{2,1,0:T(8,128)(2,1)S(1)} %bitcast.309, f32[2,1024,128]{2,1,0:T(8,128)S(1)} %copy-done.11), custom_call_target="tpu_custom_call" | custom-call | flops 5368709120 | bytes 6291456 | tf_op jit(solution)/shard_map/attend_back/pallas_call | solution.py:246
  555.2 9.4 %collective-permute-done.61 = bf16[256,256]{0,1:T(8,128)(2,1)S(1)} collective-permute-done((bf16[256,256]{0,1:T(8,128)(2,1)S(1)}, bf16[256,256]{0,1:T(8,128)(2,1)S(1)}, u32[]{:S(2)}, u32[]{:S(2)}) %collective-permute-start.61) | collective-permute-done | bytes 131104 | tf_op jit(solution)/shard_map/ppermute | solution.py:67
  575.9 3.9 fusion.12
  579.8 6.7 concatenate.191
  586.4 5.0 copy.404
  591.4 11.9 %concatenate.195 = f32[4,2,128,1028]{2,3,1,0:T(8,128)} concatenate(f32[4,2,128,1025]{2,3,1,0:T(8,128)} %copy.404, f32[4,2,128,1]{2,3,1,0:T(1,128)S(1)} %bitcast.346, f32[4,2,128,1]{2,3,1,0:T(1,128)S(1)} %bitcast.345, f32[4,2,128,1]{2,3,1,0:T(1,128)S(1)} %bitcast.344), dimensions={3} | concatenate | bytes 8421376 | tf_op jit(solution)/shard_map/concatenate | solution.py:587
  605.2 4.6 copy.405
  612.4 3.8 collective-permute-start.59
  621.8 12.5 %collective-permute-done.58 = bf16[256,384]{1,0:T(8,128)(2,1)S(1)} collective-permute-done((bf16[256,384]{1,0:T(8,128)(2,1)}, bf16[256,384]{1,0:T(8,128)(2,1)S(1)}, u32[]{:S(2)}, u32[]{:S(2)}) %collective-permute-start.58) | collective-permute-done | bytes 196640 | tf_op jit(solution)/shard_map/ppermute | solution.py:75
  645.7 6.4 copy.452
  652.0 3.9 convert.59
  665.2 3.9 collective-permute-done.90
  696.9 15.6 %collective-permute-done.95 = bf16[1,32,1028]{1,2,0:T(8,128)(2,1)} collective-permute-done((bf16[1,32,1028]{1,2,0:T(8,128)(2,1)}, bf16[1,32,1028]{1,2,0:T(8,128)(2,1)}, u32[]{:S(2)}, u32[]{:S(2)}) %collective-permute-start.95) | collective-permute-done | bytes 65824 | tf_op jit(solution)/shard_map/ppermute | solution.py:75
  (863 shorter events, 390.4 us)
Async XLA Ops:
  22.1 30.3 %collective-permute-start.5 = (bf16[256,384]{0,1:T(8,128)(2,1)S(1)}, bf16[256,384]{0,1:T(8,128)(2,1)S(1)}, u32[]{:S(2)}, u32[]{:S(2)}) collective-permute-start(bf16[256,384]{0,1:T(8,128)(2,1)S(1)} %fusion.141), channel_id=1, source_target_pairs={{1,0},{2,1},{3,2},{0,3},{5,4},{6,5},{7,6},{4,7},{9,8},{10,9},{11,1... | collective-permute-start | bytes 589832 | tf_op jit(solution)/shard_map/ppermute | solution.py:71
  27.1 25.3 %collective-permute-start.6 = (bf16[256,384]{0,1:T(8,128)(2,1)S(1)}, bf16[256,384]{0,1:T(8,128)(2,1)S(1)}, u32[]{:S(2)}, u32[]{:S(2)}) collective-permute-start(bf16[256,384]{0,1:T(8,128)(2,1)S(1)} %fusion.141), channel_id=1, source_target_pairs={{2,0},{3,1},{0,2},{1,3},{6,4},{7,5},{4,6},{5,7},{10,8},{11,9},{8,1... | collective-permute-start | bytes 589832 | tf_op jit(solution)/shard_map/ppermute | solution.py:71
  27.1 25.3 %collective-permute-start.7 = (bf16[256,384]{0,1:T(8,128)(2,1)S(1)}, bf16[256,384]{0,1:T(8,128)(2,1)S(1)}, u32[]{:S(2)}, u32[]{:S(2)}) collective-permute-start(bf16[256,384]{0,1:T(8,128)(2,1)S(1)} %fusion.141), channel_id=1, source_target_pairs={{3,0},{0,1},{1,2},{2,3},{7,4},{4,5},{5,6},{6,7},{11,8},{8,9},{9,10... | collective-permute-start | bytes 589832 | tf_op jit(solution)/shard_map/ppermute | solution.py:71
  53.7 34.3 %collective-permute-start.10 = (bf16[2,256,768]{1,2,0:T(8,128)(2,1)S(1)}, bf16[2,256,768]{1,2,0:T(8,128)(2,1)S(1)}, u32[]{:S(2)}, u32[]{:S(2)}) collective-permute-start(bf16[2,256,768]{1,2,0:T(8,128)(2,1)S(1)} %pad_maximum_fusion.27), channel_id=1, source_target_pairs={{0,8},{4,12},{8,0},{12,4},{16,24},{20,28},{24,16},{28,20},{1,9},{5... | collective-permute-start | bytes 2359304 | tf_op jit(solution)/shard_map/ppermute | solution.py:59
  55.2 32.7 %collective-permute-start.11 = (bf16[2,256,768]{1,2,0:T(8,128)(2,1)S(1)}, bf16[2,256,768]{1,2,0:T(8,128)(2,1)S(1)}, u32[]{:S(2)}, u32[]{:S(2)}) collective-permute-start(bf16[2,256,768]{1,2,0:T(8,128)(2,1)S(1)} %pad_maximum_fusion.27), channel_id=1, source_target_pairs={{16,0},{20,4},{24,8},{28,12},{0,16},{4,20},{8,24},{12,28},{17,1},{... | collective-permute-start | bytes 2359304 | tf_op jit(solution)/shard_map/ppermute | solution.py:63
  88.2 42.9 %collective-permute-start.24 = (bf16[2,256,1024]{1,2,0:T(8,128)(2,1)S(1)}, bf16[2,256,1024]{1,2,0:T(8,128)(2,1)S(1)}, u32[]{:S(2)}, u32[]{:S(2)}) collective-permute-start(bf16[2,256,1024]{1,2,0:T(8,128)(2,1)S(1)} %pad_maximum_fusion.25), channel_id=1, source_target_pairs={{0,8},{4,12},{8,0},{12,4},{16,24},{20,28},{24,16},{28,20},{1,9},{5... | collective-permute-start | bytes 3145736 | tf_op jit(solution)/shard_map/ppermute | solution.py:59
  89.8 41.4 %collective-permute-start.25 = (bf16[2,256,1024]{1,2,0:T(8,128)(2,1)S(1)}, bf16[2,256,1024]{1,2,0:T(8,128)(2,1)S(1)}, u32[]{:S(2)}, u32[]{:S(2)}) collective-permute-start(bf16[2,256,1024]{1,2,0:T(8,128)(2,1)S(1)} %pad_maximum_fusion.25), channel_id=1, source_target_pairs={{16,0},{20,4},{24,8},{28,12},{0,16},{4,20},{8,24},{12,28},{17,1},{... | collective-permute-start | bytes 3145736 | tf_op jit(solution)/shard_map/ppermute | solution.py:63
  91.0 26.5 %collective-permute-start.18 = (bf16[64,1028]{1,0:T(8,128)(2,1)S(1)}, bf16[64,1028]{1,0:T(8,128)(2,1)S(1)}, u32[]{:S(2)}, u32[]{:S(2)}) collective-permute-start(bf16[64,1028]{1,0:T(8,128)(2,1)S(1)} %slice_bitcast_fusion.36), channel_id=1, source_target_pairs={{0,8},{4,12},{8,0},{12,4},{16,24},{20,28},{24,16},{28,20},{1,9},{5... | collective-permute-start | bytes 394760 | tf_op jit(solution)/shard_map/ppermute | solution.py:59
  91.9 27.1 %collective-permute-start.19 = (bf16[64,1028]{1,0:T(8,128)(2,1)S(1)}, bf16[64,1028]{1,0:T(8,128)(2,1)S(1)}, u32[]{:S(2)}, u32[]{:S(2)}) collective-permute-start(bf16[64,1028]{1,0:T(8,128)(2,1)S(1)} %slice_bitcast_fusion.35), channel_id=1, source_target_pairs={{16,0},{20,4},{24,8},{28,12},{0,16},{4,20},{8,24},{12,28},{17,1},{... | collective-permute-start | bytes 394760 | tf_op jit(solution)/shard_map/ppermute | solution.py:63
  92.6 30.6 %collective-permute-start.22 = (bf16[2,256,256]{1,2,0:T(8,128)(2,1)S(1)}, bf16[2,256,256]{1,2,0:T(8,128)(2,1)S(1)}, u32[]{:S(2)}, u32[]{:S(2)}) collective-permute-start(bf16[2,256,256]{1,2,0:T(8,128)(2,1)S(1)} %pad_maximum_fusion.35), channel_id=1, source_target_pairs={{0,8},{4,12},{8,0},{12,4},{16,24},{20,28},{24,16},{28,20},{1,9},{5... | collective-permute-start | bytes 786440 | tf_op jit(solution)/shard_map/ppermute | solution.py:59
  139.1 24.4 %collective-permute-start.30 = (bf16[256,1024]{0,1:T(8,128)(2,1)}, bf16[256,1024]{0,1:T(8,128)(2,1)}, u32[]{:S(2)}, u32[]{:S(2)}) collective-permute-start(bf16[256,1024]{0,1:T(8,128)(2,1)} %slice_bitcast_fusion.24), channel_id=1, source_target_pairs={{0,8},{4,12},{8,0},{12,4},{16,24},{20,28},{24,16},{28,20},{1,9},{5... | collective-permute-start | bytes 1572872 | tf_op jit(solution)/shard_map/ppermute | solution.py:59
  139.9 23.7 %collective-permute-start.31 = (bf16[256,1024]{0,1:T(8,128)(2,1)}, bf16[256,1024]{0,1:T(8,128)(2,1)}, u32[]{:S(2)}, u32[]{:S(2)}) collective-permute-start(bf16[256,1024]{0,1:T(8,128)(2,1)} %slice_bitcast_fusion.23), channel_id=1, source_target_pairs={{16,0},{20,4},{24,8},{28,12},{0,16},{4,20},{8,24},{12,28},{17,1},{... | collective-permute-start | bytes 1572872 | tf_op jit(solution)/shard_map/ppermute | solution.py:63
  153.5 21.7 %collective-permute-start.26 = (bf16[4,1,128,1028]{2,0,3,1:T(4,128)(2,1)}, bf16[4,1,128,1028]{2,0,3,1:T(4,128)(2,1)}, u32[]{:S(2)}, u32[]{:S(2)}) collective-permute-start(bf16[4,1,128,1028]{2,0,3,1:T(4,128)(2,1)} %copy.388), channel_id=1, source_target_pairs={{0,4},{4,0},{8,12},{12,8},{16,20},{20,16},{24,28},{28,24},{1,5},{5... | collective-permute-start | bytes 3158024 | tf_op jit(solution)/shard_map/ppermute | solution.py:56
  166.8 32.1 %collective-permute-start.40 = (bf16[2,256,1024]{1,2,0:T(8,128)(2,1)}, bf16[2,256,1024]{1,2,0:T(8,128)(2,1)}, u32[]{:S(2)}, u32[]{:S(2)}) collective-permute-start(bf16[2,256,1024]{1,2,0:T(8,128)(2,1)} %pad_maximum_fusion.26), channel_id=1, source_target_pairs={{0,8},{4,12},{8,0},{12,4},{16,24},{20,28},{24,16},{28,20},{1,9},{5... | collective-permute-start | bytes 3145736 | tf_op jit(solution)/shard_map/ppermute | solution.py:59
  168.0 30.9 %collective-permute-start.41 = (bf16[2,256,1024]{1,2,0:T(8,128)(2,1)}, bf16[2,256,1024]{1,2,0:T(8,128)(2,1)}, u32[]{:S(2)}, u32[]{:S(2)}) collective-permute-start(bf16[2,256,1024]{1,2,0:T(8,128)(2,1)} %pad_maximum_fusion.26), channel_id=1, source_target_pairs={{16,0},{20,4},{24,8},{28,12},{0,16},{4,20},{8,24},{12,28},{17,1},{... | collective-permute-start | bytes 3145736 | tf_op jit(solution)/shard_map/ppermute | solution.py:63
  169.5 29.4 %collective-permute-start.42 = (bf16[2,64,1025]{2,1,0:T(8,128)(2,1)}, bf16[2,64,1025]{2,1,0:T(8,128)(2,1)}, u32[]{:S(2)}, u32[]{:S(2)}) collective-permute-start(bf16[2,64,1025]{2,1,0:T(8,128)(2,1)} %pad_maximum_fusion.33), channel_id=1, source_target_pairs={{0,8},{4,12},{8,0},{12,4},{16,24},{20,28},{24,16},{28,20},{1,9},{5... | collective-permute-start | bytes 787208 | tf_op jit(solution)/shard_map/ppermute | solution.py:59
  170.2 28.7 %collective-permute-start.43 = (bf16[2,64,1025]{2,1,0:T(8,128)(2,1)}, bf16[2,64,1025]{2,1,0:T(8,128)(2,1)}, u32[]{:S(2)}, u32[]{:S(2)}) collective-permute-start(bf16[2,64,1025]{2,1,0:T(8,128)(2,1)} %pad_maximum_fusion.33), channel_id=1, source_target_pairs={{16,0},{20,4},{24,8},{28,12},{0,16},{4,20},{8,24},{12,28},{17,1},{... | collective-permute-start | bytes 787208 | tf_op jit(solution)/shard_map/ppermute | solution.py:63
  198.8 23.2 %collective-permute-start.27 = (bf16[512,1024]{1,0:T(8,128)(2,1)S(1)}, bf16[512,1024]{1,0:T(8,128)(2,1)S(1)}, u32[]{:S(2)}, u32[]{:S(2)}) collective-permute-start(bf16[512,1024]{1,0:T(8,128)(2,1)S(1)} %multiply_convert_fusion.8), channel_id=1, source_target_pairs={{0,4},{4,0},{8,12},{12,8},{16,20},{20,16},{24,28},{28,24},{1,5},{5... | collective-permute-start | bytes 3145736 | tf_op jit(solution)/shard_map/ppermute | solution.py:56
  200.5 19.1 %collective-permute-start.44 = (bf16[256,1024]{0,1:T(8,128)(2,1)S(1)}, bf16[256,1024]{0,1:T(8,128)(2,1)S(1)}, u32[]{:S(2)}, u32[]{:S(2)}) collective-permute-start(bf16[256,1024]{0,1:T(8,128)(2,1)S(1)} %slice_bitcast_fusion.19), channel_id=1, source_target_pairs={{0,8},{4,12},{8,0},{12,4},{16,24},{20,28},{24,16},{28,20},{1,9},{5... | collective-permute-start | bytes 1572872 | tf_op jit(solution)/shard_map/ppermute | solution.py:59
  282.1 18.7 %collective-permute-start.48 = (bf16[512,1024]{1,0:T(8,128)(2,1)}, bf16[512,1024]{1,0:T(8,128)(2,1)}, u32[]{:S(2)}, u32[]{:S(2)}) collective-permute-start(bf16[512,1024]{1,0:T(8,128)(2,1)} %add_convert_fusion.2), channel_id=1, source_target_pairs={{0,4},{4,0},{8,12},{12,8},{16,20},{20,16},{24,28},{28,24},{1,5},{5... | collective-permute-start | bytes 3145736 | tf_op jit(solution)/shard_map/ppermute | solution.py:56
  316.0 51.5 %collective-permute-start.50 = (bf16[512,1024]{1,0:T(8,128)(2,1)}, bf16[512,1024]{1,0:T(8,128)(2,1)}, u32[]{:S(2)}, u32[]{:S(2)}) collective-permute-start(bf16[512,1024]{1,0:T(8,128)(2,1)} %get-tuple-element.575), channel_id=1, source_target_pairs={{0,4},{4,0},{8,12},{12,8},{16,20},{20,16},{24,28},{28,24},{1,5},{5... | collective-permute-start | bytes 3145736 | tf_op jit(solution)/shard_map/ppermute | solution.py:56
  344.0 49.6 %collective-permute-start.97 = (bf16[4,128,1025]{1,0,2:T(4,128)(2,1)}, bf16[4,128,1025]{1,0,2:T(4,128)(2,1)}, u32[]{:S(2)}, u32[]{:S(2)}) collective-permute-start(bf16[4,128,1025]{1,0,2:T(4,128)(2,1)} %copy.421), channel_id=1, source_target_pairs={{0,4},{4,0},{8,12},{12,8},{16,20},{20,16},{24,28},{28,24},{1,5},{5... | collective-permute-start | bytes 3148808 | tf_op jit(solution)/shard_map/ppermute | solution.py:56
  371.8 54.0 %collective-permute-start.74 = (bf16[512,1024]{1,0:T(8,128)(2,1)}, bf16[512,1024]{1,0:T(8,128)(2,1)}, u32[]{:S(2)}, u32[]{:S(2)}) collective-permute-start(bf16[512,1024]{1,0:T(8,128)(2,1)} %convolution_convert_fusion.3), channel_id=1, source_target_pairs={{0,8},{4,12},{8,0},{12,4},{16,24},{20,28},{24,16},{28,20},{1,9},{5... | collective-permute-start | bytes 3145736 | tf_op jit(solution)/shard_map/ppermute | solution.py:59
  376.2 51.8 %collective-permute-start.77 = (bf16[512,1024]{1,0:T(8,128)(2,1)}, bf16[512,1024]{1,0:T(8,128)(2,1)}, u32[]{:S(2)}, u32[]{:S(2)}) collective-permute-start(bf16[512,1024]{1,0:T(8,128)(2,1)} %convolution_convert_fusion.2), channel_id=1, source_target_pairs={{0,16},{4,20},{8,24},{12,28},{16,0},{20,4},{24,8},{28,12},{1,17},{... | collective-permute-start | bytes 3145736 | tf_op jit(solution)/shard_map/ppermute | solution.py:67
  422.1 22.2 %collective-permute-start.67 = (bf16[512,1024]{1,0:T(8,128)(2,1)S(1)}, bf16[512,1024]{1,0:T(8,128)(2,1)S(1)}, u32[]{:S(2)}, u32[]{:S(2)}) collective-permute-start(bf16[512,1024]{1,0:T(8,128)(2,1)S(1)} %convolution_convert_fusion.5), channel_id=1, source_target_pairs={{0,8},{4,12},{8,0},{12,4},{16,24},{20,28},{24,16},{28,20},{1,9},{5... | collective-permute-start | bytes 3145736 | tf_op jit(solution)/shard_map/ppermute | solution.py:59
  423.0 25.8 %collective-permute-start.70 = (bf16[512,1024]{1,0:T(8,128)(2,1)S(1)}, bf16[512,1024]{1,0:T(8,128)(2,1)S(1)}, u32[]{:S(2)}, u32[]{:S(2)}) collective-permute-start(bf16[512,1024]{1,0:T(8,128)(2,1)S(1)} %convolution_convert_fusion.4), channel_id=1, source_target_pairs={{0,16},{4,20},{8,24},{12,28},{16,0},{20,4},{24,8},{28,12},{1,17},{... | collective-permute-start | bytes 3145736 | tf_op jit(solution)/shard_map/ppermute | solution.py:67
  425.2 26.9 %collective-permute-start.51 = (bf16[512,1024]{1,0:T(8,128)(2,1)S(1)}, bf16[512,1024]{1,0:T(8,128)(2,1)S(1)}, u32[]{:S(2)}, u32[]{:S(2)}) collective-permute-start(bf16[512,1024]{1,0:T(8,128)(2,1)S(1)} %copy-done.185), channel_id=1, source_target_pairs={{0,4},{4,0},{8,12},{12,8},{16,20},{20,16},{24,28},{28,24},{1,5},{5... | collective-permute-start | bytes 3145736 | tf_op jit(solution)/shard_map/ppermute | solution.py:56
  428.0 31.2 %collective-permute-start.75 = (bf16[256,1024]{1,0:T(8,128)(2,1)S(1)}, bf16[256,1024]{1,0:T(8,128)(2,1)S(1)}, u32[]{:S(2)}, u32[]{:S(2)}) collective-permute-start(bf16[256,1024]{1,0:T(8,128)(2,1)S(1)} %fusion.31), channel_id=1, source_target_pairs={{0,16},{4,20},{8,24},{12,28},{16,0},{20,4},{24,8},{28,12},{1,17},{... | collective-permute-start | bytes 1572872 | tf_op jit(solution)/shard_map/ppermute | solution.py:67
  430.0 25.8 %collective-permute-start.78 = (bf16[256,1024]{1,0:T(8,128)(2,1)S(1)}, bf16[256,1024]{1,0:T(8,128)(2,1)S(1)}, u32[]{:S(2)}, u32[]{:S(2)}) collective-permute-start(bf16[256,1024]{1,0:T(8,128)(2,1)S(1)} %fusion.32), channel_id=1, source_target_pairs={{0,8},{4,12},{8,0},{12,4},{16,24},{20,28},{24,16},{28,20},{1,9},{5... | collective-permute-start | bytes 1572872 | tf_op jit(solution)/shard_map/ppermute | solution.py:59
  455.7 51.1 %collective-permute-start.52 = (bf16[512,1024]{1,0:T(8,128)(2,1)S(1)}, bf16[512,1024]{1,0:T(8,128)(2,1)S(1)}, u32[]{:S(2)}, u32[]{:S(2)}) collective-permute-start(bf16[512,1024]{1,0:T(8,128)(2,1)S(1)} %get-tuple-element.573), channel_id=1, source_target_pairs={{0,4},{4,0},{8,12},{12,8},{16,20},{20,16},{24,28},{28,24},{1,5},{5... | collective-permute-start | bytes 3145736 | tf_op jit(solution)/shard_map/ppermute | solution.py:56
  459.2 33.1 %collective-permute-start.79 = (bf16[256,512]{1,0:T(8,128)(2,1)S(1)}, bf16[256,512]{1,0:T(8,128)(2,1)S(1)}, u32[]{:S(2)}, u32[]{:S(2)}) collective-permute-start(bf16[256,512]{1,0:T(8,128)(2,1)S(1)} %get-tuple-element.629), channel_id=1, source_target_pairs={{0,2},{1,3},{2,0},{3,1},{4,6},{5,7},{6,4},{7,5},{8,10},{9,11},{10,... | collective-permute-start | bytes 786440 | tf_op jit(solution)/shard_map/ppermute | solution.py:75
  461.9 30.4 %collective-permute-start.76 = (bf16[256,512]{1,0:T(8,128)(2,1)S(1)}, bf16[256,512]{1,0:T(8,128)(2,1)S(1)}, u32[]{:S(2)}, u32[]{:S(2)}) collective-permute-start(bf16[256,512]{1,0:T(8,128)(2,1)S(1)} %split.157), channel_id=1, source_target_pairs={{0,1},{1,2},{2,3},{3,0},{4,5},{5,6},{6,7},{7,4},{8,9},{9,10},{10,1... | collective-permute-start | bytes 786440 | tf_op jit(solution)/shard_map/ppermute | solution.py:75
  464.5 28.7 %collective-permute-start.73 = (bf16[256,512]{1,0:T(8,128)(2,1)S(1)}, bf16[256,512]{1,0:T(8,128)(2,1)S(1)}, u32[]{:S(2)}, u32[]{:S(2)}) collective-permute-start(bf16[256,512]{1,0:T(8,128)(2,1)S(1)} %get-tuple-element.628), channel_id=1, source_target_pairs={{0,3},{1,0},{2,1},{3,2},{4,7},{5,4},{6,5},{7,6},{8,11},{9,8},{10,9... | collective-permute-start | bytes 786440 | tf_op jit(solution)/shard_map/ppermute | solution.py:75
  469.8 36.1 %collective-permute-start.72 = (bf16[256,512]{1,0:T(8,128)(2,1)S(1)}, bf16[256,512]{1,0:T(8,128)(2,1)S(1)}, u32[]{:S(2)}, u32[]{:S(2)}) collective-permute-start(bf16[256,512]{1,0:T(8,128)(2,1)S(1)} %get-tuple-element.627), channel_id=1, source_target_pairs={{0,2},{1,3},{2,0},{3,1},{4,6},{5,7},{6,4},{7,5},{8,10},{9,11},{10,... | collective-permute-start | bytes 786440 | tf_op jit(solution)/shard_map/ppermute | solution.py:75
  524.7 23.6 %collective-permute-start.60 = (bf16[512,256]{0,1:T(8,128)(2,1)}, bf16[512,256]{0,1:T(8,128)(2,1)}, u32[]{:S(2)}, u32[]{:S(2)}) collective-permute-start(bf16[512,256]{0,1:T(8,128)(2,1)} %convolution_convert_fusion.9), channel_id=1, source_target_pairs={{0,8},{4,12},{8,0},{12,4},{16,24},{20,28},{24,16},{28,20},{1,9},{5... | collective-permute-start | bytes 786440 | tf_op jit(solution)/shard_map/ppermute | solution.py:59
  527.3 18.7 %collective-permute-start.63 = (bf16[512,256]{0,1:T(8,128)(2,1)}, bf16[512,256]{0,1:T(8,128)(2,1)}, u32[]{:S(2)}, u32[]{:S(2)}) collective-permute-start(bf16[512,256]{0,1:T(8,128)(2,1)} %convolution_convert_fusion.8), channel_id=1, source_target_pairs={{0,16},{4,20},{8,24},{12,28},{16,0},{20,4},{24,8},{28,12},{1,17},{... | collective-permute-start | bytes 786440 | tf_op jit(solution)/shard_map/ppermute | solution.py:67
  530.1 39.5 %collective-permute-start.53 = (bf16[512,768]{1,0:T(8,128)(2,1)}, bf16[512,768]{1,0:T(8,128)(2,1)S(1)}, u32[]{:S(2)}, u32[]{:S(2)}) collective-permute-start(bf16[512,768]{1,0:T(8,128)(2,1)} %convolution_convert_fusion.7), channel_id=1, source_target_pairs={{0,8},{4,12},{8,0},{12,4},{16,24},{20,28},{24,16},{28,20},{1,9},{5... | collective-permute-start | bytes 2359304 | tf_op jit(solution)/shard_map/ppermute | solution.py:59
  543.7 27.6 %collective-permute-start.56 = (bf16[512,768]{1,0:T(8,128)(2,1)S(1)}, bf16[512,768]{1,0:T(8,128)(2,1)S(1)}, u32[]{:S(2)}, u32[]{:S(2)}) collective-permute-start(bf16[512,768]{1,0:T(8,128)(2,1)S(1)} %convolution_convert_fusion.6), channel_id=1, source_target_pairs={{0,16},{4,20},{8,24},{12,28},{16,0},{20,4},{24,8},{28,12},{1,17},{... | collective-permute-start | bytes 2359304 | tf_op jit(solution)/shard_map/ppermute | solution.py:67
  545.9 27.6 %collective-permute-start.88 = (bf16[512,1024]{1,0:T(8,128)(2,1)S(1)}, bf16[512,1024]{1,0:T(8,128)(2,1)S(1)}, u32[]{:S(2)}, u32[]{:S(2)}) collective-permute-start(bf16[512,1024]{1,0:T(8,128)(2,1)S(1)} %add_convert_fusion), channel_id=1, source_target_pairs={{0,4},{4,0},{8,12},{12,8},{16,20},{20,16},{24,28},{28,24},{1,5},{5... | collective-permute-start | bytes 3145736 | tf_op jit(solution)/shard_map/ppermute | solution.py:56
  555.2 62.7 %collective-permute-start.66 = (bf16[256,128]{0,1:T(8,128)(2,1)}, bf16[256,128]{0,1:T(8,128)(2,1)}, u32[]{:S(2)}, u32[]{:S(2)}) collective-permute-start(bf16[256,128]{0,1:T(8,128)(2,1)} %get-tuple-element.666), channel_id=1, source_target_pairs={{0,3},{1,0},{2,1},{3,2},{4,7},{5,4},{6,5},{7,6},{8,11},{9,8},{10,9... | collective-permute-start | bytes 196616 | tf_op jit(solution)/shard_map/ppermute | solution.py:75
  564.6 53.4 %collective-permute-start.65 = (bf16[256,128]{0,1:T(8,128)(2,1)}, bf16[256,128]{0,1:T(8,128)(2,1)}, u32[]{:S(2)}, u32[]{:S(2)}) collective-permute-start(bf16[256,128]{0,1:T(8,128)(2,1)} %get-tuple-element.665), channel_id=1, source_target_pairs={{0,2},{1,3},{2,0},{3,1},{4,6},{5,7},{6,4},{7,5},{8,10},{9,11},{10,... | collective-permute-start | bytes 196616 | tf_op jit(solution)/shard_map/ppermute | solution.py:75
  569.6 49.1 %collective-permute-start.62 = (bf16[256,128]{0,1:T(8,128)(2,1)}, bf16[256,128]{0,1:T(8,128)(2,1)}, u32[]{:S(2)}, u32[]{:S(2)}) collective-permute-start(bf16[256,128]{0,1:T(8,128)(2,1)} %split.161), channel_id=1, source_target_pairs={{0,1},{1,2},{2,3},{3,0},{4,5},{5,6},{6,7},{7,4},{8,9},{9,10},{10,1... | collective-permute-start | bytes 196616 | tf_op jit(solution)/shard_map/ppermute | solution.py:75
  571.3 41.1 %collective-permute-start.54 = (bf16[256,768]{1,0:T(8,128)(2,1)}, bf16[256,768]{1,0:T(8,128)(2,1)}, u32[]{:S(2)}, u32[]{:S(2)}) collective-permute-start(bf16[256,768]{1,0:T(8,128)(2,1)} %fusion.35), channel_id=1, source_target_pairs={{0,16},{4,20},{8,24},{12,28},{16,0},{20,4},{24,8},{28,12},{1,17},{... | collective-permute-start | bytes 1179656 | tf_op jit(solution)/shard_map/ppermute | solution.py:67
  573.6 36.3 %collective-permute-start.57 = (bf16[256,768]{1,0:T(8,128)(2,1)}, bf16[256,768]{1,0:T(8,128)(2,1)}, u32[]{:S(2)}, u32[]{:S(2)}) collective-permute-start(bf16[256,768]{1,0:T(8,128)(2,1)} %fusion.37), channel_id=1, source_target_pairs={{0,8},{4,12},{8,0},{12,4},{16,24},{20,28},{24,16},{28,20},{1,9},{5... | collective-permute-start | bytes 1179656 | tf_op jit(solution)/shard_map/ppermute | solution.py:59
  609.9 28.7 %collective-permute-start.89 = (bf16[4,128,1028]{1,0,2:T(4,128)(2,1)}, bf16[4,128,1028]{1,0,2:T(4,128)(2,1)}, u32[]{:S(2)}, u32[]{:S(2)}) collective-permute-start(bf16[4,128,1028]{1,0,2:T(4,128)(2,1)} %copy.405), channel_id=1, source_target_pairs={{0,4},{4,0},{8,12},{12,8},{16,20},{20,16},{24,28},{28,24},{1,5},{5... | collective-permute-start | bytes 3158024 | tf_op jit(solution)/shard_map/ppermute | solution.py:56
  638.6 24.6 %collective-permute-start.81 = (f32[128,1536]{1,0:T(8,128)}, f32[128,1536]{1,0:T(8,128)}, u32[]{:S(2)}, u32[]{:S(2)}) collective-permute-start(f32[128,1536]{1,0:T(8,128)} %constant_dynamic-slice_fusion.2), channel_id=1, source_target_pairs={{0,4},{4,0},{8,12},{12,8},{16,20},{20,16},{24,28},{28,24},{1,5},{5... | collective-permute-start | bytes 2359304 | tf_op jit(solution)/shard_map/ppermute | solution.py:56
  687.8 24.8 %collective-permute-start.95 = (bf16[1,32,1028]{1,2,0:T(8,128)(2,1)}, bf16[1,32,1028]{1,2,0:T(8,128)(2,1)}, u32[]{:S(2)}, u32[]{:S(2)}) collective-permute-start(bf16[1,32,1028]{1,2,0:T(8,128)(2,1)} %get-tuple-element.625), channel_id=1, source_target_pairs={{0,2},{1,3},{2,0},{3,1},{4,6},{5,7},{6,4},{7,5},{8,10},{9,11},{10,... | collective-permute-start | bytes 197384 | tf_op jit(solution)/shard_map/ppermute | solution.py:75
  691.4 21.2 %collective-permute-start.92 = (bf16[1,32,1028]{1,2,0:T(8,128)(2,1)}, bf16[1,32,1028]{1,2,0:T(8,128)(2,1)}, u32[]{:S(2)}, u32[]{:S(2)}) collective-permute-start(bf16[1,32,1028]{1,2,0:T(8,128)(2,1)} %split.156), channel_id=1, source_target_pairs={{0,1},{1,2},{2,3},{3,0},{4,5},{5,6},{6,7},{7,4},{8,9},{9,10},{10,1... | collective-permute-start | bytes 197384 | tf_op jit(solution)/shard_map/ppermute | solution.py:75
  (266 other events, 3145.6 us)

commit v2 on v1

v2 whole, which is shorter than its diff:
```python
import functools
import math

import jax
import jax.numpy as jnp
from jax import lax
from jax.experimental import pallas as pl
from jax.experimental.pallas import tpu as pltpu
from jax.sharding import PartitionSpec as P

HEAD = 64
STEP = 5

RATE_MATRIX = 0.03
RATE_GAIN = 0.25
DECAY_RATE = 0.01
CLIP_NORM = 0.002
NORM_EPS = 1e-05
ADAM_EPS = 1e-08

BF = jnp.bfloat16
F32 = jnp.float32
LOG2E = math.log2(math.e)
NN = (((1,), (0,)), ((), ()))
NT = (((1,), (1,)), ((), ()))
TN = (((0,), (0,)), ((), ()))
VMEM_BYTES = 28 * 1024 * 1024
SMALL_VMEM = 24 * 1024 * 1024


def dot(left, right, dims=NN):
    return lax.dot_general(left, right, dims, preferred_element_type=F32)


def barrier(*values):
    return lax.optimization_barrier(values)


class Place:
    def __init__(self):
        self.dp = lax.axis_size("dp")
        self.nz = lax.axis_size("tensor")
        self.ny = self.dp // 4
        index = lax.axis_index("dp")
        self.z = lax.axis_index("tensor")
        self.c = index % 2
        self.x = (index // 2) % 2
        self.y = index // 4
        self.blocks = [(0, 0), (0, 1)]
        self.blocks += [(k, 1) for k in range(1, self.ny)]
        self.blocks += [(k, 0) for k in range(1, self.ny)]

    def at(self, ky, kx):
        return self.blocks.index((ky, kx))

    def swap_c(self, value):
        return lax.ppermute(value, "dp", [(i, i ^ 1) for i in range(self.dp)])

    def swap_x(self, value):
        return lax.ppermute(value, "dp", [(i, i ^ 2) for i in range(self.dp)])

    def from_y(self, value, k):
        n = self.dp
        return lax.ppermute(value, "dp", [((i + 4 * k) % n, i) for i in range(n)])

    def to_y(self, value, k):
        n = self.dp
        return lax.ppermute(value, "dp", [(i, (i + 4 * k) % n) for i in range(n)])

    def from_z(self, value, k):
        n = self.nz
        return lax.ppermute(value, "tensor", [((i + k) % n, i) for i in range(n)])

    def to_z(self, value, k):
        n = self.nz
        return lax.ppermute(value, "tensor", [(i, (i + k) % n) for i in range(n)])

    def all_z(self, value):
        return lax.all_to_all(value, "tensor", 0, 0)

    def total(self, value):
        value = value + self.swap_c(value)
        n = self.dp
        around = [
            lax.ppermute(value, "dp", [(((i ^ (2 * kx)) + 4 * ky) % n, i) for i in range(n)])
            for ky, kx in self.blocks[1:]
        ]
        value = value + sum(around)
        return value + sum(self.from_z(value, k) for k in range(1, self.nz))

    def in_order(self, mine, other, axis):
        first = jnp.where(self.c == 0, mine, other)
        last = jnp.where(self.c == 0, other, mine)
        return jnp.concatenate([first, last], axis)


class Cell:
    def __init__(self, value):
        self.v = value


def cells(*values):
    return [Cell(v) for v in values]


def fence(*held):
    held = list(dict.fromkeys(held))
    for cell, value in zip(held, barrier(*[c.v for c in held])):
        cell.v = value


class Slots:
    def __init__(self):
        self.flight = []

    def slot(self, stages, *also, wait=True):
        plans = [stage() for stage in stages]
        sends = [s for plan, _ in plans for s in plan]
        fence(*(self.flight if wait else ()), *[c for _, c in sends], *also)
        out = [Cell(send(c.v)) for send, c in sends]
        self.flight = out if wait else self.flight + out
        at = 0
        for plan, take in plans:
            take(out[at : at + len(plan)])
            at += len(plan)


class Gather:
    def __init__(self, place, own, axis, groups=None):
        self.place, self.own, self.axis, self.groups = place, Cell(own), axis, groups
        self.ks = range(1, place.ny)

    def over_z(self, *after):
        place = self.place
        fence(self.own, *after)
        own = self.own.v
        self.parts = Cell(place.all_z(jnp.broadcast_to(own[None], (place.nz,) + own.shape)))

    def near(self):
        place, half = self.place, self.place.nz // 2
        parts, groups = self.parts.v, self.groups or [(0, self.own.v.shape[1])]
        self.both = Cell(
            jnp.stack(
                [
                    jnp.concatenate(
                        [parts[i][:, g0:g1] for g0, g1 in groups for i in range(lo, lo + half)],
                        self.axis,
                    )
                    for lo in (0, half)
                ]
            )
        )

        def take(out):
            self.by_x, self.by_y = out[0], out[1:]

        plan = [(place.swap_x, self.both)]
        return plan + [(functools.partial(place.from_y, k=k), self.both) for k in self.ks], take

    def far(self):
        place = self.place

        def take(out):
            self.far_a, self.far_b = out[: place.ny - 1], out[place.ny - 1 :]

        plan = [(lambda v: place.swap_x(v[0]), v) for v in self.by_y]
        return plan + [(lambda v, k=k: place.from_y(v[1], k), self.by_x) for k in self.ks], take

    def pieces(self):
        out = []
        for half, far in ((0, self.far_a), (1, self.far_b)):
            out.append(
                [self.both.v[half], self.by_x.v[half]]
                + [v.v for v in far]
                + [v.v[half] for v in self.by_y]
            )
        return out

    def arrays(self):
        cells = [self.both, self.by_x, *self.far_a, *self.far_b, *self.by_y]
        return [c.v for c in cells]


class Reduce:
    def __init__(self, place, whole, axis, groups=None):
        self.place, self.whole, self.axis, self.groups = place, whole, axis, groups
        self.ks = range(1, place.ny)

    def near(self):
        place = self.place
        a, b = self.whole

        def take(out):
            self.got_a, self.got_b = out[0], out[1:]

        plan = [(place.swap_x, Cell(a[1 : 1 + place.ny]))]
        for k in self.ks:
            if place.ny == 2:
                sent = b[2:4]
            else:
                sent = jnp.stack([b[place.at(k, 1)], b[place.at(k, 0)]])
            plan.append((functools.partial(place.to_y, k=k), Cell(sent)))
        return plan, take

    def far(self):
        place = self.place
        a, b = self.whole

        def take(out):
            self.far_a, self.far_b = out[:-1], out[-1]

        def along(got, k):
            sent = a[place.at(k, 0)].astype(F32) + got[k].astype(F32)
            return place.to_y(sent.astype(BF), k)

        def across(first):
            sent = b[1].astype(F32) + first[0].astype(F32)
            for other in self.got_b[1:]:
                sent = sent + other.v[0].astype(F32)
            return place.swap_x(sent.astype(BF))

        plan = [(functools.partial(along, k=k), self.got_a) for k in self.ks]
        return plan + [(across, self.got_b[0])], take

    def over_z(self, *after):
        place, half = self.place, self.place.nz // 2
        a, b = self.whole
        own_a = a[0].astype(F32) + self.got_a.v[0].astype(F32) + sum(v.v.astype(F32) for v in self.far_a)
        own_b = (
            b[0].astype(F32) + sum(v.v[1].astype(F32) for v in self.got_b) + self.far_b.v.astype(F32)
        )
        if self.axis == 0:
            chunks = jnp.split(own_a, half, 0) + jnp.split(own_b, half, 0)
        else:
            chunks = []
            for own in (own_a, own_b):
                parts = [jnp.split(own[:, half * g0 : half * g1], half, 1) for g0, g1 in self.groups]
                chunks += [jnp.concatenate(v, 1) for v in zip(*parts)]
        sent = Cell(jnp.stack([v.astype(BF) for v in chunks]))
        fence(sent, *after)
        if self.axis == 0:
            pieces = [
                lax.dynamic_index_in_dim(sent.v, (place.z + k) % place.nz, 0, keepdims=False)
                for k in range(place.nz)
            ]
            moved = [place.to_z(pieces[k], k) for k in range(1, place.nz)]
            self.got = Cell(jnp.stack(pieces[:1] + moved))
        else:
            self.got = Cell(place.all_z(sent.v))

    def result(self):
        return jnp.sum(self.got.v.astype(F32), 0)


def forward_kernel(c_ref, start_ref, qkv_ref, o_ref, lse_ref, k_s, v_s):
    c = c_ref[0]
    half = qkv_ref.shape[1]
    total = 2 * half
    block = min(256, half)
    per_half = half // block
    scale = HEAD ** (-0.5) * LOG2E
    for b in range(2):
        k_s[b * half : (b + 1) * half] = qkv_ref[b ^ c, :, 128:256]
        v_s[b * half : (b + 1) * half] = qkv_ref[b ^ c, :, 256:384]
    lane = lax.broadcasted_iota(jnp.int32, (block, 128), 1)
    for qb in range(total // block):
        rel = (qb // per_half) ^ c
        r0 = (qb % per_half) * block
        n = (qb + 1) * block
        q = qkv_ref[rel, r0 : r0 + block, 0:128]
        row = qb * block + lax.broadcasted_iota(jnp.int32, (block, n), 0)
        col = lax.broadcasted_iota(jnp.int32, (block, n), 1)
        start = start_ref[qb * block : (qb + 1) * block, 0:1]
        allowed = (col >= start) & (col <= row)
        outs = []
        for h in range(2):
            qh = jnp.where((lane >= 64) == (h == 1), q, jnp.zeros_like(q))
            s = dot(qh, k_s[0:n], NT)
            s = jnp.where(allowed, s, -1e30)
            top = jnp.max(s, -1, keepdims=True)
            p = jnp.exp2((s - top) * scale)
            total_p = jnp.sum(p, -1, keepdims=True)
            outs.append(dot(p.astype(BF), v_s[0:n]) / total_p)
            lse = top * scale + jnp.log2(total_p)
            lse_ref[0, qb * block : (qb + 1) * block, h * 64 : (h + 1) * 64] = jnp.broadcast_to(
                lse, (block, 64)
            )
        o_ref[rel, r0 : r0 + block, :] = jnp.where(lane < 64, outs[0], outs[1]).astype(BF)


def backward_kernel(c_ref, start_ref, qkv_ref, o_ref, go_ref, lse_ref, out_ref, k_s, v_s, gk_s, gv_s):
    c = c_ref[0]
    half = qkv_ref.shape[1]
    total = 2 * half
    block = min(256, half)
    per_half = half // block
    scale = HEAD ** (-0.5)
    for b in range(2):
        k_s[b * half : (b + 1) * half] = qkv_ref[b ^ c, :, 128:256]
        v_s[b * half : (b + 1) * half] = qkv_ref[b ^ c, :, 256:384]
    lane = lax.broadcasted_iota(jnp.int32, (block, 128), 1)
    for step, qb in enumerate(reversed(range(total // block))):
        rel = (qb // per_half) ^ c
        r0 = (qb % per_half) * block
        n = (qb + 1) * block
        q = qkv_ref[rel, r0 : r0 + block, 0:128]
        go = go_ref[rel, r0 : r0 + block, :]
        o = o_ref[rel, r0 : r0 + block, :]
        row = qb * block + lax.broadcasted_iota(jnp.int32, (block, n), 0)
        col = lax.broadcasted_iota(jnp.int32, (block, n), 1)
        start = start_ref[qb * block : (qb + 1) * block, 0:1]
        allowed = (col >= start) & (col <= row)
        both = go.astype(F32) * o.astype(F32)
        gq = None
        for h in range(2):
            mine = (lane >= 64) == (h == 1)
            qh = jnp.where(mine, q, jnp.zeros_like(q))
            gh = jnp.where(mine, go, jnp.zeros_like(go))
            s = dot(qh, k_s[0:n], NT)
            lse = lse_ref[0, qb * block : (qb + 1) * block, h * 64 : h * 64 + 1]
            p = jnp.where(allowed, jnp.exp2(jnp.minimum(s * (scale * LOG2E) - lse, 1.0)), 0.0)
            gp = dot(gh, v_s[0:n], NT)
            inner = jnp.sum(jnp.where(mine, both, 0.0), -1, keepdims=True)
            gs = (p * (gp - inner)).astype(BF)
            pb = p.astype(BF)
            gqh = dot(gs, k_s[0:n])
            gq = gqh if gq is None else jnp.where(lane < 64, gq, gqh)
            gk = dot(gs, qh, TN)
            gv = dot(pb, gh, TN)
            if step == 0 and h == 0:
                gk_s[0:n] = gk
                gv_s[0:n] = gv
            else:
                gk_s[0:n] += gk
                gv_s[0:n] += gv
        out_ref[rel, r0 : r0 + block, 0:128] = (gq * scale).astype(BF)
    for b in range(2):
        out_ref[b ^ c, :, 128:256] = (gk_s[b * half : (b + 1) * half] * scale).astype(BF)
        out_ref[b ^ c, :, 256:384] = gv_s[b * half : (b + 1) * half].astype(BF)


def attention(c_index, starts, qkv):
    rows, cols = qkv.shape
    half, pairs = rows // 2, cols // 384
    smem = pl.BlockSpec(memory_space=pltpu.SMEM)
    out, lse = pl.pallas_call(
        forward_kernel,
        grid=(pairs,),
        in_specs=[
            smem,
            pl.BlockSpec((rows, 1), lambda j: (0, 0)),
            pl.BlockSpec((2, half, 384), lambda j: (0, 0, j)),
        ],
        out_specs=[
            pl.BlockSpec((2, half, 128), lambda j: (0, 0, j)),
            pl.BlockSpec((1, rows, 128), lambda j: (j, 0, 0)),
        ],
        out_shape=[
            jax.ShapeDtypeStruct((2, half, pairs * 128), BF),
            jax.ShapeDtypeStruct((pairs, rows, 128), F32),
        ],
        scratch_shapes=[pltpu.VMEM((rows, 128), BF), pltpu.VMEM((rows, 128), BF)],
        compiler_params=pltpu.CompilerParams(vmem_limit_bytes=VMEM_BYTES),
        cost_estimate=pl.CostEstimate(
            flops=1, bytes_accessed=1, transcendentals=0
        ),
        name="attend",
    )(c_index, starts, qkv.reshape(2, half, cols))
    return out.reshape(rows, pairs * 128), lse


def attention_back(c_index, starts, qkv, out, grad, lse):
    rows, cols = qkv.shape
    half, pairs = rows // 2, cols // 384
    smem = pl.BlockSpec(memory_space=pltpu.SMEM)
    wide = pl.BlockSpec((2, half, 384), lambda j: (0, 0, j))
    thin = pl.BlockSpec((2, half, 128), lambda j: (0, 0, j))
    result = pl.pallas_call(
        backward_kernel,
        grid=(pairs,),
        in_specs=[
            smem,
            pl.BlockSpec((rows, 1), lambda j: (0, 0)),
            wide,
            thin,
            thin,
            pl.BlockSpec((1, rows, 128), lambda j: (j, 0, 0)),
        ],
        out_specs=wide,
        out_shape=jax.ShapeDtypeStruct((2, half, cols), BF),
        scratch_shapes=[
            pltpu.VMEM((rows, 128), BF),
            pltpu.VMEM((rows, 128), BF),
            pltpu.VMEM((rows, 128), F32),
            pltpu.VMEM((rows, 128), F32),
        ],
        compiler_params=pltpu.CompilerParams(vmem_limit_bytes=VMEM_BYTES),
        cost_estimate=pl.CostEstimate(
            flops=1, bytes_accessed=1, transcendentals=0
        ),
        name="attend_back",
    )(
        c_index,
        starts,
        qkv.reshape(2, half, cols),
        out.reshape(2, half, pairs * 128),
        grad.reshape(2, half, pairs * 128),
        lse,
    )
    return result.reshape(rows, cols)


def cheap():
    return pl.CostEstimate(flops=1, bytes_accessed=1, transcendentals=0)


def call(kernel, args, shapes, scratch=(), name=None):
    vmem = pl.BlockSpec(memory_space=pltpu.VMEM)
    return pl.pallas_call(
        kernel,
        in_specs=[vmem] * len(args),
        out_specs=[vmem] * len(shapes),
        out_shape=shapes,
        scratch_shapes=list(scratch),
        compiler_params=pltpu.CompilerParams(vmem_limit_bytes=SMALL_VMEM),
        cost_estimate=cheap(),
        name=name,
    )(*args)


def piece_at(refs, blocks, half, i):
    far = (blocks - 2) // 2
    if i < 2:
        return refs[i].at[half]
    if i < 2 + far:
        return refs[i + half * far]
    return refs[i + far].at[half]


def gelu_parts(value):
    phi = 0.5 * (1.0 + lax.erf(value * (0.5**0.5)))
    slope = phi + value * (jnp.exp(-0.5 * value * value) * (1.0 / math.sqrt(2.0 * math.pi)))
    return value * phi, slope


def across_kernel(blocks, count, lo, hi, kind, *refs):
    mine_ref, theirs_ref = refs[:2]
    weights = refs[2 : 2 + count]
    refs = refs[2 + count :]
    slopes = ()
    if kind == "slope":
        slopes, refs = refs[:2], refs[2:]
    joined_ref, refs = refs[0], refs[1:]
    outs, w_s = refs[:-1], refs[-1]
    rows = mine_ref.shape[0]
    tile = min(512, rows)
    size = w_s.shape[1] // blocks
    for half in range(2):
        for i in range(blocks):
            w_s[half, i * size : (i + 1) * size] = piece_at(weights, blocks, half, i)[:, lo:hi]
    for base, source in ((0, mine_ref), (rows, theirs_ref)):

        @pl.loop(0, rows // tile)
        def _(step):
            r = pl.multiple_of(step * tile, tile)
            at = pl.ds(pl.multiple_of(base + step * tile, tile), tile)
            left = source[pl.ds(r, tile), :]
            joined_ref[at, :] = left
            for half in range(2):
                value = dot(left, w_s[half])
                if kind == "gelu":
                    value, slope = gelu_parts(value)
                    outs[2 + half][at, :] = slope.astype(BF)
                elif kind == "slope":
                    value = value * slopes[half][at, :].astype(F32)
                outs[half][at, :] = value.astype(BF)


def across(mine, theirs, gather, span, kind="plain", slopes=()):
    arrays = gather.arrays()
    blocks = len(gather.place.blocks)
    lo, hi = span
    rows, width = mine.shape
    units = hi - lo
    count = 4 if kind == "gelu" else 2
    out = call(
        functools.partial(across_kernel, blocks, len(arrays), lo, hi, kind),
        [mine, theirs, *arrays, *slopes],
        [jax.ShapeDtypeStruct((2 * rows, width), BF)]
        + [jax.ShapeDtypeStruct((2 * rows, units), BF)] * count,
        [pltpu.VMEM((2, width, units), BF)],
        "across_" + kind,
    )
    return out[0], list(out[1:3]), list(out[3:])


def grads_kernel(blocks, sizes, *refs):
    pairs = len(sizes)
    inputs, outs = refs[: 3 * pairs], refs[3 * pairs :]
    cut = inputs[0].shape[1] // blocks
    at = 0
    for p, size in enumerate(sizes):
        left_ref, rights = inputs[3 * p], inputs[3 * p + 1 : 3 * p + 3]
        for i in range(blocks):
            left = left_ref[:, i * cut : (i + 1) * cut]
            for half in range(2):
                value = dot(left, rights[half][...], TN)
                outs[half][i, :, at : at + size] = value.astype(BF)
        at += size


def weight_grads(place, *pairs):
    blocks = len(place.blocks)
    sizes = [rights[0].shape[1] for _, rights in pairs]
    width = pairs[0][0].shape[1]
    args = [v for left, rights in pairs for v in (left, *rights)]
    shape = jax.ShapeDtypeStruct((blocks, width // blocks, sum(sizes)), BF)
    return call(
        functools.partial(grads_kernel, blocks, sizes), args, [shape, shape], (), "grads"
    )


def back_kernel(blocks, count, lo, hi, row0, *refs):
    lefts, weights, out_ref = refs[:2], refs[2 : 2 + count], refs[2 + count]
    rows, width = out_ref.shape
    tile = min(512, rows)
    size = width // blocks

    @pl.loop(0, rows // tile)
    def _(step):
        r = pl.multiple_of(step * tile, tile)
        at = pl.ds(pl.multiple_of(row0 + step * tile, tile), tile)
        left_a, left_b = lefts[0][at, :], lefts[1][at, :]
        for i in range(blocks):
            value = dot(left_a, piece_at(weights, blocks, 0, i)[:, lo:hi], NT)
            value = value + dot(left_b, piece_at(weights, blocks, 1, i)[:, lo:hi], NT)
            out_ref[pl.ds(r, tile), i * size : (i + 1) * size] = value.astype(out_ref.dtype)


def back(lefts, gather, span, row0, rows, dtype):
    arrays = gather.arrays()
    blocks = len(gather.place.blocks)
    width = blocks * arrays[0].shape[1]
    return call(
        functools.partial(back_kernel, blocks, len(arrays), *span, row0),
        [*lefts, *arrays],
        [jax.ShapeDtypeStruct((rows, width), dtype)],
        (),
        "back",
    )[0]


def lookup_kernel(blocks, count, *refs):
    codes_refs, weights, outs = refs[:2], refs[2 : 2 + count], refs[2 + count : -1]
    w_s = refs[-1]
    rows, cols = codes_refs[0].shape[0], weights[0].shape[-1]
    size = weights[0].shape[1]
    for i in range(blocks):
        for h in range(2):
            w_s[(2 * i + h) * size : (2 * i + h + 1) * size] = piece_at(weights, blocks, h, i)[...]
    for codes_ref, out_ref in zip(codes_refs, outs):
        hot = lax.broadcasted_iota(jnp.int32, (rows, cols), 1) == codes_ref[...]
        hot = jnp.where(hot, 1.0, 0.0).astype(BF)
        out_ref[...] = dot(hot, w_s[...], NT).astype(BF)


def lookup(mine, theirs, gather):
    arrays = gather.arrays()
    blocks = len(gather.place.blocks)
    features = blocks * 2 * arrays[0].shape[1]
    shape = jax.ShapeDtypeStruct((mine.shape[0], features), BF)
    return call(
        functools.partial(lookup_kernel, blocks, len(arrays)),
        [mine, theirs, *arrays],
        [shape, shape],
        [pltpu.VMEM((features, arrays[0].shape[2]), BF)],
        "lookup",
    )


def start_kernel(blocks, factor, c_ref, mine_ref, got_ref, coded_ref, x_ref, y_ref, gains_ref):
    even = c_ref[0] == 0
    rows, width = x_ref.shape
    tile = min(64, rows)
    size = width // (2 * blocks)

    def both(at):
        mine, got = mine_ref[at, :].astype(F32), got_ref[at, :].astype(F32)
        out = []
        for i in range(blocks):
            a, b = mine[:, i * size : (i + 1) * size], got[:, i * size : (i + 1) * size]
            out += [jnp.where(even, a, b), jnp.where(even, b, a)]
        return jnp.concatenate(out, 1)

    gains_ref[...] = both(slice(rows, mine_ref.shape[0]))

    @pl.loop(0, rows // tile)
    def _(step):
        at = pl.ds(pl.multiple_of(step * tile, tile), tile)
        x = both(at) * factor + coded_ref[at, :]
        x_ref[at, :] = x
        y_ref[at, :] = (row_stats(x)[0] * gains_ref[0:1, :]).astype(BF)


def start_norm(blocks, c_index, mine, got, coded):
    rows, width = coded.shape
    vmem, smem = pl.BlockSpec(memory_space=pltpu.VMEM), pl.BlockSpec(memory_space=pltpu.SMEM)
    return pl.pallas_call(
        functools.partial(start_kernel, blocks, math.sqrt(width)),
        in_specs=[smem, vmem, vmem, vmem],
        out_specs=[vmem] * 3,
        out_shape=[
            jax.ShapeDtypeStruct((rows, width), F32),
            jax.ShapeDtypeStruct((rows, width), BF),
            jax.ShapeDtypeStruct((mine.shape[0] - rows, width), F32),
        ],
        compiler_params=pltpu.CompilerParams(vmem_limit_bytes=SMALL_VMEM),
        cost_estimate=cheap(),
        name="start",
    )(c_index, mine, got, coded)


def row_stats(x):
    centered = x - jnp.mean(x, -1, keepdims=True)
    inverse = lax.rsqrt(jnp.mean(centered * centered, -1, keepdims=True) + NORM_EPS)
    return centered * inverse, inverse


def norm_kernel(terms, *refs):
    parts, gain_ref, x_ref, y_ref = refs[:terms], refs[terms], refs[terms + 1], refs[terms + 2]
    rows = x_ref.shape[0]
    tile = min(64, rows)

    @pl.loop(0, rows // tile)
    def _(step):
        at = pl.ds(pl.multiple_of(step * tile, tile), tile)
        x = parts[0][at, :].astype(F32)
        for part in parts[1:]:
            x = x + part[at, :].astype(F32)
        x_ref[at, :] = x
        y_ref[at, :] = (row_stats(x)[0] * gain_ref[...]).astype(BF)


def norm(parts, gain):
    shape = parts[0].shape
    return call(
        functools.partial(norm_kernel, len(parts)),
        [*parts, gain],
        [jax.ShapeDtypeStruct(shape, F32), jax.ShapeDtypeStruct(shape, BF)],
        (),
        "norm",
    )


def norm_back_kernel(terms, extra, *refs):
    parts, refs = refs[:terms], refs[terms:]
    others, refs = refs[:extra], refs[extra:]
    x_ref, gain_ref, out_ref, low_ref, sum_ref = refs
    rows = x_ref.shape[0]
    tile = min(64, rows)
    sum_ref[...] = jnp.zeros_like(sum_ref)

    @pl.loop(0, rows // tile)
    def _(step):
        at = pl.ds(pl.multiple_of(step * tile, tile), tile)
        grad = parts[0][at, :].astype(F32)
        for part in parts[1:]:
            grad = grad + part[at, :].astype(F32)
        normed, inverse = row_stats(x_ref[at, :])
        scaled = grad * gain_ref[...]
        value = inverse * (
            scaled
            - jnp.mean(scaled, -1, keepdims=True)
            - normed * jnp.mean(scaled * normed, -1, keepdims=True)
        )
        for other in others:
            value = value + other[at, :]
        out_ref[at, :] = value
        low_ref[at, :] = value.astype(BF)
        sum_ref[...] += jnp.sum(grad * normed, 0, keepdims=True)


def norm_back(parts, others, x, gain):
    shape = x.shape
    return call(
        functools.partial(norm_back_kernel, len(parts), len(others)),
        [*parts, *others, x, gain],
        [
            jax.ShapeDtypeStruct(shape, F32),
            jax.ShapeDtypeStruct(shape, BF),
            jax.ShapeDtypeStruct((1, shape[1]), F32),
        ],
        (),
        "norm_back",
    )


def doc_layout(lengths_row, total_rows):
    places = jnp.arange(total_rows, dtype=jnp.int32)
    bound_one = lengths_row[0]
    bound_two = lengths_row[0] + lengths_row[1]
    doc_ids = (places >= bound_one).astype(jnp.int32) + (places >= bound_two).astype(jnp.int32)
    starts = jnp.where(doc_ids == 0, 0, jnp.where(doc_ids == 1, bound_one, bound_two))
    return (doc_ids, starts, places - starts)


def next_codes(codes_row, doc_ids, end_code):
    later = jnp.concatenate([codes_row[1:], jnp.full((1,), end_code, jnp.int32)])
    later_doc = jnp.concatenate([doc_ids[1:], jnp.full((1,), -1, jnp.int32)])
    return jnp.where(later_doc == doc_ids, later, end_code)


def head_loss(logits, targets, weights_row):
    top_score = jnp.max(logits, -1, keepdims=True)
    expo = jnp.exp(logits - top_score)
    totals = jnp.sum(expo, -1, keepdims=True)
    target_hit = jnp.arange(logits.shape[1], dtype=jnp.int32)[None, :] == targets[:, None]
    picked = jnp.sum(jnp.where(target_hit, logits, 0.0), -1)
    loss_value = jnp.sum(weights_row * (top_score[:, 0] + jnp.log(totals[:, 0]) - picked))
    grad_logits = ((expo / totals - target_hit.astype(F32)) * weights_row[:, None]).astype(BF)
    return (loss_value, grad_logits)


def adam_kernel(scale_ref, c_ref, *refs):
    correct = 1.0 - 0.5**STEP
    sources, refs = [refs[3 * i : 3 * i + 3] for i in range(6)], refs[18:]
    attn_k, attn_g, up_k, up_g, down_k, down_g, embed_ref, head_ref, gain_ref = refs[:9]
    refs = refs[9:]
    outs = [refs[4 * i : 4 + 4 * i] for i in range(6)]
    bufs = [refs[24 + 4 * i : 28 + 4 * i] for i in range(6)]
    states = [refs[48 + 3 * i : 51 + 3 * i] for i in range(6)]
    sems, in_sems = refs[66:68]
    order = (0, 2, 3, 4, 1, 5)

    def fetches(i):
        return [
            pltpu.make_async_copy(source, state, in_sems.at[i, k])
            for k, (source, state) in enumerate(zip(sources[i], states[i]))
        ]

    for i in order:
        for copy in fetches(i):
            copy.start()

    def arrive(i):
        for copy in fetches(i):
            copy.wait()

    scale = scale_ref[0]
    even = c_ref[0] == 0

    def pair(keep, got):
        return jnp.where(even, keep, got) * scale, jnp.where(even, got, keep) * scale

    def step(i, at, grad):
        master_ref, first_ref, second_ref = states[i]
        rate = RATE_GAIN if i == 5 else RATE_MATRIX
        decay = 0.0 if i == 5 else DECAY_RATE
        master = master_ref[at]
        first_new = 0.5 * first_ref[at] + 0.5 * grad
        second_new = 0.5 * second_ref[at] + 0.5 * grad * grad
        master_new = master - rate * (
            first_new / correct / (jnp.sqrt(second_new / correct) + ADAM_EPS) + decay * master
        )
        for buf, value in zip(bufs[i], (master_new, first_new, second_new, master_new.astype(BF))):
            buf[at] = value

    def copies(i):
        return [
            pltpu.make_async_copy(buf, out, sems.at[i, k])
            for k, (buf, out) in enumerate(zip(bufs[i], outs[i]))
        ]

    def send(i):
        for copy in copies(i):
            copy.start()

    every = slice(None)
    arrive(0)
    lanes = states[0][0].shape[2] // 2
    for j in range(3):
        cut = slice(j * lanes, (j + 1) * lanes)
        for k, grad in enumerate(pair(attn_k[:, cut], attn_g[:, cut])):
            step(0, (j, every, slice(k * lanes, (k + 1) * lanes)), grad)
    send(0)
    arrive(2)
    size = states[2][0].shape[1] // 2
    for k, grad in enumerate(pair(up_k[...], up_g[...])):
        step(2, (every, slice(k * size, (k + 1) * size)), grad)
    send(2)
    arrive(3)
    size = states[3][0].shape[0] // 2
    for k, grad in enumerate(pair(down_k[...], down_g[...])):
        step(3, (slice(k * size, (k + 1) * size), every), grad.T)
    send(3)
    arrive(4)
    vocab = states[4][0].shape[2]
    step(4, (0, every, every), embed_ref[:, 0:vocab] * scale)
    step(4, (1, every, every), head_ref[:, 0:vocab] * scale)
    send(4)
    arrive(1)
    size = states[1][0].shape[0] // 2
    cut = slice(3 * lanes, attn_k.shape[1])
    for k, grad in enumerate(pair(attn_k[:, cut], attn_g[:, cut])):
        step(1, (slice(k * size, (k + 1) * size), every), grad.T)
    send(1)
    arrive(5)
    step(5, (every, every), gain_ref[...] * scale)
    send(5)
    for i in range(6):
        for copy in copies(i):
            copy.wait()


def adam(scale, c_index, states, grads):
    shapes = []
    for group in states:
        shapes += [jax.ShapeDtypeStruct(group[0].shape, t) for t in (F32, F32, F32, BF)]
    args = [v for group in states for v in group] + list(grads)
    vmem, smem = pl.BlockSpec(memory_space=pltpu.VMEM), pl.BlockSpec(memory_space=pltpu.SMEM)
    hbm = pl.BlockSpec(memory_space=pl.ANY)
    return pl.pallas_call(
        adam_kernel,
        in_specs=[smem, smem] + [hbm] * 18 + [vmem] * len(grads),
        out_specs=[hbm] * len(shapes),
        out_shape=shapes,
        scratch_shapes=[pltpu.VMEM(s.shape, s.dtype) for s in shapes]
        + [pltpu.VMEM(v.shape, v.dtype) for v in args[:18]]
        + [pltpu.SemaphoreType.DMA((6, 4)), pltpu.SemaphoreType.DMA((6, 3))],
        compiler_params=pltpu.CompilerParams(vmem_limit_bytes=2 * VMEM_BYTES),
        cost_estimate=cheap(),
        name="adam",
    )(scale, c_index, *args)


def body(
    codes,
    doc_lengths,
    loss_mask,
    qkv_master,
    qkv_first,
    qkv_second,
    out_master,
    out_first,
    out_second,
    up_master,
    up_first,
    up_second,
    down_master,
    down_first,
    down_second,
    table_master,
    table_first,
    table_second,
    gain_master,
    gain_first,
    gain_second,
):
    place = Place()
    nz, ny, nb = place.nz, place.ny, len(place.blocks)
    c, z = place.c, place.z
    feat = qkv_master.shape[0]
    width = feat * place.dp
    total_rows = codes.shape[1]
    half_rows = total_rows // 2
    vocab = table_master.shape[1]
    thin = table_master.shape[2]

    joined = jnp.concatenate([codes, loss_mask, doc_lengths], 1)
    other = place.swap_c(joined)
    four = place.in_order(joined, other, 0)
    row = lax.dynamic_index_in_dim(four, z, 0, keepdims=False)
    codes_row = row[:total_rows]
    mask_row = row[total_rows : 2 * total_rows]
    lengths_row = row[2 * total_rows :]
    doc_ids, starts, local_pos = doc_layout(lengths_row, total_rows)
    targets = next_codes(codes_row, doc_ids, vocab - 1)
    first_row = c * half_rows
    my_codes = lax.dynamic_slice_in_dim(codes_row, first_row, half_rows, 0)
    my_local = lax.dynamic_slice_in_dim(local_pos, first_row, half_rows, 0)
    my_targets = lax.dynamic_slice_in_dim(targets, first_row, half_rows, 0)
    my_mask = lax.dynamic_slice_in_dim(mask_row, first_row, half_rows, 0).astype(F32)
    c_index = jnp.reshape(c, (1,)).astype(jnp.int32)
    starts_col = starts.reshape(total_rows, 1)

    def halves(matrix, axis):
        size = matrix.shape[axis] // 2
        keep = lax.dynamic_slice_in_dim(matrix, c * size, size, axis)
        send = lax.dynamic_slice_in_dim(matrix, (1 - c) * size, size, axis)
        return keep, send

    cols = -(-(vocab + 3) // 128) * 128
    table_t = jnp.swapaxes(table_master.astype(BF), 1, 2)
    embed_p = jnp.concatenate(
        [table_t[0], gain_master.astype(BF).T, jnp.zeros((thin, cols - vocab - 3), BF)], 1
    )
    head_p = jnp.concatenate([table_t[1], jnp.zeros((thin, cols - vocab), BF)], 1)
    slots = Slots()
    g_embed, g_head = Gather(place, embed_p, 0), Gather(place, head_p, 0)

    qkv_b, out_b, up_b, down_b = (
        v.astype(BF) for v in (qkv_master, out_master, up_master, down_master)
    )
    qkv_k, qkv_s = (v.reshape(feat, -1) for v in halves(qkv_b, 2))
    out_k, out_s = (v.T for v in halves(out_b, 0))
    up_k, up_s = halves(up_b, 1)
    down_k, down_s = (v.T for v in halves(down_b, 0))
    units = [v.shape[1] for v in (qkv_k, out_k, up_k, down_k)]
    keep = jnp.concatenate([qkv_k, out_k, up_k, down_k], 1)
    send = jnp.concatenate([qkv_s, out_s, up_s, down_s], 1)
    recv = place.swap_c(send)
    chip = place.in_order(keep, recv, 0)
    edges = [sum(units[:i]) for i in range(5)]
    g_attn = Gather(place, chip[:, : edges[2]], 1, [(0, units[0]), (units[0], edges[2])])
    g_up = Gather(place, chip[:, edges[2] : edges[3]], 1)
    g_down = Gather(place, chip[:, edges[3] :], 1)

    block = jnp.asarray([k for k, _ in place.blocks], jnp.int32)
    block_x = jnp.asarray([k for _, k in place.blocks], jnp.int32)
    chip_at = ((place.y + block) % ny) * 2 + (place.x ^ block_x)
    feature = (
        chip_at[:, None] * (2 * feat) + jnp.arange(2 * feat, dtype=jnp.int32)[None, :]
    ).reshape(width)
    freqs = jnp.exp((feature // 2).astype(F32) * (-2.0 * math.log(10000.0) / width))
    angles = my_local.astype(F32)[:, None] * freqs[None, :]
    coded = Cell(jnp.where((feature % 2 == 0)[None, :], jnp.sin(angles), jnp.cos(angles)))

    def branch(lefts, gather, span):
        theirs = back(lefts, gather, span, half_rows, half_rows, BF)
        got = place.swap_c(theirs)
        return back(lefts, gather, span, 0, half_rows, F32), got

    def table(gather):
        a, b = (jnp.stack(v) for v in gather.pieces())
        mine = jnp.concatenate([a, b], 1).reshape(nb, 1, nz * thin, cols)
        return place.in_order(mine, place.swap_c(mine), 1).reshape(width, cols)

    def code_rows(half):
        own = lax.dynamic_slice_in_dim(codes_row, half * half_rows, half_rows, 0)
        gain_codes = vocab + jnp.arange(16, dtype=jnp.int32)
        return jnp.concatenate([own, jnp.where(gain_codes < vocab + 3, gain_codes, -1)])[:, None]

    codes_c = cells(code_rows(c), code_rows(1 - c))
    g_attn.over_z()
    slots.slot([g_attn.near], coded, g_embed.own, *codes_c)
    g_embed.over_z()
    g_up.over_z(g_embed.parts)
    early = Slots()
    early.slot([g_embed.near])
    early.slot([g_embed.far])
    slots.slot([g_up.near, g_attn.far], *early.flight)
    g_head.over_z(g_up.parts)
    g_down.over_z(g_head.parts)
    found, found_other = lookup(codes_c[0].v, codes_c[1].v, g_embed)
    start, attn_m, gains = start_norm(nb, c_index, found, place.swap_c(found_other), coded.v)
    gains = [gains[i : i + 1] for i in range(3)]
    one_hot = (my_codes[:, None] == jnp.arange(cols, dtype=jnp.int32)[None, :]).astype(BF)
    attn_c, other_c = cells(attn_m, place.swap_c(attn_m))

    slots.slot([g_down.near, g_up.far], attn_c, other_c)
    span_qkv = (0, nz // 2 * units[0])
    span_out = (span_qkv[1], nz // 2 * edges[2])
    span_up, span_down = (0, nz // 2 * units[2]), (0, nz // 2 * units[3])
    attn_in, qkv, _ = across(attn_c.v, other_c.v, g_attn, span_qkv)
    mixed, lse = zip(*(attention(c_index, starts_col, v) for v in qkv))
    theirs_c = Cell(back(mixed, g_attn, span_out, half_rows, half_rows, BF))
    mine_c = Cell(back(mixed, g_attn, span_out, 0, half_rows, F32))

    slots.slot([g_head.near, g_down.far], theirs_c, mine_c)
    middle, ffn_m = norm([start, mine_c.v, place.swap_c(theirs_c.v)], gains[1])
    ffn_in, hidden, slope = across(ffn_m, place.swap_c(ffn_m), g_up, span_up, "gelu")
    hidden_c = cells(*hidden)
    slots.slot([g_head.far], *hidden_c)
    hidden = [v.v for v in hidden_c]
    final, features = norm([middle, *branch(hidden, g_down, span_down)], gains[2])
    a, b = (jnp.stack(v) for v in g_head.pieces())
    mine = jnp.concatenate([a, b], 1).reshape(nb, 1, nz * thin, cols)
    head_t = place.in_order(mine, place.swap_c(mine), 1).reshape(width, cols)
    logits = dot(features, head_t)
    logits = jnp.where(jnp.arange(cols)[None, :] < vocab, logits, -1e30)
    loss_local, grad_logits = head_loss(logits, my_targets, my_mask)

    slots = Slots()
    cut = 2 * feat

    def matrix_sum(*pairs):
        whole = weight_grads(place, *pairs)
        groups, start_at = [], 0
        for _, rights in pairs:
            size = rights[0].shape[1] // (nz // 2)
            groups.append((start_at, start_at + size))
            start_at += size
        return Reduce(place, whole, 1, groups)

    def table_sum(left, right, extra=None):
        def by_c(values):
            size = nz * thin
            even, odd = (
                jnp.concatenate([values[..., (2 * i + k) * size : (2 * i + k + 1) * size] for i in range(nb)], -1)
                for k in (0, 1)
            )
            return jnp.where(c == 0, even, odd), jnp.where(c == 0, odd, even)

        left_k, left_s = by_c(left)
        own = dot(left_k, right, TN)
        sent = dot(left_s, right, TN)
        if extra is not None:
            extra_k, extra_s = (
                jnp.pad(v.T, ((0, 0), (vocab, cols - vocab - extra.shape[0]))) for v in by_c(extra)
            )
            own, sent = own + extra_k, sent + extra_s
        got = place.swap_c(sent.astype(BF))
        chip_sum = (own + got.astype(F32)).astype(BF).reshape(nb, 2, nz // 2 * thin, cols)
        return Reduce(place, [chip_sum[:, 0], chip_sum[:, 1]], 0)

    r_head = table_sum(features, grad_logits)
    grad_feat = dot(grad_logits, head_t, NT)
    grad_final, grad_down, gain_three = norm_back([grad_feat], [], final, gains[2])
    grad_down_c, other_c = cells(grad_down, place.swap_c(grad_down))
    slots.slot([r_head.near], grad_down_c, other_c)
    grad_down, other = grad_down_c.v, other_c.v
    r_down = matrix_sum((jnp.concatenate([grad_down, other], 0), hidden))

    grad_down_c, other_c = cells(grad_down, other)
    slots.slot([r_down.near, r_head.far], grad_down_c, other_c)
    _, grad_up, _ = across(grad_down_c.v, other_c.v, g_down, span_down, "slope", slope)
    theirs_c = Cell(back(grad_up, g_up, span_up, half_rows, half_rows, BF))
    mine_c = Cell(back(grad_up, g_up, span_up, 0, half_rows, F32))
    r_up = matrix_sum((ffn_in, grad_up))

    slots.slot([r_up.near, r_down.far], theirs_c, mine_c)
    grad_mid, grad_out, gain_two = norm_back(
        [mine_c.v, place.swap_c(theirs_c.v)], [grad_final], middle, gains[1]
    )
    grad_out, grad_mixed, _ = across(grad_out, place.swap_c(grad_out), g_attn, span_out)
    grad_qkv = [
        attention_back(c_index, starts_col, q, o, g, ls)
        for q, o, g, ls in zip(qkv, mixed, grad_mixed, lse)
    ]
    r_attn = matrix_sum((attn_in, grad_qkv), (grad_out, mixed))
    theirs_c = Cell(back(grad_qkv, g_attn, span_qkv, half_rows, half_rows, BF))
    mine_c = Cell(back(grad_qkv, g_attn, span_qkv, 0, half_rows, F32))

    slots.slot([r_attn.near, r_up.far], theirs_c, mine_c)
    r_down.over_z()
    grad_start, _, gain_one = norm_back(
        [mine_c.v, place.swap_c(theirs_c.v)], [grad_mid], start, gains[0]
    )
    gain_grad = jnp.concatenate([gain_one, gain_two, gain_three], 0)
    r_embed = table_sum((grad_start * math.sqrt(width)).astype(BF), one_hot, gain_grad)

    slots.slot([r_attn.far, r_embed.near])
    r_up.over_z(r_down.got)
    slots.slot([r_embed.far])
    r_head.over_z(slots.flight[0])
    r_attn.over_z(r_up.got)
    r_embed.over_z(r_up.got)

    def shards(total):
        keep_g, send_g = halves(total, 0)
        return keep_g, place.swap_c(send_g)

    head_sum, down_sum, up_sum = r_head.result(), r_down.result(), r_up.result()
    down_k, down_g = shards(down_sum)
    up_k, up_g = shards(up_sum)
    attn_sum = r_attn.result()
    attn_k, attn_g = shards(attn_sum)
    embed_sum = r_embed.result()
    squares = sum(
        jnp.sum(v * v) for v in (head_sum, down_sum, up_sum, attn_sum, embed_sum)
    )
    stats = jnp.stack([loss_local, jnp.sum(my_mask), squares])
    stats = place.total(stats)
    loss_all, count_all = stats[0], stats[1]
    norm_all = jnp.sqrt(stats[2] / (count_all * count_all))
    factor = jnp.minimum(1.0, CLIP_NORM / (norm_all + 1e-06))
    scale = jnp.reshape(factor / count_all, (1,))
    states = (
        [jnp.swapaxes(v, 0, 1) for v in (qkv_master, qkv_first, qkv_second)],
        (out_master, out_first, out_second),
        (up_master, up_first, up_second),
        (down_master, down_first, down_second),
        [jnp.swapaxes(v, 1, 2) for v in (table_master, table_first, table_second)],
        (gain_master, gain_first, gain_second),
    )
    gain_sum = embed_sum[:, vocab : vocab + 3].T
    grads = (attn_k, attn_g, up_k, up_g, down_k, down_g, embed_sum, head_sum, gain_sum)
    new = list(adam(scale, c_index, states, grads))
    new[0:4] = [jnp.swapaxes(v, 0, 1) for v in new[0:4]]
    new[16:20] = [jnp.swapaxes(v, 1, 2) for v in new[16:20]]
    return tuple(new) + (loss_all, count_all, norm_all)


def solution(mesh):
    rows, cols = P("dp", None, "tensor"), P("tensor", "dp")
    plain, both, gain = P("dp", "tensor"), P(None, None, ("dp", "tensor")), P(None, ("dp", "tensor"))
    kinds = (rows, cols, plain, cols, both, gain)
    in_specs = (P("dp", None),) * 3 + tuple(k for k in kinds for _ in range(3))
    out_specs = tuple(k for k in kinds for _ in range(4)) + (P(),) * 3
    return jax.shard_map(body, mesh=mesh, in_specs=in_specs, out_specs=out_specs, check_vma=False)
```

time: 776 us -> 491 us (0.63)
  local copies, waits for them, and re-layouts: 182 us -> 49.2 us
  matrix products: 125 us -> 10.1 us
  Pallas kernels: 36.3 us -> 123 us
  waiting for transfers between devices: 210 us -> 130 us
  starting transfers between devices: 127 us -> 94.1 us
  other arithmetic: 71.1 us -> 55.4 us
  blocking collectives: 0 us -> 11.5 us
    dot_general x53 -> x6, matrix products: 125 us -> 10.1 us  [dot(): return lax.dot_general(left, right, dims, preferred_element_type=F32)]
    pallas_call x0 -> x23, Pallas kernels: none -> 86.6 us  [the longest x21 77.7 us: call(): pl.pallas_call(kernel, in_specs=[vmem] * len(args), out_specs=[vmem] * le...]
    ppermute x18 -> x6, waiting for transfers between devices: 67.2 us -> 17.6 us  [to_z(): return lax.ppermute(value, 'tensor', [(i, (i + k) % n) for i in range(n)])]
    ppermute x24 -> x3, waiting for transfers between devices: 49.9 us -> 4.95 us  [from_z(): return lax.ppermute(value, 'tensor', [((i + k) % n, i) for i in range(n)])]
    ppermute x24 -> x3, starting transfers between devices: 45.1 us -> 4.16 us  [from_z(): return lax.ppermute(value, 'tensor', [((i + k) % n, i) for i in range(n)])]
    all_to_all x0 -> x7, waiting for transfers between devices: none -> 38.7 us  [all_z(): return lax.all_to_all(value, 'tensor', 0, 0)]
    concatenate x5 -> x6, local copies, waits for them, and re-layouts: 34.7 us -> 0.23 us  [the longest x4 0.12 us: over_z(): chunks += [jnp.concatenate(v, 1) for v in zip(*parts)]]
    all_to_all x0 -> x7, starting transfers between devices: none -> 32.7 us  [all_z(): return lax.all_to_all(value, 'tensor', 0, 0)]
  transfers between devices with their start and end apart: 111 -> 77, of which waited for: 40 -> 33; matrix products, arithmetic and copies ran while one was open for 37% -> 19% of each run, Pallas kernels for 1% -> 24%
where the time goes in v2:
time: 491 us; the launch traced here: 485 us
  waiting for transfers between devices  130 us (26%)
  Pallas kernels  123 us (25%)
  starting transfers between devices  94.1 us (19%)
  other arithmetic  55.4 us (11%)
  local copies, waits for them, and re-layouts  49.2 us (10%)
  blocking collectives  11.5 us (2%)
  between operations  11.3 us (2%)
  matrix products  10.1 us (2%)
    pallas_call x21, Pallas kernels, call(): pl.pallas_call(kernel, in_specs=[vmem] * len(args), out_specs=[vmem] * le...  77.7 us
    ppermute x20, waiting for transfers between devices, swap_x(): return lax.ppermute(value, 'dp', [(i, i ^ 2) for i in range(self.dp)])  45 us
    all_to_all x7, waiting for transfers between devices, all_z(): return lax.all_to_all(value, 'tensor', 0, 0)  38.7 us
    all_to_all x7, starting transfers between devices, all_z(): return lax.all_to_all(value, 'tensor', 0, 0)  32.7 us
    pallas_call x2, Pallas kernels, attention_back(): pl.pallas_call(backward_kernel, grid=(pairs,), in_specs=[smem, pl.BlockSp...  20.8 us
    ppermute x20, starting transfers between devices, swap_x(): return lax.ppermute(value, 'dp', [(i, i ^ 2) for i in range(self.dp)])  19.8 us
    ppermute x6, waiting for transfers between devices, to_z(): return lax.ppermute(value, 'tensor', [(i, (i + k) % n) for i in range(n)])  17.6 us
    unnamed x147, local copies, waits for them, and re-layouts  16.3 us
  transfers between devices with their start and end apart: 77, of which 33 were waited for; matrix products, arithmetic and copies ran while one was open for 19% of the time, Pallas kernels for 24%

profile of v2, /device:TPU:0, one launch (start us, length us, event | category | flops | bytes accessed | tf_op | source)
XLA Modules:
  0.0 485.2 jit_solution(2770522226108925894)
XLA Ops:
  7.6 6.2 %all-to-all-start = ((bf16[4,256,512]{2,1,0:T(8,128)(2,1)}), bf16[4,256,512]{2,1,0:T(8,128)(2,1)S(1)}, u32[]{:S(2)}, u32[]{:S(2)}) async-start(bf16[4,256,512]{2,1,0:T(8,128)(2,1)} %broadcast_in_dim.51), calls=%async_computation | async-start | bytes 2097152 | tf_op jit(solution)/shard_map/all_to_all | solution.py:79
  17.4 8.8 %fusion.1.coded_ref = f32[512,1024]{1,0:T(8,128)} fusion(f32[1024]{0:T(1024)S(1)} %fusion.48, f32[512]{0:T(512)S(1)} %dynamic-slice_convert_fusion, pred[1024]{0:T(1024)(128)(4,1)S(1)} %fusion.45), kind=kLoop, calls=%fused_computation.15 | loop fusion | flops 1048576 | bytes 2104320 | tf_op jit(solution)/shard_map/jit(_where)/select_n | solution.py:926
  26.2 13.6 %all-to-all-done = bf16[4,256,512]{2,1,0:T(8,128)(2,1)S(1)} async-done(((bf16[4,256,512]{2,1,0:T(8,128)(2,1)}), bf16[4,256,512]{2,1,0:T(8,128)(2,1)S(1)}, u32[]{:S(2)}, u32[]{:S(2)}) %all-to-all-start) | async-done | bytes 1048608 | tf_op jit(solution)/shard_map/all_to_all | solution.py:79
  40.4 11.5 %all_to_all.40 = bf16[4,32,1152]{2,1,0:T(8,128)(2,1)S(1)} all-to-all(bf16[4,32,1152]{2,1,0:T(8,128)(2,1)S(1)} %broadcast_in_dim.62), channel_id=1, replica_groups=mesh['dp'=8,'tensor'=4] {'tensor'}, dimensions={0} | all-to-all | bytes 589824 | tf_op jit(solution)/shard_map/all_to_all | solution.py:79
  53.1 4.3 all-to-all-start.2
  63.4 4.2 collective-permute-done.2.refs_3_
  71.2 9.8 %all-to-all-done.2 = bf16[4,256,512]{2,1,0:T(8,128)(2,1)} async-done(((bf16[4,256,512]{2,1,0:T(8,128)(2,1)}), bf16[4,256,512]{2,1,0:T(8,128)(2,1)}, u32[]{:S(2)}, u32[]{:S(2)}) %all-to-all-start.2) | async-done | bytes 1048608 | tf_op jit(solution)/shard_map/all_to_all | solution.py:79
  81.8 4.1 all-to-all-start.3
  89.0 6.0 %all-to-all-done.3 = bf16[4,32,1152]{2,1,0:T(8,128)(2,1)} async-done(((bf16[4,32,1152]{2,1,0:T(8,128)(2,1)}), bf16[4,32,1152]{2,1,0:T(8,128)(2,1)}, u32[]{:S(2)}, u32[]{:S(2)}) %all-to-all-start.3) | async-done | bytes 294944 | tf_op jit(solution)/shard_map/all_to_all | solution.py:79
  98.8 4.4 all-to-all-start.4
  105.8 2.9 lookup.1
  116.2 2.8 start.1
  121.4 6.1 %all-to-all-done.4 = bf16[4,256,512]{2,1,0:T(8,128)(2,1)} async-done(((bf16[4,256,512]{2,1,0:T(8,128)(2,1)}), bf16[4,256,512]{2,1,0:T(8,128)(2,1)}, u32[]{:S(2)}, u32[]{:S(2)}) %all-to-all-start.4) | async-done | bytes 1048608 | tf_op jit(solution)/shard_map/all_to_all | solution.py:79
  128.9 19.9 %collective-permute-done.11.refs_4_ = bf16[256,1024]{1,0:T(8,128)(2,1)} collective-permute-done((bf16[256,1024]{1,0:T(8,128)(2,1)}, bf16[256,1024]{1,0:T(8,128)(2,1)}, u32[]{:S(2)}, u32[]{:S(2)}) %collective-permute-start.11) | collective-permute-done | bytes 524320 | tf_op jit(solution)/shard_map/ppermute | solution.py:60
  155.3 5.3 %across_plain.2 = (bf16[1024,1024]{1,0:T(8,128)(2,1)S(1)}, bf16[1024,768]{1,0:T(8,128)(2,1)S(1)}, bf16[1024,768]{1,0:T(8,128)(2,1)S(1)}) custom-call(bf16[512,1024]{1,0:T(8,128)(2,1)} %get-tuple-element.196.refs_0_, bf16[512,1024]{1,0:T(8,128)(2,1)} %collective-permute-done.13.refs_1_, bf16[2,256,1024]{2,1,0:T(8,128)(2,1)S(1)} %pad_maximum_fusion.2.refs_2_, ...), custom_call_target="tpu_custom_call" | custom-call | flops 1 | bytes 1 | tf_op jit(solution)/shard_map/across_plain/pallas_call | solution.py:419
  162.0 7.7 %attend.3 = (bf16[2,512,256]{2,1,0:T(8,128)(2,1)S(1)}, f32[2,1024,128]{2,1,0:T(8,128)S(1)}) custom-call(s32[1]{0:T(128)} %bitcast.1.c_ref, s32[1024,1]{1,0:T(8,128)S(1)} %copy-done, bf16[2,512,768]{2,1,0:T(8,128)(2,1)S(1)} %bitcast.355), custom_call_target="tpu_custom_call" | custom-call | flops 1 | bytes 1 | tf_op jit(solution)/shard_map/attend/pallas_call | solution.py:346
  171.8 8.1 %attend.2 = (bf16[2,512,256]{2,1,0:T(8,128)(2,1)S(1)}, f32[2,1024,128]{2,1,0:T(8,128)S(1)}) custom-call(s32[1]{0:T(128)} %bitcast.1.c_ref, s32[1024,1]{1,0:T(8,128)S(1)} %copy-done, bf16[2,512,768]{2,1,0:T(8,128)(2,1)S(1)} %bitcast.353), custom_call_target="tpu_custom_call" | custom-call | flops 1 | bytes 1 | tf_op jit(solution)/shard_map/attend/pallas_call | solution.py:346
  179.9 2.5 back.9.refs_1_
  185.9 2.6 collective-permute-done.18.refs_2_
  194.8 8.0 %across_gelu.1 = (bf16[1024,1024]{1,0:T(8,128)(2,1)S(1)}, bf16[1024,1024]{1,0:T(8,128)(2,1)S(1)}, bf16[1024,1024]{1,0:T(8,128)(2,1)S(1)}, bf16[1024,1024]{1,0:T(8,128)(2,1)S(1)}, bf16[1024,1024]{1,0:T(8,128)(2,1)S(1)}) custom-call(bf16[512,1024]{1,0:T(8,128)(2,1)S(1)} %get-tuple-element.211.refs_0_, bf16[512,1024]{1,0:T(8,128)(2,1)S(1)} %collective-permute-done.23.refs_1_, ...), custom_call_target="tpu_custom_call" | custom-call | flops 1 | bytes 1 | tf_op jit(solution)/shard_map/across_gelu/pallas_call | solution.py:419
  202.8 8.4 %collective-permute-done.19 = bf16[2,64,1152]{2,1,0:T(8,128)(2,1)S(1)} collective-permute-done((bf16[2,64,1152]{2,1,0:T(8,128)(2,1)S(1)}, bf16[2,64,1152]{2,1,0:T(8,128)(2,1)S(1)}, u32[]{:S(2)}, u32[]{:S(2)}) %collective-permute-start.19) | collective-permute-done | bytes 294944 | tf_op jit(solution)/shard_map/ppermute | solution.py:60
  230.9 2.7 norm_back.3
  237.6 4.5 grads.3
  249.8 4.8 across_slope.1
  254.6 4.2 back.13.refs_0_
  258.8 6.4 %back.12 = bf16[512,1024]{1,0:T(8,128)(2,1)} custom-call(bf16[1024,1024]{1,0:T(8,128)(2,1)S(1)} %get-tuple-element.240.refs_1_.refs_0_, bf16[1024,1024]{1,0:T(8,128)(2,1)S(1)} %get-tuple-element.241.refs_2_.refs_1_, bf16[2,256,1024]{2,1,0:T(8,128)(2,1)} %pad_maximum_fusion.3.refs_2_, bf16[2,256,1024]{2,1,0:T(8,128)(2,1)} %collective-permute-done.9.refs_3_, ...), custom_call_target="tpu_custom_call" | custom-call | flops 1 | bytes 1 | tf_op jit(solution)/shard_map/back/pallas_call | solution.py:419
  265.2 4.6 grads.4
  284.4 3.9 norm_back.4
  292.2 2.6 across_plain.3
  294.9 10.3 %attend_back.3 = bf16[2,512,768]{2,1,0:T(8,128)(2,1)S(1)} custom-call(s32[1]{0:T(128)} %bitcast.1.c_ref, s32[1024,1]{1,0:T(8,128)S(1)} %copy-done.1, bf16[2,512,768]{2,1,0:T(8,128)(2,1)S(1)} %bitcast.356, bf16[2,512,256]{2,1,0:T(8,128)(2,1)S(1)} %copy-done.3, bf16[2,512,256]{2,1,0:T(8,128)(2,1)S(1)} %bitcast.358, f32[2,1024,128]{2,1,0:T(8,128)S(1)} %copy-done.35), custom_call_target="tpu_custom_call" | custom-call | flops 1 | bytes 1 | tf_op jit(solution)/shard_map/attend_back/pallas_call | solution.py:378
  305.2 10.5 %attend_back.2 = bf16[2,512,768]{2,1,0:T(8,128)(2,1)S(1)} custom-call(s32[1]{0:T(128)} %bitcast.1.c_ref, s32[1024,1]{1,0:T(8,128)S(1)} %copy-done.1, bf16[2,512,768]{2,1,0:T(8,128)(2,1)S(1)} %bitcast.354, bf16[2,512,256]{2,1,0:T(8,128)(2,1)S(1)} %copy-done.5, bf16[2,512,256]{2,1,0:T(8,128)(2,1)S(1)} %bitcast.357, f32[2,1024,128]{2,1,0:T(8,128)S(1)} %copy-done.33), custom_call_target="tpu_custom_call" | custom-call | flops 1 | bytes 1 | tf_op jit(solution)/shard_map/attend_back/pallas_call | solution.py:378
  315.7 3.0 back.15.refs_0_
  318.8 3.2 back.14
  322.0 4.6 grads.5
  337.6 3.7 norm_back.5
  348.0 5.1 %all-to-all-start.5 = ((bf16[4,256,512]{2,1,0:T(8,128)(2,1)}), bf16[4,256,512]{2,1,0:T(8,128)(2,1)}, u32[]{:S(2)}, u32[]{:S(2)}) async-start(bf16[4,256,512]{2,1,0:T(8,128)(2,1)} %pad_maximum_fusion.6), calls=%async_computation.5 | async-start | bytes 2097152 | tf_op jit(solution)/shard_map/all_to_all | solution.py:79
  353.1 3.2 add_convert_fusion
  358.9 9.5 %collective-permute-done.44 = bf16[2,256,1024]{2,1,0:T(8,128)(2,1)} collective-permute-done((bf16[2,256,1024]{2,1,0:T(8,128)(2,1)}, bf16[2,256,1024]{2,1,0:T(8,128)(2,1)}, u32[]{:S(2)}, u32[]{:S(2)}) %collective-permute-start.44) | collective-permute-done | bytes 1048608 | tf_op jit(solution)/shard_map/ppermute | solution.py:60
  383.2 5.1 %all-to-all-start.6 = ((bf16[4,256,512]{2,1,0:T(8,128)(2,1)}), bf16[4,256,512]{2,1,0:T(8,128)(2,1)S(1)}, u32[]{:S(2)}, u32[]{:S(2)}) async-start(bf16[4,256,512]{2,1,0:T(8,128)(2,1)} %pad_maximum_fusion.5), calls=%async_computation.6 | async-start | bytes 2097152 | tf_op jit(solution)/shard_map/all_to_all | solution.py:79
  392.6 3.3 collective-permute-done.51
  402.9 2.7 collective-permute-done.52
  413.3 3.2 all-to-all-done.6
  416.5 3.5 all-to-all-start.7
  425.1 2.4 collective-permute-start.58
  431.2 10.6 %collective-permute-done.57 = bf16[32,1152]{1,0:T(8,128)(2,1)S(1)} collective-permute-done((bf16[32,1152]{1,0:T(8,128)(2,1)S(1)}, bf16[32,1152]{1,0:T(8,128)(2,1)S(1)}, u32[]{:S(2)}, u32[]{:S(2)}) %collective-permute-start.57) | collective-permute-done | bytes 73760 | tf_op jit(solution)/shard_map/ppermute | solution.py:76
  441.8 7.0 %collective-permute-done.58 = bf16[32,1152]{1,0:T(8,128)(2,1)S(1)} collective-permute-done((bf16[32,1152]{1,0:T(8,128)(2,1)S(1)}, bf16[32,1152]{1,0:T(8,128)(2,1)S(1)}, u32[]{:S(2)}, u32[]{:S(2)}) %collective-permute-start.58) | collective-permute-done | bytes 73760 | tf_op jit(solution)/shard_map/ppermute | solution.py:76
  471.0 2.4 collective-permute-done.66
  477.6 6.2 %adam.1 = (f32[3,128,256]{2,1,0:T(8,128)}, f32[3,128,256]{2,1,0:T(8,128)}, f32[3,128,256]{2,1,0:T(8,128)}, bf16[3,128,256]{2,1,0:T(8,128)(2,1)}, f32[256,128]{1,...) custom-call(f32[1]{0:T(128)} %bitcast.146.scale_ref, ...), custom_call_target="tpu_custom_call" | custom-call | flops 1 | bytes 1 | tf_op jit(solution)/shard_map/adam/pallas_call | solution.py:822
  (455 shorter events, 193.4 us)
Async XLA Ops:
  7.6 32.3 %all-to-all-start = ((bf16[4,256,512]{2,1,0:T(8,128)(2,1)}), bf16[4,256,512]{2,1,0:T(8,128)(2,1)S(1)}, u32[]{:S(2)}, u32[]{:S(2)}) async-start(bf16[4,256,512]{2,1,0:T(8,128)(2,1)} %broadcast_in_dim.51), calls=%async_computation | async-start | bytes 2097152 | tf_op jit(solution)/shard_map/all_to_all | solution.py:79
  53.1 27.9 %all-to-all-start.2 = ((bf16[4,256,512]{2,1,0:T(8,128)(2,1)}), bf16[4,256,512]{2,1,0:T(8,128)(2,1)}, u32[]{:S(2)}, u32[]{:S(2)}) async-start(bf16[4,256,512]{2,1,0:T(8,128)(2,1)} %broadcast_in_dim.100), calls=%async_computation.2 | async-start | bytes 2097152 | tf_op jit(solution)/shard_map/all_to_all | solution.py:79
  60.6 45.2 %collective-permute-start.4 = (bf16[2,256,1024]{2,1,0:T(8,128)(2,1)S(1)}, bf16[2,256,1024]{2,1,0:T(8,128)(2,1)S(1)}, u32[]{:S(2)}, u32[]{:S(2)}) collective-permute-start(bf16[2,256,1024]{2,1,0:T(8,128)(2,1)S(1)} %pad_maximum_fusion.2.refs_2_), channel_id=1, source_target_pairs={{0,8},{4,12},{8,0},{12,4},{16,24},{20,28},{24,16},{28,20},{1,9},{5... | collective-permute-start | bytes 3145736 | tf_op jit(solution)/shard_map/ppermute | solution.py:60
  61.2 44.6 %collective-permute-start.5 = (bf16[2,256,1024]{2,1,0:T(8,128)(2,1)S(1)}, bf16[2,256,1024]{2,1,0:T(8,128)(2,1)S(1)}, u32[]{:S(2)}, u32[]{:S(2)}) collective-permute-start(bf16[2,256,1024]{2,1,0:T(8,128)(2,1)S(1)} %pad_maximum_fusion.2.refs_2_), channel_id=1, source_target_pairs={{16,0},{20,4},{24,8},{28,12},{0,16},{4,20},{8,24},{12,28},{17,1},{... | collective-permute-start | bytes 3145736 | tf_op jit(solution)/shard_map/ppermute | solution.py:64
  70.7 35.1 %collective-permute-start.6 = (bf16[64,1152]{1,0:T(8,128)(2,1)}, bf16[64,1152]{1,0:T(8,128)(2,1)}, u32[]{:S(2)}, u32[]{:S(2)}) collective-permute-start(bf16[64,1152]{1,0:T(8,128)(2,1)} %slice_bitcast_fusion.43), channel_id=1, source_target_pairs={{0,8},{4,12},{8,0},{12,4},{16,24},{20,28},{24,16},{28,20},{1,9},{5... | collective-permute-start | bytes 442376 | tf_op jit(solution)/shard_map/ppermute | solution.py:60
  81.8 13.2 %all-to-all-start.3 = ((bf16[4,32,1152]{2,1,0:T(8,128)(2,1)}), bf16[4,32,1152]{2,1,0:T(8,128)(2,1)}, u32[]{:S(2)}, u32[]{:S(2)}) async-start(bf16[4,32,1152]{2,1,0:T(8,128)(2,1)} %broadcast_in_dim.101), calls=%async_computation.3 | async-start | bytes 589824 | tf_op jit(solution)/shard_map/all_to_all | solution.py:79
  87.5 18.3 %collective-permute-start.7 = (bf16[64,1152]{1,0:T(8,128)(2,1)}, bf16[64,1152]{1,0:T(8,128)(2,1)}, u32[]{:S(2)}, u32[]{:S(2)}) collective-permute-start(bf16[64,1152]{1,0:T(8,128)(2,1)} %slice_bitcast_fusion.42), channel_id=1, source_target_pairs={{16,0},{20,4},{24,8},{28,12},{0,16},{4,20},{8,24},{12,28},{17,1},{... | collective-permute-start | bytes 442376 | tf_op jit(solution)/shard_map/ppermute | solution.py:64
  98.8 28.6 %all-to-all-start.4 = ((bf16[4,256,512]{2,1,0:T(8,128)(2,1)}), bf16[4,256,512]{2,1,0:T(8,128)(2,1)}, u32[]{:S(2)}, u32[]{:S(2)}) async-start(bf16[4,256,512]{2,1,0:T(8,128)(2,1)} %broadcast_in_dim.102), calls=%async_computation.4 | async-start | bytes 2097152 | tf_op jit(solution)/shard_map/all_to_all | solution.py:79
  110.5 38.4 %collective-permute-start.10 = (bf16[2,256,1024]{2,1,0:T(8,128)(2,1)}, bf16[2,256,1024]{2,1,0:T(8,128)(2,1)}, u32[]{:S(2)}, u32[]{:S(2)}) collective-permute-start(bf16[2,256,1024]{2,1,0:T(8,128)(2,1)} %pad_maximum_fusion.3.refs_2_), channel_id=1, source_target_pairs={{16,0},{20,4},{24,8},{28,12},{0,16},{4,20},{8,24},{12,28},{17,1},{... | collective-permute-start | bytes 3145736 | tf_op jit(solution)/shard_map/ppermute | solution.py:64
  112.0 36.8 %collective-permute-start.9 = (bf16[2,256,1024]{2,1,0:T(8,128)(2,1)}, bf16[2,256,1024]{2,1,0:T(8,128)(2,1)}, u32[]{:S(2)}, u32[]{:S(2)}) collective-permute-start(bf16[2,256,1024]{2,1,0:T(8,128)(2,1)} %pad_maximum_fusion.3.refs_2_), channel_id=1, source_target_pairs={{0,8},{4,12},{8,0},{12,4},{16,24},{20,28},{24,16},{28,20},{1,9},{5... | collective-permute-start | bytes 3145736 | tf_op jit(solution)/shard_map/ppermute | solution.py:60
  114.3 34.5 %collective-permute-start.11 = (bf16[256,1024]{1,0:T(8,128)(2,1)}, bf16[256,1024]{1,0:T(8,128)(2,1)}, u32[]{:S(2)}, u32[]{:S(2)}) collective-permute-start(bf16[256,1024]{1,0:T(8,128)(2,1)} %slice_bitcast_fusion.5), channel_id=1, source_target_pairs={{0,8},{4,12},{8,0},{12,4},{16,24},{20,28},{24,16},{28,20},{1,9},{5... | collective-permute-start | bytes 1572872 | tf_op jit(solution)/shard_map/ppermute | solution.py:60
  115.7 33.2 %collective-permute-start.12 = (bf16[256,1024]{1,0:T(8,128)(2,1)}, bf16[256,1024]{1,0:T(8,128)(2,1)}, u32[]{:S(2)}, u32[]{:S(2)}) collective-permute-start(bf16[256,1024]{1,0:T(8,128)(2,1)} %slice_bitcast_fusion.4), channel_id=1, source_target_pairs={{16,0},{20,4},{24,8},{28,12},{0,16},{4,20},{8,24},{12,28},{17,1},{... | collective-permute-start | bytes 1572872 | tf_op jit(solution)/shard_map/ppermute | solution.py:64
  120.3 28.5 %collective-permute-start.13 = (bf16[512,1024]{1,0:T(8,128)(2,1)}, bf16[512,1024]{1,0:T(8,128)(2,1)}, u32[]{:S(2)}, u32[]{:S(2)}) collective-permute-start(bf16[512,1024]{1,0:T(8,128)(2,1)} %get-tuple-element.196.refs_0_), channel_id=1, source_target_pairs={{0,4},{4,0},{8,12},{12,8},{16,20},{20,16},{24,28},{28,24},{1,5},{5... | collective-permute-start | bytes 3145736 | tf_op jit(solution)/shard_map/ppermute | solution.py:57
  148.8 37.0 %collective-permute-start.14 = (bf16[2,256,1024]{2,1,0:T(8,128)(2,1)S(1)}, bf16[2,256,1024]{2,1,0:T(8,128)(2,1)S(1)}, u32[]{:S(2)}, u32[]{:S(2)}) collective-permute-start(bf16[2,256,1024]{2,1,0:T(8,128)(2,1)S(1)} %pad_maximum_fusion.4.refs_2_), channel_id=1, source_target_pairs={{0,8},{4,12},{8,0},{12,4},{16,24},{20,28},{24,16},{28,20},{1,9},{5... | collective-permute-start | bytes 3145736 | tf_op jit(solution)/shard_map/ppermute | solution.py:60
  150.4 35.4 %collective-permute-start.15 = (bf16[2,256,1024]{2,1,0:T(8,128)(2,1)S(1)}, bf16[2,256,1024]{2,1,0:T(8,128)(2,1)S(1)}, u32[]{:S(2)}, u32[]{:S(2)}) collective-permute-start(bf16[2,256,1024]{2,1,0:T(8,128)(2,1)S(1)} %pad_maximum_fusion.4.refs_2_), channel_id=1, source_target_pairs={{16,0},{20,4},{24,8},{28,12},{0,16},{4,20},{8,24},{12,28},{17,1},{... | collective-permute-start | bytes 3145736 | tf_op jit(solution)/shard_map/ppermute | solution.py:64
  152.0 32.6 %collective-permute-start.16 = (bf16[256,1024]{1,0:T(8,128)(2,1)S(1)}, bf16[256,1024]{1,0:T(8,128)(2,1)S(1)}, u32[]{:S(2)}, u32[]{:S(2)}) collective-permute-start(bf16[256,1024]{1,0:T(8,128)(2,1)S(1)} %slice_bitcast_fusion.3), channel_id=1, source_target_pairs={{0,8},{4,12},{8,0},{12,4},{16,24},{20,28},{24,16},{28,20},{1,9},{5... | collective-permute-start | bytes 1572872 | tf_op jit(solution)/shard_map/ppermute | solution.py:60
  153.7 32.2 %collective-permute-start.17 = (bf16[256,1024]{1,0:T(8,128)(2,1)S(1)}, bf16[256,1024]{1,0:T(8,128)(2,1)S(1)}, u32[]{:S(2)}, u32[]{:S(2)}) collective-permute-start(bf16[256,1024]{1,0:T(8,128)(2,1)S(1)} %slice_bitcast_fusion.2), channel_id=1, source_target_pairs={{16,0},{20,4},{24,8},{28,12},{0,16},{4,20},{8,24},{12,28},{17,1},{... | collective-permute-start | bytes 1572872 | tf_op jit(solution)/shard_map/ppermute | solution.py:64
  190.6 20.9 %collective-permute-start.21 = (bf16[256,1024]{1,0:T(8,128)(2,1)S(1)}, bf16[256,1024]{1,0:T(8,128)(2,1)S(1)}, u32[]{:S(2)}, u32[]{:S(2)}) collective-permute-start(bf16[256,1024]{1,0:T(8,128)(2,1)S(1)} %slice_bitcast_fusion.1), channel_id=1, source_target_pairs={{0,8},{4,12},{8,0},{12,4},{16,24},{20,28},{24,16},{28,20},{1,9},{5... | collective-permute-start | bytes 1572872 | tf_op jit(solution)/shard_map/ppermute | solution.py:60
  191.2 20.3 %collective-permute-start.22 = (bf16[256,1024]{1,0:T(8,128)(2,1)S(1)}, bf16[256,1024]{1,0:T(8,128)(2,1)S(1)}, u32[]{:S(2)}, u32[]{:S(2)}) collective-permute-start(bf16[256,1024]{1,0:T(8,128)(2,1)S(1)} %slice_bitcast_fusion), channel_id=1, source_target_pairs={{16,0},{20,4},{24,8},{28,12},{0,16},{4,20},{8,24},{12,28},{17,1},{... | collective-permute-start | bytes 1572872 | tf_op jit(solution)/shard_map/ppermute | solution.py:64
  191.9 19.3 %collective-permute-start.19 = (bf16[2,64,1152]{2,1,0:T(8,128)(2,1)S(1)}, bf16[2,64,1152]{2,1,0:T(8,128)(2,1)S(1)}, u32[]{:S(2)}, u32[]{:S(2)}) collective-permute-start(bf16[2,64,1152]{2,1,0:T(8,128)(2,1)S(1)} %pad_maximum_fusion.14), channel_id=1, source_target_pairs={{0,8},{4,12},{8,0},{12,4},{16,24},{20,28},{24,16},{28,20},{1,9},{5... | collective-permute-start | bytes 884744 | tf_op jit(solution)/shard_map/ppermute | solution.py:60
  193.3 18.1 %collective-permute-start.20 = (bf16[2,64,1152]{2,1,0:T(8,128)(2,1)S(1)}, bf16[2,64,1152]{2,1,0:T(8,128)(2,1)S(1)}, u32[]{:S(2)}, u32[]{:S(2)}) collective-permute-start(bf16[2,64,1152]{2,1,0:T(8,128)(2,1)S(1)} %pad_maximum_fusion.14), channel_id=1, source_target_pairs={{16,0},{20,4},{24,8},{28,12},{0,16},{4,20},{8,24},{12,28},{17,1},{... | collective-permute-start | bytes 884744 | tf_op jit(solution)/shard_map/ppermute | solution.py:64
  245.6 28.5 %collective-permute-start.32 = (bf16[2,256,1024]{2,1,0:T(8,128)(2,1)S(1)}, bf16[2,256,1024]{2,1,0:T(8,128)(2,1)}, u32[]{:S(2)}, u32[]{:S(2)}) collective-permute-start(bf16[2,256,1024]{2,1,0:T(8,128)(2,1)S(1)} %slice.538), channel_id=1, source_target_pairs={{0,8},{4,12},{8,0},{12,4},{16,24},{20,28},{24,16},{28,20},{1,9},{5... | collective-permute-start | bytes 3145736 | tf_op jit(solution)/shard_map/ppermute | solution.py:60
  247.1 27.0 %collective-permute-start.33 = (bf16[2,256,1024]{2,1,0:T(8,128)(2,1)S(1)}, bf16[2,256,1024]{2,1,0:T(8,128)(2,1)}, u32[]{:S(2)}, u32[]{:S(2)}) collective-permute-start(bf16[2,256,1024]{2,1,0:T(8,128)(2,1)S(1)} %slice.539), channel_id=1, source_target_pairs={{0,16},{4,20},{8,24},{12,28},{16,0},{20,4},{24,8},{28,12},{1,17},{... | collective-permute-start | bytes 3145736 | tf_op jit(solution)/shard_map/ppermute | solution.py:68
  247.8 26.3 %collective-permute-start.34 = (bf16[64,1152]{1,0:T(8,128)(2,1)S(1)}, bf16[64,1152]{1,0:T(8,128)(2,1)S(1)}, u32[]{:S(2)}, u32[]{:S(2)}) collective-permute-start(bf16[64,1152]{1,0:T(8,128)(2,1)S(1)} %get-tuple-element.332), channel_id=1, source_target_pairs={{0,16},{4,20},{8,24},{12,28},{16,0},{20,4},{24,8},{28,12},{1,17},{... | collective-permute-start | bytes 442376 | tf_op jit(solution)/shard_map/ppermute | solution.py:68
  249.3 24.8 %collective-permute-start.35 = (bf16[64,1152]{1,0:T(8,128)(2,1)S(1)}, bf16[64,1152]{1,0:T(8,128)(2,1)S(1)}, u32[]{:S(2)}, u32[]{:S(2)}) collective-permute-start(bf16[64,1152]{1,0:T(8,128)(2,1)S(1)} %get-tuple-element.331), channel_id=1, source_target_pairs={{0,8},{4,12},{8,0},{12,4},{16,24},{20,28},{24,16},{28,20},{1,9},{5... | collective-permute-start | bytes 442376 | tf_op jit(solution)/shard_map/ppermute | solution.py:60
  276.8 52.6 %collective-permute-start.39 = (bf16[256,1024]{1,0:T(8,128)(2,1)S(1)}, bf16[256,1024]{1,0:T(8,128)(2,1)S(1)}, u32[]{:S(2)}, u32[]{:S(2)}) collective-permute-start(bf16[256,1024]{1,0:T(8,128)(2,1)S(1)} %fusion.12), channel_id=1, source_target_pairs={{0,8},{4,12},{8,0},{12,4},{16,24},{20,28},{24,16},{28,20},{1,9},{5... | collective-permute-start | bytes 1572872 | tf_op jit(solution)/shard_map/ppermute | solution.py:60
  277.4 52.0 %collective-permute-start.36 = (bf16[2,256,1024]{2,1,0:T(8,128)(2,1)}, bf16[2,256,1024]{2,1,0:T(8,128)(2,1)S(1)}, u32[]{:S(2)}, u32[]{:S(2)}) collective-permute-start(bf16[2,256,1024]{2,1,0:T(8,128)(2,1)} %slice.545), channel_id=1, source_target_pairs={{0,8},{4,12},{8,0},{12,4},{16,24},{20,28},{24,16},{28,20},{1,9},{5... | collective-permute-start | bytes 3145736 | tf_op jit(solution)/shard_map/ppermute | solution.py:60
  278.9 50.6 %collective-permute-start.37 = (bf16[2,256,1024]{2,1,0:T(8,128)(2,1)}, bf16[2,256,1024]{2,1,0:T(8,128)(2,1)S(1)}, u32[]{:S(2)}, u32[]{:S(2)}) collective-permute-start(bf16[2,256,1024]{2,1,0:T(8,128)(2,1)} %slice.546), channel_id=1, source_target_pairs={{0,16},{4,20},{8,24},{12,28},{16,0},{20,4},{24,8},{28,12},{1,17},{... | collective-permute-start | bytes 3145736 | tf_op jit(solution)/shard_map/ppermute | solution.py:68
  289.6 39.8 %collective-permute-start.38 = (bf16[256,1024]{1,0:T(8,128)(2,1)S(1)}, bf16[256,1024]{1,0:T(8,128)(2,1)S(1)}, u32[]{:S(2)}, u32[]{:S(2)}) collective-permute-start(bf16[256,1024]{1,0:T(8,128)(2,1)S(1)} %fusion.11), channel_id=1, source_target_pairs={{0,16},{4,20},{8,24},{12,28},{16,0},{20,4},{24,8},{28,12},{1,17},{... | collective-permute-start | bytes 1572872 | tf_op jit(solution)/shard_map/ppermute | solution.py:68
  331.5 27.4 %collective-permute-start.47 = (bf16[256,1024]{1,0:T(8,128)(2,1)}, bf16[256,1024]{1,0:T(8,128)(2,1)}, u32[]{:S(2)}, u32[]{:S(2)}) collective-permute-start(bf16[256,1024]{1,0:T(8,128)(2,1)} %fusion.14), channel_id=1, source_target_pairs={{0,8},{4,12},{8,0},{12,4},{16,24},{20,28},{24,16},{28,20},{1,9},{5... | collective-permute-start | bytes 1572872 | tf_op jit(solution)/shard_map/ppermute | solution.py:60
  334.1 24.8 %collective-permute-start.46 = (bf16[256,1024]{1,0:T(8,128)(2,1)}, bf16[256,1024]{1,0:T(8,128)(2,1)}, u32[]{:S(2)}, u32[]{:S(2)}) collective-permute-start(bf16[256,1024]{1,0:T(8,128)(2,1)} %fusion.13), channel_id=1, source_target_pairs={{0,16},{4,20},{8,24},{12,28},{16,0},{20,4},{24,8},{28,12},{1,17},{... | collective-permute-start | bytes 1572872 | tf_op jit(solution)/shard_map/ppermute | solution.py:68
  334.7 33.7 %collective-permute-start.44 = (bf16[2,256,1024]{2,1,0:T(8,128)(2,1)}, bf16[2,256,1024]{2,1,0:T(8,128)(2,1)}, u32[]{:S(2)}, u32[]{:S(2)}) collective-permute-start(bf16[2,256,1024]{2,1,0:T(8,128)(2,1)} %slice.553), channel_id=1, source_target_pairs={{0,8},{4,12},{8,0},{12,4},{16,24},{20,28},{24,16},{28,20},{1,9},{5... | collective-permute-start | bytes 3145736 | tf_op jit(solution)/shard_map/ppermute | solution.py:60
  336.3 34.5 %collective-permute-start.45 = (bf16[2,256,1024]{2,1,0:T(8,128)(2,1)}, bf16[2,256,1024]{2,1,0:T(8,128)(2,1)}, u32[]{:S(2)}, u32[]{:S(2)}) collective-permute-start(bf16[2,256,1024]{2,1,0:T(8,128)(2,1)} %slice.554), channel_id=1, source_target_pairs={{0,16},{4,20},{8,24},{12,28},{16,0},{20,4},{24,8},{28,12},{1,17},{... | collective-permute-start | bytes 3145736 | tf_op jit(solution)/shard_map/ppermute | solution.py:68
  348.0 35.2 %all-to-all-start.5 = ((bf16[4,256,512]{2,1,0:T(8,128)(2,1)}), bf16[4,256,512]{2,1,0:T(8,128)(2,1)}, u32[]{:S(2)}, u32[]{:S(2)}) async-start(bf16[4,256,512]{2,1,0:T(8,128)(2,1)} %pad_maximum_fusion.6), calls=%async_computation.5 | async-start | bytes 2097152 | tf_op jit(solution)/shard_map/all_to_all | solution.py:79
  373.0 23.0 %collective-permute-start.49 = (bf16[256,1024]{1,0:T(8,128)(2,1)}, bf16[256,1024]{1,0:T(8,128)(2,1)}, u32[]{:S(2)}, u32[]{:S(2)}) collective-permute-start(bf16[256,1024]{1,0:T(8,128)(2,1)} %fusion.16), channel_id=1, source_target_pairs={{0,8},{4,12},{8,0},{12,4},{16,24},{20,28},{24,16},{28,20},{1,9},{5... | collective-permute-start | bytes 1572872 | tf_op jit(solution)/shard_map/ppermute | solution.py:60
  376.6 19.4 %collective-permute-start.48 = (bf16[256,1024]{1,0:T(8,128)(2,1)}, bf16[256,1024]{1,0:T(8,128)(2,1)}, u32[]{:S(2)}, u32[]{:S(2)}) collective-permute-start(bf16[256,1024]{1,0:T(8,128)(2,1)} %fusion.15), channel_id=1, source_target_pairs={{0,16},{4,20},{8,24},{12,28},{16,0},{20,4},{24,8},{28,12},{1,17},{... | collective-permute-start | bytes 1572872 | tf_op jit(solution)/shard_map/ppermute | solution.py:68
  377.3 15.3 %collective-permute-start.50 = (bf16[2,64,1152]{2,1,0:T(8,128)(2,1)}, bf16[2,64,1152]{2,1,0:T(8,128)(2,1)}, u32[]{:S(2)}, u32[]{:S(2)}) collective-permute-start(bf16[2,64,1152]{2,1,0:T(8,128)(2,1)} %get-tuple-element.275), channel_id=1, source_target_pairs={{0,8},{4,12},{8,0},{12,4},{16,24},{20,28},{24,16},{28,20},{1,9},{5... | collective-permute-start | bytes 884744 | tf_op jit(solution)/shard_map/ppermute | solution.py:60
  377.8 18.1 %collective-permute-start.51 = (bf16[2,64,1152]{2,1,0:T(8,128)(2,1)}, bf16[2,64,1152]{2,1,0:T(8,128)(2,1)}, u32[]{:S(2)}, u32[]{:S(2)}) collective-permute-start(bf16[2,64,1152]{2,1,0:T(8,128)(2,1)} %get-tuple-element.276), channel_id=1, source_target_pairs={{0,16},{4,20},{8,24},{12,28},{16,0},{20,4},{24,8},{28,12},{1,17},{... | collective-permute-start | bytes 884744 | tf_op jit(solution)/shard_map/ppermute | solution.py:68
  383.2 33.3 %all-to-all-start.6 = ((bf16[4,256,512]{2,1,0:T(8,128)(2,1)}), bf16[4,256,512]{2,1,0:T(8,128)(2,1)S(1)}, u32[]{:S(2)}, u32[]{:S(2)}) async-start(bf16[4,256,512]{2,1,0:T(8,128)(2,1)} %pad_maximum_fusion.5), calls=%async_computation.6 | async-start | bytes 2097152 | tf_op jit(solution)/shard_map/all_to_all | solution.py:79
  390.5 86.2 %collective-permute-start.69 = (f32[128,512]{1,0:T(8,128)}, f32[128,512]{1,0:T(8,128)}, u32[]{:S(2)}, u32[]{:S(2)}) collective-permute-start(f32[128,512]{1,0:T(8,128)} %get-tuple-element.368), channel_id=1, source_target_pairs={{0,4},{4,0},{8,12},{12,8},{16,20},{20,16},{24,28},{28,24},{1,5},{5... | collective-permute-start | bytes 786440 | tf_op jit(solution)/shard_map/ppermute | solution.py:57
  406.3 13.7 %collective-permute-start.53 = (bf16[32,1152]{1,0:T(8,128)(2,1)}, bf16[32,1152]{1,0:T(8,128)(2,1)}, u32[]{:S(2)}, u32[]{:S(2)}) collective-permute-start(bf16[32,1152]{1,0:T(8,128)(2,1)} %get-tuple-element.397), channel_id=1, source_target_pairs={{0,1},{1,2},{2,3},{3,0},{4,5},{5,6},{6,7},{7,4},{8,9},{9,10},{10,1... | collective-permute-start | bytes 221192 | tf_op jit(solution)/shard_map/ppermute | solution.py:76
  408.3 11.8 %collective-permute-start.54 = (bf16[32,1152]{1,0:T(8,128)(2,1)}, bf16[32,1152]{1,0:T(8,128)(2,1)}, u32[]{:S(2)}, u32[]{:S(2)}) collective-permute-start(bf16[32,1152]{1,0:T(8,128)(2,1)} %get-tuple-element.396), channel_id=1, source_target_pairs={{0,2},{1,3},{2,0},{3,1},{4,6},{5,7},{6,4},{7,5},{8,10},{9,11},{10,... | collective-permute-start | bytes 221192 | tf_op jit(solution)/shard_map/ppermute | solution.py:76
  416.5 33.8 %all-to-all-start.7 = ((bf16[4,256,512]{2,1,0:T(8,128)(2,1)}), bf16[4,256,512]{2,1,0:T(8,128)(2,1)S(1)}, u32[]{:S(2)}, u32[]{:S(2)}) async-start(bf16[4,256,512]{2,1,0:T(8,128)(2,1)} %maximum_maximum_fusion), calls=%async_computation.7 | async-start | bytes 2097152 | tf_op jit(solution)/shard_map/all_to_all | solution.py:79
  423.1 18.7 %collective-permute-start.57 = (bf16[32,1152]{1,0:T(8,128)(2,1)S(1)}, bf16[32,1152]{1,0:T(8,128)(2,1)S(1)}, u32[]{:S(2)}, u32[]{:S(2)}) collective-permute-start(bf16[32,1152]{1,0:T(8,128)(2,1)S(1)} %get-tuple-element.393), channel_id=1, source_target_pairs={{0,1},{1,2},{2,3},{3,0},{4,5},{5,6},{6,7},{7,4},{8,9},{9,10},{10,1... | collective-permute-start | bytes 221192 | tf_op jit(solution)/shard_map/ppermute | solution.py:76
  425.1 23.7 %collective-permute-start.58 = (bf16[32,1152]{1,0:T(8,128)(2,1)S(1)}, bf16[32,1152]{1,0:T(8,128)(2,1)S(1)}, u32[]{:S(2)}, u32[]{:S(2)}) collective-permute-start(bf16[32,1152]{1,0:T(8,128)(2,1)S(1)} %get-tuple-element.392), channel_id=1, source_target_pairs={{0,2},{1,3},{2,0},{3,1},{4,6},{5,7},{6,4},{7,5},{8,10},{9,11},{10,... | collective-permute-start | bytes 221192 | tf_op jit(solution)/shard_map/ppermute | solution.py:76
  427.5 21.3 %collective-permute-start.59 = (bf16[32,1152]{1,0:T(8,128)(2,1)S(1)}, bf16[32,1152]{1,0:T(8,128)(2,1)S(1)}, u32[]{:S(2)}, u32[]{:S(2)}) collective-permute-start(bf16[32,1152]{1,0:T(8,128)(2,1)S(1)} %get-tuple-element.391), channel_id=1, source_target_pairs={{0,3},{1,0},{2,1},{3,2},{4,7},{5,4},{6,5},{7,6},{8,11},{9,8},{10,9... | collective-permute-start | bytes 221192 | tf_op jit(solution)/shard_map/ppermute | solution.py:76
  429.8 46.9 %collective-permute-start.68 = (f32[128,512]{1,0:T(8,128)S(1)}, f32[128,512]{1,0:T(8,128)S(1)}, u32[]{:S(2)}, u32[]{:S(2)}) collective-permute-start(f32[128,512]{1,0:T(8,128)S(1)} %get-tuple-element.370), channel_id=1, source_target_pairs={{0,4},{4,0},{8,12},{12,8},{16,20},{20,16},{24,28},{28,24},{1,5},{5... | collective-permute-start | bytes 786440 | tf_op jit(solution)/shard_map/ppermute | solution.py:57
  454.6 22.2 %collective-permute-start.67 = (f32[128,512]{1,0:T(8,128)S(1)}, f32[128,512]{1,0:T(8,128)S(1)}, u32[]{:S(2)}, u32[]{:S(2)}) collective-permute-start(f32[128,512]{1,0:T(8,128)S(1)} %get-tuple-element.372), channel_id=1, source_target_pairs={{0,4},{4,0},{8,12},{12,8},{16,20},{20,16},{24,28},{28,24},{1,5},{5... | collective-permute-start | bytes 786440 | tf_op jit(solution)/shard_map/ppermute | solution.py:57
  (100 other events, 574.5 us)

commit v3 on v2

--- a/solution.py
+++ b/solution.py
@@ -78,6 +78,10 @@
     def all_z(self, value):
         return lax.all_to_all(value, "tensor", 0, 0)
 
+    def from_block(self, value, block):
+        (ky, kx), n = block, self.dp
+        return lax.ppermute(value, "dp", [(((i ^ (2 * kx)) + 4 * ky) % n, i) for i in range(n)])
+
     def total(self, value):
         value = value + self.swap_c(value)
         n = self.dp
@@ -128,13 +132,12 @@
 class Gather:
     def __init__(self, place, own, axis, groups=None):
         self.place, self.own, self.axis, self.groups = place, Cell(own), axis, groups
+        self.wide = Cell(jnp.broadcast_to(own[None], (place.nz,) + own.shape))
         self.ks = range(1, place.ny)
 
     def over_z(self, *after):
-        place = self.place
-        fence(self.own, *after)
-        own = self.own.v
-        self.parts = Cell(place.all_z(jnp.broadcast_to(own[None], (place.nz,) + own.shape)))
+        fence(self.wide, *after)
+        self.parts = Cell(self.place.all_z(self.wide.v))
 
     def near(self):
         place, half = self.place, self.place.nz // 2
@@ -250,6 +253,30 @@
 
     def result(self):
         return jnp.sum(self.got.v.astype(F32), 0)
+
+
+class GatherTable:
+    def __init__(self, place, own):
+        self.place, self.own = place, own
+
+    def over_z(self):
+        place, own = self.place, self.own
+        parts = [own] + [place.from_z(own, k) for k in range(1, place.nz)]
+        parts = jnp.roll(jnp.stack(parts), place.z, 0)
+        self.parts = Cell(parts.reshape(-1, own.shape[1]))
+
+    def around(self):
+        place = self.place
+
+        def take(out):
+            self.others = out
+
+        return [
+            (functools.partial(place.from_block, block=block), self.parts) for block in place.blocks[1:]
+        ], take
+
+    def arrays(self):
+        return [c.v for c in [self.parts] + self.others]
 
 
 def forward_kernel(c_ref, start_ref, qkv_ref, o_ref, lse_ref, k_s, v_s):
@@ -554,10 +581,9 @@
     codes_refs, weights, outs = refs[:2], refs[2 : 2 + count], refs[2 + count : -1]
     w_s = refs[-1]
     rows, cols = codes_refs[0].shape[0], weights[0].shape[-1]
-    size = weights[0].shape[1]
+    size = weights[0].shape[0]
     for i in range(blocks):
-        for h in range(2):
-            w_s[(2 * i + h) * size : (2 * i + h + 1) * size] = piece_at(weights, blocks, h, i)[...]
+        w_s[i * size : (i + 1) * size] = weights[i][...]
     for codes_ref, out_ref in zip(codes_refs, outs):
         hot = lax.broadcasted_iota(jnp.int32, (rows, cols), 1) == codes_ref[...]
         hot = jnp.where(hot, 1.0, 0.0).astype(BF)
@@ -567,13 +593,13 @@
 def lookup(mine, theirs, gather):
     arrays = gather.arrays()
     blocks = len(gather.place.blocks)
-    features = blocks * 2 * arrays[0].shape[1]
+    features = blocks * arrays[0].shape[0]
     shape = jax.ShapeDtypeStruct((mine.shape[0], features), BF)
     return call(
         functools.partial(lookup_kernel, blocks, len(arrays)),
         [mine, theirs, *arrays],
         [shape, shape],
-        [pltpu.VMEM((features, arrays[0].shape[2]), BF)],
+        [pltpu.VMEM((features, arrays[0].shape[1]), BF)],
         "lookup",
     )
 
@@ -760,7 +786,8 @@
         first_new = 0.5 * first_ref[at] + 0.5 * grad
         second_new = 0.5 * second_ref[at] + 0.5 * grad * grad
         master_new = master - rate * (
-            first_new / correct / (jnp.sqrt(second_new / correct) + ADAM_EPS) + decay * master
+            first_new * (1.0 / correct) / (jnp.sqrt(second_new * (1.0 / correct)) + ADAM_EPS)
+            + decay * master
         )
         for buf, value in zip(bufs[i], (master_new, first_new, second_new, master_new.astype(BF))):
             buf[at] = value
@@ -896,7 +923,7 @@
     )
     head_p = jnp.concatenate([table_t[1], jnp.zeros((thin, cols - vocab), BF)], 1)
     slots = Slots()
-    g_embed, g_head = Gather(place, embed_p, 0), Gather(place, head_p, 0)
+    g_embed, g_head = GatherTable(place, embed_p), Gather(place, head_p, 0)
 
     qkv_b, out_b, up_b, down_b = (
         v.astype(BF) for v in (qkv_master, out_master, up_master, down_master)
@@ -922,7 +949,9 @@
         chip_at[:, None] * (2 * feat) + jnp.arange(2 * feat, dtype=jnp.int32)[None, :]
     ).reshape(width)
     freqs = jnp.exp((feature // 2).astype(F32) * (-2.0 * math.log(10000.0) / width))
-    angles = my_local.astype(F32)[:, None] * freqs[None, :]
+    local_c = Cell(my_local)
+    fence(local_c, g_attn.wide)
+    angles = local_c.v.astype(F32)[:, None] * freqs[None, :]
     coded = Cell(jnp.where((feature % 2 == 0)[None, :], jnp.sin(angles), jnp.cos(angles)))
 
     def branch(lefts, gather, span):
@@ -941,23 +970,21 @@
         return jnp.concatenate([own, jnp.where(gain_codes < vocab + 3, gain_codes, -1)])[:, None]
 
     codes_c = cells(code_rows(c), code_rows(1 - c))
+    g_embed.over_z()
     g_attn.over_z()
-    slots.slot([g_attn.near], coded, g_embed.own, *codes_c)
-    g_embed.over_z()
-    g_up.over_z(g_embed.parts)
-    early = Slots()
-    early.slot([g_embed.near])
-    early.slot([g_embed.far])
-    slots.slot([g_up.near, g_attn.far], *early.flight)
-    g_head.over_z(g_up.parts)
-    g_down.over_z(g_head.parts)
+    fence(g_attn.parts, coded)
+    slots.slot([g_attn.near, g_embed.around])
+    g_up.over_z(g_attn.parts)
+    g_down.over_z(g_up.parts)
+    slots.slot([g_up.near, g_attn.far])
+    g_head.over_z(g_down.parts)
     found, found_other = lookup(codes_c[0].v, codes_c[1].v, g_embed)
     start, attn_m, gains = start_norm(nb, c_index, found, place.swap_c(found_other), coded.v)
     gains = [gains[i : i + 1] for i in range(3)]
     one_hot = (my_codes[:, None] == jnp.arange(cols, dtype=jnp.int32)[None, :]).astype(BF)
     attn_c, other_c = cells(attn_m, place.swap_c(attn_m))
 
-    slots.slot([g_down.near, g_up.far], attn_c, other_c)
+    slots.slot([g_down.near, g_up.far], attn_c, other_c, g_head.parts)
     span_qkv = (0, nz // 2 * units[0])
     span_out = (span_qkv[1], nz // 2 * edges[2])
     span_up, span_down = (0, nz // 2 * units[2]), (0, nz // 2 * units[3])

time: 491 us -> 478 us (0.974)
  blocking collectives: 11.5 us -> 0 us
    all_to_all x1 -> x0, blocking collectives: 11.5 us -> none  [all_z(): return lax.all_to_all(value, 'tensor', 0, 0)]
    ppermute x20 -> x18, waiting for transfers between devices: 45 us -> 38.6 us  [swap_x(): return lax.ppermute(value, 'dp', [(i, i ^ 2) for i in range(self.dp)])]
    ppermute x3 -> x6, starting transfers between devices: 4.16 us -> 10.3 us  [from_z(): return lax.ppermute(value, 'tensor', [((i + k) % n, i) for i in range(n)])]
    ppermute x10 -> x8, starting transfers between devices: 10.4 us -> 8.67 us  [from_y(): return lax.ppermute(value, 'dp', [((i + 4 * k) % n, i) for i in range(n)])]
    ppermute x20 -> x18, starting transfers between devices: 19.8 us -> 19.4 us  [swap_x(): return lax.ppermute(value, 'dp', [(i, i ^ 2) for i in range(self.dp)])]
    unnamed x147 -> x154, local copies, waits for them, and re-layouts: 16.3 us -> 16.5 us
  transfers between devices with their start and end apart: 77 -> 79, of which waited for: 33 -> 34; matrix products, arithmetic and copies ran while one was open for 19% -> 19% of each run, Pallas kernels for 24% -> 24%
where the time goes in v3:
time: 478 us; the launch traced here: 471 us
  waiting for transfers between devices  126 us (26%)
  Pallas kernels  122 us (26%)
  starting transfers between devices  98.3 us (21%)
  other arithmetic  57 us (12%)
  local copies, waits for them, and re-layouts  45.3 us (9%)
  between operations  11.2 us (2%)
  matrix products  10.1 us (2%)
    pallas_call x21, Pallas kernels, call(): pl.pallas_call(kernel, in_specs=[vmem] * len(args), out_specs=[vmem] * le...  76.9 us
    ppermute x18, waiting for transfers between devices, swap_x(): return lax.ppermute(value, 'dp', [(i, i ^ 2) for i in range(self.dp)])  38.6 us
    all_to_all x7, waiting for transfers between devices, all_z(): return lax.all_to_all(value, 'tensor', 0, 0)  38.4 us
    all_to_all x7, starting transfers between devices, all_z(): return lax.all_to_all(value, 'tensor', 0, 0)  30.6 us
    pallas_call x2, Pallas kernels, attention_back(): pl.pallas_call(backward_kernel, grid=(pairs,), in_specs=[smem, pl.BlockSp...  21 us
    ppermute x18, starting transfers between devices, swap_x(): return lax.ppermute(value, 'dp', [(i, i ^ 2) for i in range(self.dp)])  19.4 us
    ppermute x6, waiting for transfers between devices, to_z(): return lax.ppermute(value, 'tensor', [(i, (i + k) % n) for i in range(n)])  16.9 us
    unnamed x154, local copies, waits for them, and re-layouts  16.5 us
  transfers between devices with their start and end apart: 79, of which 34 were waited for; matrix products, arithmetic and copies ran while one was open for 19% of the time, Pallas kernels for 24%

profile of v3, /device:TPU:0, one launch (start us, length us, event | category | flops | bytes accessed | tf_op | source)
XLA Modules:
  0.0 470.7 jit_solution(16921607481251743561)
XLA Ops:
  2.7 5.1 %collective-permute-start.2 = (bf16[32,1152]{1,0:T(8,128)(2,1)S(1)}, bf16[32,1152]{1,0:T(8,128)(2,1)S(1)}, u32[]{:S(2)}, u32[]{:S(2)}) collective-permute-start(bf16[32,1152]{1,0:T(8,128)(2,1)S(1)} %concatenate.161), channel_id=1, source_target_pairs={{1,0},{2,1},{3,2},{0,3},{5,4},{6,5},{7,6},{4,7},{9,8},{10,9},{11,1... | collective-permute-start | bytes 221192 | tf_op jit(solution)/shard_map/ppermute | solution.py:72
  18.2 4.1 all-to-all-start
  22.5 8.8 %fusion.1.coded_ref = f32[512,1024]{1,0:T(8,128)} fusion(f32[1024]{0:T(1024)S(1)} %fusion.48, f32[512]{0:T(512)S(1)} %convert_element_type.434, pred[1024]{0:T(1024)(128)(4,1)S(1)} %fusion.45), kind=kLoop, calls=%fused_computation.15 | loop fusion | flops 1048576 | bytes 2104320 | tf_op jit(solution)/shard_map/jit(_where)/select_n | solution.py:955
  31.3 17.0 %all-to-all-done = bf16[4,256,512]{2,1,0:T(8,128)(2,1)S(1)} async-done(((bf16[4,256,512]{2,1,0:T(8,128)(2,1)}), bf16[4,256,512]{2,1,0:T(8,128)(2,1)S(1)}, u32[]{:S(2)}, u32[]{:S(2)}) %all-to-all-start) | async-done | bytes 1048608 | tf_op jit(solution)/shard_map/all_to_all | solution.py:79
  49.4 4.3 all-to-all-start.1
  64.3 14.7 %all-to-all-done.1 = bf16[4,256,512]{2,1,0:T(8,128)(2,1)} async-done(((bf16[4,256,512]{2,1,0:T(8,128)(2,1)}), bf16[4,256,512]{2,1,0:T(8,128)(2,1)}, u32[]{:S(2)}, u32[]{:S(2)}) %all-to-all-start.1) | async-done | bytes 1048608 | tf_op jit(solution)/shard_map/all_to_all | solution.py:79
  81.0 4.3 all-to-all-start.2
  87.8 4.5 collective-permute-done.8.refs_4_
  92.4 2.8 lookup.1
  99.0 2.8 start.1
  106.8 3.8 all-to-all-done.2
  111.3 3.7 all-to-all-start.3
  117.5 16.5 %collective-permute-done.13.refs_4_ = bf16[256,1024]{1,0:T(8,128)(2,1)} collective-permute-done((bf16[256,1024]{1,0:T(8,128)(2,1)}, bf16[256,1024]{1,0:T(8,128)(2,1)}, u32[]{:S(2)}, u32[]{:S(2)}) %collective-permute-start.13) | collective-permute-done | bytes 524320 | tf_op jit(solution)/shard_map/ppermute | solution.py:60
  141.5 5.3 %across_plain.2 = (bf16[1024,1024]{1,0:T(8,128)(2,1)S(1)}, bf16[1024,768]{1,0:T(8,128)(2,1)S(1)}, bf16[1024,768]{1,0:T(8,128)(2,1)S(1)}) custom-call(bf16[512,1024]{1,0:T(8,128)(2,1)} %get-tuple-element.198.refs_0_, bf16[512,1024]{1,0:T(8,128)(2,1)} %collective-permute-done.15.refs_1_, bf16[2,256,1024]{2,1,0:T(8,128)(2,1)S(1)} %pad_maximum_fusion.2.refs_2_, ...), custom_call_target="tpu_custom_call" | custom-call | flops 1 | bytes 1 | tf_op jit(solution)/shard_map/across_plain/pallas_call | solution.py:446
  148.1 7.7 %attend.3 = (bf16[2,512,256]{2,1,0:T(8,128)(2,1)S(1)}, f32[2,1024,128]{2,1,0:T(8,128)S(1)}) custom-call(s32[1]{0:T(128)} %bitcast.1.c_ref, s32[1024,1]{1,0:T(8,128)S(1)} %copy-done.1, bf16[2,512,768]{2,1,0:T(8,128)(2,1)S(1)} %bitcast.352), custom_call_target="tpu_custom_call" | custom-call | flops 1 | bytes 1 | tf_op jit(solution)/shard_map/attend/pallas_call | solution.py:373
  156.8 7.7 %attend.2 = (bf16[2,512,256]{2,1,0:T(8,128)(2,1)S(1)}, f32[2,1024,128]{2,1,0:T(8,128)S(1)}) custom-call(s32[1]{0:T(128)} %bitcast.1.c_ref, s32[1024,1]{1,0:T(8,128)S(1)} %copy-done.1, bf16[2,512,768]{2,1,0:T(8,128)(2,1)S(1)} %bitcast.350), custom_call_target="tpu_custom_call" | custom-call | flops 1 | bytes 1 | tf_op jit(solution)/shard_map/attend/pallas_call | solution.py:373
  164.5 2.5 back.9.refs_1_
  171.5 2.6 collective-permute-done.20.refs_2_
  180.9 8.0 %across_gelu.1 = (bf16[1024,1024]{1,0:T(8,128)(2,1)S(1)}, bf16[1024,1024]{1,0:T(8,128)(2,1)S(1)}, bf16[1024,1024]{1,0:T(8,128)(2,1)S(1)}, bf16[1024,1024]{1,0:T(8,128)(2,1)S(1)}, bf16[1024,1024]{1,0:T(8,128)(2,1)S(1)}) custom-call(bf16[512,1024]{1,0:T(8,128)(2,1)S(1)} %get-tuple-element.213.refs_0_, bf16[512,1024]{1,0:T(8,128)(2,1)S(1)} %collective-permute-done.25.refs_1_, ...), custom_call_target="tpu_custom_call" | custom-call | flops 1 | bytes 1 | tf_op jit(solution)/shard_map/across_gelu/pallas_call | solution.py:446
  188.9 8.4 %collective-permute-done.21 = bf16[2,64,1152]{2,1,0:T(8,128)(2,1)S(1)} collective-permute-done((bf16[2,64,1152]{2,1,0:T(8,128)(2,1)S(1)}, bf16[2,64,1152]{2,1,0:T(8,128)(2,1)S(1)}, u32[]{:S(2)}, u32[]{:S(2)}) %collective-permute-start.21) | collective-permute-done | bytes 294944 | tf_op jit(solution)/shard_map/ppermute | solution.py:60
  200.9 2.4 back.11
  216.8 2.9 norm_back.3
  224.7 4.5 grads.3
  236.6 4.8 %across_slope.1 = (bf16[1024,1024]{1,0:T(8,128)(2,1)}, bf16[1024,1024]{1,0:T(8,128)(2,1)S(1)}, bf16[1024,1024]{1,0:T(8,128)(2,1)S(1)}) custom-call(bf16[512,1024]{1,0:T(8,128)(2,1)S(1)} %get-tuple-element.238.refs_0_, bf16[512,1024]{1,0:T(8,128)(2,1)S(1)} %collective-permute-done.31.refs_1_, bf16[2,256,1024]{2,1,0:T(8,128)(2,1)S(1)} %copy-done, ...), custom_call_target="tpu_custom_call" | custom-call | flops 1 | bytes 1 | tf_op jit(solution)/shard_map/across_slope/pallas_call | solution.py:446
  241.4 4.2 back.13.refs_0_
  247.0 5.4 %back.12 = bf16[512,1024]{1,0:T(8,128)(2,1)} custom-call(bf16[1024,1024]{1,0:T(8,128)(2,1)S(1)} %get-tuple-element.242.refs_1_.refs_0_, bf16[1024,1024]{1,0:T(8,128)(2,1)S(1)} %get-tuple-element.243.refs_2_.refs_1_, bf16[2,256,1024]{2,1,0:T(8,128)(2,1)} %pad_maximum_fusion.3.refs_2_, bf16[2,256,1024]{2,1,0:T(8,128)(2,1)} %collective-permute-done.11.refs_3_, ...), custom_call_target="tpu_custom_call" | custom-call | flops 1 | bytes 1 | tf_op jit(solution)/shard_map/back/pallas_call | solution.py:446
  252.5 4.6 grads.4
  271.3 3.9 norm_back.4
  278.5 2.6 across_plain.3
  281.2 10.3 %attend_back.3 = bf16[2,512,768]{2,1,0:T(8,128)(2,1)S(1)} custom-call(s32[1]{0:T(128)} %bitcast.1.c_ref, s32[1024,1]{1,0:T(8,128)S(1)} %copy-done.2, bf16[2,512,768]{2,1,0:T(8,128)(2,1)S(1)} %bitcast.353, bf16[2,512,256]{2,1,0:T(8,128)(2,1)S(1)} %copy-done.4, bf16[2,512,256]{2,1,0:T(8,128)(2,1)S(1)} %bitcast.359, f32[2,1024,128]{2,1,0:T(8,128)S(1)} %copy-done.36), custom_call_target="tpu_custom_call" | custom-call | flops 1 | bytes 1 | tf_op jit(solution)/shard_map/attend_back/pallas_call | solution.py:405
  291.6 10.7 %attend_back.2 = bf16[2,512,768]{2,1,0:T(8,128)(2,1)S(1)} custom-call(s32[1]{0:T(128)} %bitcast.1.c_ref, s32[1024,1]{1,0:T(8,128)S(1)} %copy-done.2, bf16[2,512,768]{2,1,0:T(8,128)(2,1)S(1)} %bitcast.351, bf16[2,512,256]{2,1,0:T(8,128)(2,1)S(1)} %copy-done.6, bf16[2,512,256]{2,1,0:T(8,128)(2,1)S(1)} %bitcast.358, f32[2,1024,128]{2,1,0:T(8,128)S(1)} %copy-done.34), custom_call_target="tpu_custom_call" | custom-call | flops 1 | bytes 1 | tf_op jit(solution)/shard_map/attend_back/pallas_call | solution.py:405
  302.3 3.0 back.15.refs_0_
  305.3 3.2 back.14
  308.5 4.6 grads.5
  324.1 3.7 norm_back.5
  334.5 4.7 %all-to-all-start.4 = ((bf16[4,256,512]{2,1,0:T(8,128)(2,1)}), bf16[4,256,512]{2,1,0:T(8,128)(2,1)}, u32[]{:S(2)}, u32[]{:S(2)}) async-start(bf16[4,256,512]{2,1,0:T(8,128)(2,1)} %pad_maximum_fusion.6), calls=%async_computation.4 | async-start | bytes 2097152 | tf_op jit(solution)/shard_map/all_to_all | solution.py:79
  339.3 3.2 add_convert_fusion
  345.1 9.9 %collective-permute-done.46 = bf16[2,256,1024]{2,1,0:T(8,128)(2,1)} collective-permute-done((bf16[2,256,1024]{2,1,0:T(8,128)(2,1)}, bf16[2,256,1024]{2,1,0:T(8,128)(2,1)}, u32[]{:S(2)}, u32[]{:S(2)}) %collective-permute-start.46) | collective-permute-done | bytes 1048608 | tf_op jit(solution)/shard_map/ppermute | solution.py:60
  354.9 2.8 collective-permute-done.47
  370.2 4.7 %all-to-all-start.5 = ((bf16[4,256,512]{2,1,0:T(8,128)(2,1)}), bf16[4,256,512]{2,1,0:T(8,128)(2,1)S(1)}, u32[]{:S(2)}, u32[]{:S(2)}) async-start(bf16[4,256,512]{2,1,0:T(8,128)(2,1)} %pad_maximum_fusion.5), calls=%async_computation.5 | async-start | bytes 2097152 | tf_op jit(solution)/shard_map/all_to_all | solution.py:79
  379.6 2.9 collective-permute-done.53
  392.9 3.5 collective-permute-start.57
  398.6 2.9 all-to-all-done.5
  401.5 4.8 %all-to-all-start.6 = ((bf16[4,256,512]{2,1,0:T(8,128)(2,1)}), bf16[4,256,512]{2,1,0:T(8,128)(2,1)S(1)}, u32[]{:S(2)}, u32[]{:S(2)}) async-start(bf16[4,256,512]{2,1,0:T(8,128)(2,1)} %maximum_maximum_fusion), calls=%async_computation.6 | async-start | bytes 2097152 | tf_op jit(solution)/shard_map/all_to_all | solution.py:79
  417.7 9.9 %collective-permute-done.59 = bf16[32,1152]{1,0:T(8,128)(2,1)S(1)} collective-permute-done((bf16[32,1152]{1,0:T(8,128)(2,1)S(1)}, bf16[32,1152]{1,0:T(8,128)(2,1)S(1)}, u32[]{:S(2)}, u32[]{:S(2)}) %collective-permute-start.59) | collective-permute-done | bytes 73760 | tf_op jit(solution)/shard_map/ppermute | solution.py:76
  427.6 7.0 %collective-permute-done.60 = bf16[32,1152]{1,0:T(8,128)(2,1)S(1)} collective-permute-done((bf16[32,1152]{1,0:T(8,128)(2,1)S(1)}, bf16[32,1152]{1,0:T(8,128)(2,1)S(1)}, u32[]{:S(2)}, u32[]{:S(2)}) %collective-permute-start.60) | collective-permute-done | bytes 73760 | tf_op jit(solution)/shard_map/ppermute | solution.py:76
  456.6 2.4 collective-permute-done.68
  463.2 6.2 %adam.1 = (f32[3,128,256]{2,1,0:T(8,128)}, f32[3,128,256]{2,1,0:T(8,128)}, f32[3,128,256]{2,1,0:T(8,128)}, bf16[3,128,256]{2,1,0:T(8,128)(2,1)}, f32[256,128]{1,...) custom-call(f32[1]{0:T(128)} %bitcast.143.scale_ref, ...), custom_call_target="tpu_custom_call" | custom-call | flops 1 | bytes 1 | tf_op jit(solution)/shard_map/adam/pallas_call | solution.py:849
  (460 shorter events, 189.2 us)
Async XLA Ops:
  18.2 30.1 %all-to-all-start = ((bf16[4,256,512]{2,1,0:T(8,128)(2,1)}), bf16[4,256,512]{2,1,0:T(8,128)(2,1)S(1)}, u32[]{:S(2)}, u32[]{:S(2)}) async-start(bf16[4,256,512]{2,1,0:T(8,128)(2,1)} %broadcast_in_dim.56), calls=%async_computation | async-start | bytes 2097152 | tf_op jit(solution)/shard_map/all_to_all | solution.py:79
  49.4 29.6 %all-to-all-start.1 = ((bf16[4,256,512]{2,1,0:T(8,128)(2,1)}), bf16[4,256,512]{2,1,0:T(8,128)(2,1)}, u32[]{:S(2)}, u32[]{:S(2)}) async-start(bf16[4,256,512]{2,1,0:T(8,128)(2,1)} %broadcast_in_dim.94), calls=%async_computation.1 | async-start | bytes 2097152 | tf_op jit(solution)/shard_map/all_to_all | solution.py:79
  54.2 38.2 %collective-permute-start.5 = (bf16[2,256,1024]{2,1,0:T(8,128)(2,1)S(1)}, bf16[2,256,1024]{2,1,0:T(8,128)(2,1)S(1)}, u32[]{:S(2)}, u32[]{:S(2)}) collective-permute-start(bf16[2,256,1024]{2,1,0:T(8,128)(2,1)S(1)} %pad_maximum_fusion.2.refs_2_), channel_id=1, source_target_pairs={{0,8},{4,12},{8,0},{12,4},{16,24},{20,28},{24,16},{28,20},{1,9},{5... | collective-permute-start | bytes 3145736 | tf_op jit(solution)/shard_map/ppermute | solution.py:60
  55.8 36.6 %collective-permute-start.6 = (bf16[2,256,1024]{2,1,0:T(8,128)(2,1)S(1)}, bf16[2,256,1024]{2,1,0:T(8,128)(2,1)S(1)}, u32[]{:S(2)}, u32[]{:S(2)}) collective-permute-start(bf16[2,256,1024]{2,1,0:T(8,128)(2,1)S(1)} %pad_maximum_fusion.2.refs_2_), channel_id=1, source_target_pairs={{16,0},{20,4},{24,8},{28,12},{0,16},{4,20},{8,24},{12,28},{17,1},{... | collective-permute-start | bytes 3145736 | tf_op jit(solution)/shard_map/ppermute | solution.py:64
  60.8 27.0 %collective-permute-start.7 = (bf16[128,1152]{1,0:T(8,128)(2,1)S(1)}, bf16[128,1152]{1,0:T(8,128)(2,1)}, u32[]{:S(2)}, u32[]{:S(2)}) collective-permute-start(bf16[128,1152]{1,0:T(8,128)(2,1)S(1)} %bitcast.354), channel_id=1, source_target_pairs={{8,0},{12,4},{0,8},{4,12},{24,16},{28,20},{16,24},{20,28},{9,1},{1... | collective-permute-start | bytes 884744 | tf_op jit(solution)/shard_map/ppermute | solution.py:83
  61.3 30.9 %collective-permute-start.8 = (bf16[128,1152]{1,0:T(8,128)(2,1)S(1)}, bf16[128,1152]{1,0:T(8,128)(2,1)}, u32[]{:S(2)}, u32[]{:S(2)}) collective-permute-start(bf16[128,1152]{1,0:T(8,128)(2,1)S(1)} %bitcast.355), channel_id=1, source_target_pairs={{24,0},{28,4},{16,8},{20,12},{8,16},{12,20},{0,24},{4,28},{25,1},{... | collective-permute-start | bytes 884744 | tf_op jit(solution)/shard_map/ppermute | solution.py:83
  62.8 29.6 %collective-permute-start.9 = (bf16[128,1152]{1,0:T(8,128)(2,1)S(1)}, bf16[128,1152]{1,0:T(8,128)(2,1)}, u32[]{:S(2)}, u32[]{:S(2)}) collective-permute-start(bf16[128,1152]{1,0:T(8,128)(2,1)S(1)} %bitcast.356), channel_id=1, source_target_pairs={{16,0},{20,4},{24,8},{28,12},{0,16},{4,20},{8,24},{12,28},{17,1},{... | collective-permute-start | bytes 884744 | tf_op jit(solution)/shard_map/ppermute | solution.py:83
  81.0 29.5 %all-to-all-start.2 = ((bf16[4,256,512]{2,1,0:T(8,128)(2,1)}), bf16[4,256,512]{2,1,0:T(8,128)(2,1)}, u32[]{:S(2)}, u32[]{:S(2)}) async-start(bf16[4,256,512]{2,1,0:T(8,128)(2,1)} %broadcast_in_dim.93), calls=%async_computation.2 | async-start | bytes 2097152 | tf_op jit(solution)/shard_map/all_to_all | solution.py:79
  96.9 38.1 %collective-permute-start.11 = (bf16[2,256,1024]{2,1,0:T(8,128)(2,1)}, bf16[2,256,1024]{2,1,0:T(8,128)(2,1)}, u32[]{:S(2)}, u32[]{:S(2)}) collective-permute-start(bf16[2,256,1024]{2,1,0:T(8,128)(2,1)} %pad_maximum_fusion.3.refs_2_), channel_id=1, source_target_pairs={{0,8},{4,12},{8,0},{12,4},{16,24},{20,28},{24,16},{28,20},{1,9},{5... | collective-permute-start | bytes 3145736 | tf_op jit(solution)/shard_map/ppermute | solution.py:60
  98.2 36.8 %collective-permute-start.12 = (bf16[2,256,1024]{2,1,0:T(8,128)(2,1)}, bf16[2,256,1024]{2,1,0:T(8,128)(2,1)}, u32[]{:S(2)}, u32[]{:S(2)}) collective-permute-start(bf16[2,256,1024]{2,1,0:T(8,128)(2,1)} %pad_maximum_fusion.3.refs_2_), channel_id=1, source_target_pairs={{16,0},{20,4},{24,8},{28,12},{0,16},{4,20},{8,24},{12,28},{17,1},{... | collective-permute-start | bytes 3145736 | tf_op jit(solution)/shard_map/ppermute | solution.py:64
  103.1 31.9 %collective-permute-start.15 = (bf16[512,1024]{1,0:T(8,128)(2,1)}, bf16[512,1024]{1,0:T(8,128)(2,1)}, u32[]{:S(2)}, u32[]{:S(2)}) collective-permute-start(bf16[512,1024]{1,0:T(8,128)(2,1)} %get-tuple-element.198.refs_0_), channel_id=1, source_target_pairs={{0,4},{4,0},{8,12},{12,8},{16,20},{20,16},{24,28},{28,24},{1,5},{5... | collective-permute-start | bytes 3145736 | tf_op jit(solution)/shard_map/ppermute | solution.py:57
  103.9 30.1 %collective-permute-start.13 = (bf16[256,1024]{1,0:T(8,128)(2,1)}, bf16[256,1024]{1,0:T(8,128)(2,1)}, u32[]{:S(2)}, u32[]{:S(2)}) collective-permute-start(bf16[256,1024]{1,0:T(8,128)(2,1)} %slice_bitcast_fusion.5), channel_id=1, source_target_pairs={{0,8},{4,12},{8,0},{12,4},{16,24},{20,28},{24,16},{28,20},{1,9},{5... | collective-permute-start | bytes 1572872 | tf_op jit(solution)/shard_map/ppermute | solution.py:60
  106.3 28.7 %collective-permute-start.14 = (bf16[256,1024]{1,0:T(8,128)(2,1)}, bf16[256,1024]{1,0:T(8,128)(2,1)}, u32[]{:S(2)}, u32[]{:S(2)}) collective-permute-start(bf16[256,1024]{1,0:T(8,128)(2,1)} %slice_bitcast_fusion.4), channel_id=1, source_target_pairs={{16,0},{20,4},{24,8},{28,12},{0,16},{4,20},{8,24},{12,28},{17,1},{... | collective-permute-start | bytes 1572872 | tf_op jit(solution)/shard_map/ppermute | solution.py:64
  111.3 23.7 %all-to-all-start.3 = ((bf16[4,32,1152]{2,1,0:T(8,128)(2,1)}), bf16[4,32,1152]{2,1,0:T(8,128)(2,1)S(1)}, u32[]{:S(2)}, u32[]{:S(2)}) async-start(bf16[4,32,1152]{2,1,0:T(8,128)(2,1)} %broadcast_in_dim.95), calls=%async_computation.3 | async-start | bytes 589824 | tf_op jit(solution)/shard_map/all_to_all | solution.py:79
  135.0 36.5 %collective-permute-start.16 = (bf16[2,256,1024]{2,1,0:T(8,128)(2,1)}, bf16[2,256,1024]{2,1,0:T(8,128)(2,1)S(1)}, u32[]{:S(2)}, u32[]{:S(2)}) collective-permute-start(bf16[2,256,1024]{2,1,0:T(8,128)(2,1)} %pad_maximum_fusion.4.refs_2_), channel_id=1, source_target_pairs={{0,8},{4,12},{8,0},{12,4},{16,24},{20,28},{24,16},{28,20},{1,9},{5... | collective-permute-start | bytes 3145736 | tf_op jit(solution)/shard_map/ppermute | solution.py:60
  135.9 35.6 %collective-permute-start.17 = (bf16[2,256,1024]{2,1,0:T(8,128)(2,1)}, bf16[2,256,1024]{2,1,0:T(8,128)(2,1)S(1)}, u32[]{:S(2)}, u32[]{:S(2)}) collective-permute-start(bf16[2,256,1024]{2,1,0:T(8,128)(2,1)} %pad_maximum_fusion.4.refs_2_), channel_id=1, source_target_pairs={{16,0},{20,4},{24,8},{28,12},{0,16},{4,20},{8,24},{12,28},{17,1},{... | collective-permute-start | bytes 3145736 | tf_op jit(solution)/shard_map/ppermute | solution.py:64
  138.5 32.5 %collective-permute-start.18 = (bf16[256,1024]{1,0:T(8,128)(2,1)S(1)}, bf16[256,1024]{1,0:T(8,128)(2,1)S(1)}, u32[]{:S(2)}, u32[]{:S(2)}) collective-permute-start(bf16[256,1024]{1,0:T(8,128)(2,1)S(1)} %slice_bitcast_fusion.3), channel_id=1, source_target_pairs={{0,8},{4,12},{8,0},{12,4},{16,24},{20,28},{24,16},{28,20},{1,9},{5... | collective-permute-start | bytes 1572872 | tf_op jit(solution)/shard_map/ppermute | solution.py:60
  140.1 31.3 %collective-permute-start.19 = (bf16[256,1024]{1,0:T(8,128)(2,1)S(1)}, bf16[256,1024]{1,0:T(8,128)(2,1)S(1)}, u32[]{:S(2)}, u32[]{:S(2)}) collective-permute-start(bf16[256,1024]{1,0:T(8,128)(2,1)S(1)} %slice_bitcast_fusion.2), channel_id=1, source_target_pairs={{16,0},{20,4},{24,8},{28,12},{0,16},{4,20},{8,24},{12,28},{17,1},{... | collective-permute-start | bytes 1572872 | tf_op jit(solution)/shard_map/ppermute | solution.py:64
  176.7 21.7 %collective-permute-start.23 = (bf16[256,1024]{1,0:T(8,128)(2,1)S(1)}, bf16[256,1024]{1,0:T(8,128)(2,1)S(1)}, u32[]{:S(2)}, u32[]{:S(2)}) collective-permute-start(bf16[256,1024]{1,0:T(8,128)(2,1)S(1)} %slice_bitcast_fusion.1), channel_id=1, source_target_pairs={{0,8},{4,12},{8,0},{12,4},{16,24},{20,28},{24,16},{28,20},{1,9},{5... | collective-permute-start | bytes 1572872 | tf_op jit(solution)/shard_map/ppermute | solution.py:60
  178.0 20.3 %collective-permute-start.24 = (bf16[256,1024]{1,0:T(8,128)(2,1)S(1)}, bf16[256,1024]{1,0:T(8,128)(2,1)S(1)}, u32[]{:S(2)}, u32[]{:S(2)}) collective-permute-start(bf16[256,1024]{1,0:T(8,128)(2,1)S(1)} %slice_bitcast_fusion), channel_id=1, source_target_pairs={{16,0},{20,4},{24,8},{28,12},{0,16},{4,20},{8,24},{12,28},{17,1},{... | collective-permute-start | bytes 1572872 | tf_op jit(solution)/shard_map/ppermute | solution.py:64
  179.0 18.3 %collective-permute-start.21 = (bf16[2,64,1152]{2,1,0:T(8,128)(2,1)S(1)}, bf16[2,64,1152]{2,1,0:T(8,128)(2,1)S(1)}, u32[]{:S(2)}, u32[]{:S(2)}) collective-permute-start(bf16[2,64,1152]{2,1,0:T(8,128)(2,1)S(1)} %pad_maximum_fusion.13), channel_id=1, source_target_pairs={{0,8},{4,12},{8,0},{12,4},{16,24},{20,28},{24,16},{28,20},{1,9},{5... | collective-permute-start | bytes 884744 | tf_op jit(solution)/shard_map/ppermute | solution.py:60
  180.4 17.9 %collective-permute-start.22 = (bf16[2,64,1152]{2,1,0:T(8,128)(2,1)S(1)}, bf16[2,64,1152]{2,1,0:T(8,128)(2,1)S(1)}, u32[]{:S(2)}, u32[]{:S(2)}) collective-permute-start(bf16[2,64,1152]{2,1,0:T(8,128)(2,1)S(1)} %pad_maximum_fusion.13), channel_id=1, source_target_pairs={{16,0},{20,4},{24,8},{28,12},{0,16},{4,20},{8,24},{12,28},{17,1},{... | collective-permute-start | bytes 884744 | tf_op jit(solution)/shard_map/ppermute | solution.py:64
  232.4 27.9 %collective-permute-start.34 = (bf16[2,256,1024]{2,1,0:T(8,128)(2,1)S(1)}, bf16[2,256,1024]{2,1,0:T(8,128)(2,1)}, u32[]{:S(2)}, u32[]{:S(2)}) collective-permute-start(bf16[2,256,1024]{2,1,0:T(8,128)(2,1)S(1)} %slice.514), channel_id=1, source_target_pairs={{0,8},{4,12},{8,0},{12,4},{16,24},{20,28},{24,16},{28,20},{1,9},{5... | collective-permute-start | bytes 3145736 | tf_op jit(solution)/shard_map/ppermute | solution.py:60
  233.2 27.2 %collective-permute-start.35 = (bf16[2,256,1024]{2,1,0:T(8,128)(2,1)S(1)}, bf16[2,256,1024]{2,1,0:T(8,128)(2,1)}, u32[]{:S(2)}, u32[]{:S(2)}) collective-permute-start(bf16[2,256,1024]{2,1,0:T(8,128)(2,1)S(1)} %slice.515), channel_id=1, source_target_pairs={{0,16},{4,20},{8,24},{12,28},{16,0},{20,4},{24,8},{28,12},{1,17},{... | collective-permute-start | bytes 3145736 | tf_op jit(solution)/shard_map/ppermute | solution.py:68
  234.8 25.5 %collective-permute-start.36 = (bf16[64,1152]{1,0:T(8,128)(2,1)S(1)}, bf16[64,1152]{1,0:T(8,128)(2,1)S(1)}, u32[]{:S(2)}, u32[]{:S(2)}) collective-permute-start(bf16[64,1152]{1,0:T(8,128)(2,1)S(1)} %get-tuple-element.334), channel_id=1, source_target_pairs={{0,16},{4,20},{8,24},{12,28},{16,0},{20,4},{24,8},{28,12},{1,17},{... | collective-permute-start | bytes 442376 | tf_op jit(solution)/shard_map/ppermute | solution.py:68
  235.4 25.0 %collective-permute-start.37 = (bf16[64,1152]{1,0:T(8,128)(2,1)S(1)}, bf16[64,1152]{1,0:T(8,128)(2,1)S(1)}, u32[]{:S(2)}, u32[]{:S(2)}) collective-permute-start(bf16[64,1152]{1,0:T(8,128)(2,1)S(1)} %get-tuple-element.333), channel_id=1, source_target_pairs={{0,8},{4,12},{8,0},{12,4},{16,24},{20,28},{24,16},{28,20},{1,9},{5... | collective-permute-start | bytes 442376 | tf_op jit(solution)/shard_map/ppermute | solution.py:60
  263.1 52.9 %collective-permute-start.41 = (bf16[256,1024]{1,0:T(8,128)(2,1)S(1)}, bf16[256,1024]{1,0:T(8,128)(2,1)S(1)}, u32[]{:S(2)}, u32[]{:S(2)}) collective-permute-start(bf16[256,1024]{1,0:T(8,128)(2,1)S(1)} %fusion.12), channel_id=1, source_target_pairs={{0,8},{4,12},{8,0},{12,4},{16,24},{20,28},{24,16},{28,20},{1,9},{5... | collective-permute-start | bytes 1572872 | tf_op jit(solution)/shard_map/ppermute | solution.py:60
  264.2 51.8 %collective-permute-start.38 = (bf16[2,256,1024]{2,1,0:T(8,128)(2,1)}, bf16[2,256,1024]{2,1,0:T(8,128)(2,1)S(1)}, u32[]{:S(2)}, u32[]{:S(2)}) collective-permute-start(bf16[2,256,1024]{2,1,0:T(8,128)(2,1)} %slice.521), channel_id=1, source_target_pairs={{0,8},{4,12},{8,0},{12,4},{16,24},{20,28},{24,16},{28,20},{1,9},{5... | collective-permute-start | bytes 3145736 | tf_op jit(solution)/shard_map/ppermute | solution.py:60
  265.2 50.8 %collective-permute-start.39 = (bf16[2,256,1024]{2,1,0:T(8,128)(2,1)}, bf16[2,256,1024]{2,1,0:T(8,128)(2,1)S(1)}, u32[]{:S(2)}, u32[]{:S(2)}) collective-permute-start(bf16[2,256,1024]{2,1,0:T(8,128)(2,1)} %slice.522), channel_id=1, source_target_pairs={{0,16},{4,20},{8,24},{12,28},{16,0},{20,4},{24,8},{28,12},{1,17},{... | collective-permute-start | bytes 3145736 | tf_op jit(solution)/shard_map/ppermute | solution.py:68
  276.5 39.4 %collective-permute-start.40 = (bf16[256,1024]{1,0:T(8,128)(2,1)S(1)}, bf16[256,1024]{1,0:T(8,128)(2,1)S(1)}, u32[]{:S(2)}, u32[]{:S(2)}) collective-permute-start(bf16[256,1024]{1,0:T(8,128)(2,1)S(1)} %fusion.11), channel_id=1, source_target_pairs={{0,16},{4,20},{8,24},{12,28},{16,0},{20,4},{24,8},{28,12},{1,17},{... | collective-permute-start | bytes 1572872 | tf_op jit(solution)/shard_map/ppermute | solution.py:68
  318.0 27.1 %collective-permute-start.49 = (bf16[256,1024]{1,0:T(8,128)(2,1)}, bf16[256,1024]{1,0:T(8,128)(2,1)}, u32[]{:S(2)}, u32[]{:S(2)}) collective-permute-start(bf16[256,1024]{1,0:T(8,128)(2,1)} %fusion.14), channel_id=1, source_target_pairs={{0,8},{4,12},{8,0},{12,4},{16,24},{20,28},{24,16},{28,20},{1,9},{5... | collective-permute-start | bytes 1572872 | tf_op jit(solution)/shard_map/ppermute | solution.py:60
  321.1 24.0 %collective-permute-start.48 = (bf16[256,1024]{1,0:T(8,128)(2,1)}, bf16[256,1024]{1,0:T(8,128)(2,1)}, u32[]{:S(2)}, u32[]{:S(2)}) collective-permute-start(bf16[256,1024]{1,0:T(8,128)(2,1)} %fusion.13), channel_id=1, source_target_pairs={{0,16},{4,20},{8,24},{12,28},{16,0},{20,4},{24,8},{28,12},{1,17},{... | collective-permute-start | bytes 1572872 | tf_op jit(solution)/shard_map/ppermute | solution.py:68
  322.0 33.0 %collective-permute-start.46 = (bf16[2,256,1024]{2,1,0:T(8,128)(2,1)}, bf16[2,256,1024]{2,1,0:T(8,128)(2,1)}, u32[]{:S(2)}, u32[]{:S(2)}) collective-permute-start(bf16[2,256,1024]{2,1,0:T(8,128)(2,1)} %slice.529), channel_id=1, source_target_pairs={{0,8},{4,12},{8,0},{12,4},{16,24},{20,28},{24,16},{28,20},{1,9},{5... | collective-permute-start | bytes 3145736 | tf_op jit(solution)/shard_map/ppermute | solution.py:60
  323.4 34.3 %collective-permute-start.47 = (bf16[2,256,1024]{2,1,0:T(8,128)(2,1)}, bf16[2,256,1024]{2,1,0:T(8,128)(2,1)}, u32[]{:S(2)}, u32[]{:S(2)}) collective-permute-start(bf16[2,256,1024]{2,1,0:T(8,128)(2,1)} %slice.530), channel_id=1, source_target_pairs={{0,16},{4,20},{8,24},{12,28},{16,0},{20,4},{24,8},{28,12},{1,17},{... | collective-permute-start | bytes 3145736 | tf_op jit(solution)/shard_map/ppermute | solution.py:68
  334.5 35.7 %all-to-all-start.4 = ((bf16[4,256,512]{2,1,0:T(8,128)(2,1)}), bf16[4,256,512]{2,1,0:T(8,128)(2,1)}, u32[]{:S(2)}, u32[]{:S(2)}) async-start(bf16[4,256,512]{2,1,0:T(8,128)(2,1)} %pad_maximum_fusion.6), calls=%async_computation.4 | async-start | bytes 2097152 | tf_op jit(solution)/shard_map/all_to_all | solution.py:79
  359.9 22.5 %collective-permute-start.51 = (bf16[256,1024]{1,0:T(8,128)(2,1)}, bf16[256,1024]{1,0:T(8,128)(2,1)}, u32[]{:S(2)}, u32[]{:S(2)}) collective-permute-start(bf16[256,1024]{1,0:T(8,128)(2,1)} %fusion.16), channel_id=1, source_target_pairs={{0,8},{4,12},{8,0},{12,4},{16,24},{20,28},{24,16},{28,20},{1,9},{5... | collective-permute-start | bytes 1572872 | tf_op jit(solution)/shard_map/ppermute | solution.py:60
  363.1 19.4 %collective-permute-start.50 = (bf16[256,1024]{1,0:T(8,128)(2,1)}, bf16[256,1024]{1,0:T(8,128)(2,1)}, u32[]{:S(2)}, u32[]{:S(2)}) collective-permute-start(bf16[256,1024]{1,0:T(8,128)(2,1)} %fusion.15), channel_id=1, source_target_pairs={{0,16},{4,20},{8,24},{12,28},{16,0},{20,4},{24,8},{28,12},{1,17},{... | collective-permute-start | bytes 1572872 | tf_op jit(solution)/shard_map/ppermute | solution.py:68
  364.4 15.2 %collective-permute-start.52 = (bf16[2,64,1152]{2,1,0:T(8,128)(2,1)}, bf16[2,64,1152]{2,1,0:T(8,128)(2,1)}, u32[]{:S(2)}, u32[]{:S(2)}) collective-permute-start(bf16[2,64,1152]{2,1,0:T(8,128)(2,1)} %get-tuple-element.277), channel_id=1, source_target_pairs={{0,8},{4,12},{8,0},{12,4},{16,24},{20,28},{24,16},{28,20},{1,9},{5... | collective-permute-start | bytes 884744 | tf_op jit(solution)/shard_map/ppermute | solution.py:60
  365.0 17.4 %collective-permute-start.53 = (bf16[2,64,1152]{2,1,0:T(8,128)(2,1)}, bf16[2,64,1152]{2,1,0:T(8,128)(2,1)}, u32[]{:S(2)}, u32[]{:S(2)}) collective-permute-start(bf16[2,64,1152]{2,1,0:T(8,128)(2,1)} %get-tuple-element.278), channel_id=1, source_target_pairs={{0,16},{4,20},{8,24},{12,28},{16,0},{20,4},{24,8},{28,12},{1,17},{... | collective-permute-start | bytes 884744 | tf_op jit(solution)/shard_map/ppermute | solution.py:68
  370.2 31.4 %all-to-all-start.5 = ((bf16[4,256,512]{2,1,0:T(8,128)(2,1)}), bf16[4,256,512]{2,1,0:T(8,128)(2,1)S(1)}, u32[]{:S(2)}, u32[]{:S(2)}) async-start(bf16[4,256,512]{2,1,0:T(8,128)(2,1)} %pad_maximum_fusion.5), calls=%async_computation.5 | async-start | bytes 2097152 | tf_op jit(solution)/shard_map/all_to_all | solution.py:79
  377.2 85.1 %collective-permute-start.71 = (f32[128,512]{1,0:T(8,128)}, f32[128,512]{1,0:T(8,128)}, u32[]{:S(2)}, u32[]{:S(2)}) collective-permute-start(f32[128,512]{1,0:T(8,128)} %get-tuple-element.370), channel_id=1, source_target_pairs={{0,4},{4,0},{8,12},{12,8},{16,20},{20,16},{24,28},{28,24},{1,5},{5... | collective-permute-start | bytes 786440 | tf_op jit(solution)/shard_map/ppermute | solution.py:57
  392.9 13.6 %collective-permute-start.57 = (bf16[32,1152]{1,0:T(8,128)(2,1)}, bf16[32,1152]{1,0:T(8,128)(2,1)}, u32[]{:S(2)}, u32[]{:S(2)}) collective-permute-start(bf16[32,1152]{1,0:T(8,128)(2,1)} %get-tuple-element.397), channel_id=1, source_target_pairs={{0,3},{1,0},{2,1},{3,2},{4,7},{5,4},{6,5},{7,6},{8,11},{9,8},{10,9... | collective-permute-start | bytes 221192 | tf_op jit(solution)/shard_map/ppermute | solution.py:76
  401.5 34.5 %all-to-all-start.6 = ((bf16[4,256,512]{2,1,0:T(8,128)(2,1)}), bf16[4,256,512]{2,1,0:T(8,128)(2,1)S(1)}, u32[]{:S(2)}, u32[]{:S(2)}) async-start(bf16[4,256,512]{2,1,0:T(8,128)(2,1)} %maximum_maximum_fusion), calls=%async_computation.6 | async-start | bytes 2097152 | tf_op jit(solution)/shard_map/all_to_all | solution.py:79
  409.5 18.1 %collective-permute-start.59 = (bf16[32,1152]{1,0:T(8,128)(2,1)S(1)}, bf16[32,1152]{1,0:T(8,128)(2,1)S(1)}, u32[]{:S(2)}, u32[]{:S(2)}) collective-permute-start(bf16[32,1152]{1,0:T(8,128)(2,1)S(1)} %get-tuple-element.395), channel_id=1, source_target_pairs={{0,1},{1,2},{2,3},{3,0},{4,5},{5,6},{6,7},{7,4},{8,9},{9,10},{10,1... | collective-permute-start | bytes 221192 | tf_op jit(solution)/shard_map/ppermute | solution.py:76
  411.6 23.0 %collective-permute-start.60 = (bf16[32,1152]{1,0:T(8,128)(2,1)S(1)}, bf16[32,1152]{1,0:T(8,128)(2,1)S(1)}, u32[]{:S(2)}, u32[]{:S(2)}) collective-permute-start(bf16[32,1152]{1,0:T(8,128)(2,1)S(1)} %get-tuple-element.394), channel_id=1, source_target_pairs={{0,2},{1,3},{2,0},{3,1},{4,6},{5,7},{6,4},{7,5},{8,10},{9,11},{10,... | collective-permute-start | bytes 221192 | tf_op jit(solution)/shard_map/ppermute | solution.py:76
  413.9 20.6 %collective-permute-start.61 = (bf16[32,1152]{1,0:T(8,128)(2,1)S(1)}, bf16[32,1152]{1,0:T(8,128)(2,1)S(1)}, u32[]{:S(2)}, u32[]{:S(2)}) collective-permute-start(bf16[32,1152]{1,0:T(8,128)(2,1)S(1)} %get-tuple-element.393), channel_id=1, source_target_pairs={{0,3},{1,0},{2,1},{3,2},{4,7},{5,4},{6,5},{7,6},{8,11},{9,8},{10,9... | collective-permute-start | bytes 221192 | tf_op jit(solution)/shard_map/ppermute | solution.py:76
  416.3 46.0 %collective-permute-start.70 = (f32[128,512]{1,0:T(8,128)S(1)}, f32[128,512]{1,0:T(8,128)S(1)}, u32[]{:S(2)}, u32[]{:S(2)}) collective-permute-start(f32[128,512]{1,0:T(8,128)S(1)} %get-tuple-element.372), channel_id=1, source_target_pairs={{0,4},{4,0},{8,12},{12,8},{16,20},{20,16},{24,28},{28,24},{1,5},{5... | collective-permute-start | bytes 786440 | tf_op jit(solution)/shard_map/ppermute | solution.py:57
  440.3 22.0 %collective-permute-start.69 = (f32[128,512]{1,0:T(8,128)S(1)}, f32[128,512]{1,0:T(8,128)S(1)}, u32[]{:S(2)}, u32[]{:S(2)}) collective-permute-start(f32[128,512]{1,0:T(8,128)S(1)} %get-tuple-element.374), channel_id=1, source_target_pairs={{0,4},{4,0},{8,12},{12,8},{16,20},{20,16},{24,28},{28,24},{1,5},{5... | collective-permute-start | bytes 786440 | tf_op jit(solution)/shard_map/ppermute | solution.py:57
  (102 other events, 624.8 us)

commit v4 on v3

--- a/solution.py
+++ b/solution.py
@@ -1065,10 +1065,11 @@
         for q, o, g, ls in zip(qkv, mixed, grad_mixed, lse)
     ]
     r_attn = matrix_sum((attn_in, grad_qkv), (grad_out, mixed))
+    grad_qkv_c = cells(*grad_qkv)
     theirs_c = Cell(back(grad_qkv, g_attn, span_qkv, half_rows, half_rows, BF))
-    mine_c = Cell(back(grad_qkv, g_attn, span_qkv, 0, half_rows, F32))
-
-    slots.slot([r_attn.near, r_up.far], theirs_c, mine_c)
+
+    slots.slot([r_attn.near, r_up.far], theirs_c, *grad_qkv_c)
+    mine_c = Cell(back([v.v for v in grad_qkv_c], g_attn, span_qkv, 0, half_rows, F32))
     r_down.over_z()
     grad_start, _, gain_one = norm_back(
         [mine_c.v, place.swap_c(theirs_c.v)], [grad_mid], start, gains[0]

time: 478 us -> 476 us (level)
    unnamed x154 -> x136, local copies, waits for them, and re-layouts: 16.5 us -> 15.7 us
  transfers between devices with their start and end apart: 79 -> 79, of which waited for: 34 -> 34; matrix products, arithmetic and copies ran while one was open for 19% -> 18% of each run, Pallas kernels for 24% -> 24%
where the time goes in v4:
time: 476 us; the launch traced here: 469 us
  waiting for transfers between devices  127 us (27%)
  Pallas kernels  122 us (26%)
  starting transfers between devices  98 us (21%)
  other arithmetic  58.4 us (12%)
  local copies, waits for them, and re-layouts  44.4 us (9%)
  between operations  11.1 us (2%)
  matrix products  7.82 us (2%)
    pallas_call x21, Pallas kernels, call(): pl.pallas_call(kernel, in_specs=[vmem] * len(args), out_specs=[vmem] * le...  76.9 us
    all_to_all x7, waiting for transfers between devices, all_z(): return lax.all_to_all(value, 'tensor', 0, 0)  41.2 us
    ppermute x18, waiting for transfers between devices, swap_x(): return lax.ppermute(value, 'dp', [(i, i ^ 2) for i in range(self.dp)])  37.6 us
    all_to_all x7, starting transfers between devices, all_z(): return lax.all_to_all(value, 'tensor', 0, 0)  29.3 us
    pallas_call x2, Pallas kernels, attention_back(): pl.pallas_call(backward_kernel, grid=(pairs,), in_specs=[smem, pl.BlockSp...  21 us
    ppermute x18, starting transfers between devices, swap_x(): return lax.ppermute(value, 'dp', [(i, i ^ 2) for i in range(self.dp)])  19.3 us
    ppermute x6, waiting for transfers between devices, to_z(): return lax.ppermute(value, 'tensor', [(i, (i + k) % n) for i in range(n)])  16.5 us
    unnamed x136, local copies, waits for them, and re-layouts  15.7 us
  transfers between devices with their start and end apart: 79, of which 34 were waited for; matrix products, arithmetic and copies ran while one was open for 18% of the time, Pallas kernels for 24%

profile of v4, /device:TPU:0, one launch (start us, length us, event | category | flops | bytes accessed | tf_op | source)
XLA Modules:
  0.0 468.9 jit_solution(10420756194623912462)
XLA Ops:
  2.7 5.1 %collective-permute-start.2 = (bf16[32,1152]{1,0:T(8,128)(2,1)S(1)}, bf16[32,1152]{1,0:T(8,128)(2,1)S(1)}, u32[]{:S(2)}, u32[]{:S(2)}) collective-permute-start(bf16[32,1152]{1,0:T(8,128)(2,1)S(1)} %concatenate.161), channel_id=1, source_target_pairs={{1,0},{2,1},{3,2},{0,3},{5,4},{6,5},{7,6},{4,7},{9,8},{10,9},{11,1... | collective-permute-start | bytes 221192 | tf_op jit(solution)/shard_map/ppermute | solution.py:72
  18.2 4.1 all-to-all-start
  22.5 8.8 %fusion.1.coded_ref = f32[512,1024]{1,0:T(8,128)} fusion(f32[1024]{0:T(1024)S(1)} %fusion.48, f32[512]{0:T(512)S(1)} %convert_element_type.434, pred[1024]{0:T(1024)(128)(4,1)S(1)} %fusion.45), kind=kLoop, calls=%fused_computation.15 | loop fusion | flops 1048576 | bytes 2104320 | tf_op jit(solution)/shard_map/jit(_where)/select_n | solution.py:955
  31.3 17.0 %all-to-all-done = bf16[4,256,512]{2,1,0:T(8,128)(2,1)S(1)} async-done(((bf16[4,256,512]{2,1,0:T(8,128)(2,1)}), bf16[4,256,512]{2,1,0:T(8,128)(2,1)S(1)}, u32[]{:S(2)}, u32[]{:S(2)}) %all-to-all-start) | async-done | bytes 1048608 | tf_op jit(solution)/shard_map/all_to_all | solution.py:79
  49.4 4.2 all-to-all-start.1
  64.3 14.7 %all-to-all-done.1 = bf16[4,256,512]{2,1,0:T(8,128)(2,1)} async-done(((bf16[4,256,512]{2,1,0:T(8,128)(2,1)}), bf16[4,256,512]{2,1,0:T(8,128)(2,1)}, u32[]{:S(2)}, u32[]{:S(2)}) %all-to-all-start.1) | async-done | bytes 1048608 | tf_op jit(solution)/shard_map/all_to_all | solution.py:79
  81.0 4.3 all-to-all-start.2
  87.8 4.5 collective-permute-done.8.refs_4_
  92.4 2.8 lookup.1
  99.0 2.8 start.1
  106.8 3.8 all-to-all-done.2
  111.3 3.7 all-to-all-start.3
  117.4 16.6 %collective-permute-done.13.refs_4_ = bf16[256,1024]{1,0:T(8,128)(2,1)} collective-permute-done((bf16[256,1024]{1,0:T(8,128)(2,1)}, bf16[256,1024]{1,0:T(8,128)(2,1)}, u32[]{:S(2)}, u32[]{:S(2)}) %collective-permute-start.13) | collective-permute-done | bytes 524320 | tf_op jit(solution)/shard_map/ppermute | solution.py:60
  141.5 5.3 %across_plain.2 = (bf16[1024,1024]{1,0:T(8,128)(2,1)S(1)}, bf16[1024,768]{1,0:T(8,128)(2,1)S(1)}, bf16[1024,768]{1,0:T(8,128)(2,1)S(1)}) custom-call(bf16[512,1024]{1,0:T(8,128)(2,1)} %get-tuple-element.199.refs_0_, bf16[512,1024]{1,0:T(8,128)(2,1)} %collective-permute-done.15.refs_1_, bf16[2,256,1024]{2,1,0:T(8,128)(2,1)S(1)} %pad_maximum_fusion.2.refs_2_, ...), custom_call_target="tpu_custom_call" | custom-call | flops 1 | bytes 1 | tf_op jit(solution)/shard_map/across_plain/pallas_call | solution.py:446
  148.2 7.7 %attend.3 = (bf16[2,512,256]{2,1,0:T(8,128)(2,1)S(1)}, f32[2,1024,128]{2,1,0:T(8,128)S(1)}) custom-call(s32[1]{0:T(128)} %bitcast.1.c_ref, s32[1024,1]{1,0:T(8,128)S(1)} %copy-done.1, bf16[2,512,768]{2,1,0:T(8,128)(2,1)S(1)} %bitcast.352), custom_call_target="tpu_custom_call" | custom-call | flops 1 | bytes 1 | tf_op jit(solution)/shard_map/attend/pallas_call | solution.py:373
  156.9 7.7 %attend.2 = (bf16[2,512,256]{2,1,0:T(8,128)(2,1)S(1)}, f32[2,1024,128]{2,1,0:T(8,128)S(1)}) custom-call(s32[1]{0:T(128)} %bitcast.1.c_ref, s32[1024,1]{1,0:T(8,128)S(1)} %copy-done.1, bf16[2,512,768]{2,1,0:T(8,128)(2,1)S(1)} %bitcast.350), custom_call_target="tpu_custom_call" | custom-call | flops 1 | bytes 1 | tf_op jit(solution)/shard_map/attend/pallas_call | solution.py:373
  164.6 2.5 back.9.refs_1_
  171.5 2.6 collective-permute-done.20.refs_2_
  180.9 8.0 %across_gelu.1 = (bf16[1024,1024]{1,0:T(8,128)(2,1)S(1)}, bf16[1024,1024]{1,0:T(8,128)(2,1)S(1)}, bf16[1024,1024]{1,0:T(8,128)(2,1)S(1)}, bf16[1024,1024]{1,0:T(8,128)(2,1)S(1)}, bf16[1024,1024]{1,0:T(8,128)(2,1)S(1)}) custom-call(bf16[512,1024]{1,0:T(8,128)(2,1)S(1)} %get-tuple-element.214.refs_0_, bf16[512,1024]{1,0:T(8,128)(2,1)S(1)} %collective-permute-done.25.refs_1_, ...), custom_call_target="tpu_custom_call" | custom-call | flops 1 | bytes 1 | tf_op jit(solution)/shard_map/across_gelu/pallas_call | solution.py:446
  188.9 8.4 %collective-permute-done.21 = bf16[2,64,1152]{2,1,0:T(8,128)(2,1)S(1)} collective-permute-done((bf16[2,64,1152]{2,1,0:T(8,128)(2,1)S(1)}, bf16[2,64,1152]{2,1,0:T(8,128)(2,1)S(1)}, u32[]{:S(2)}, u32[]{:S(2)}) %collective-permute-start.21) | collective-permute-done | bytes 294944 | tf_op jit(solution)/shard_map/ppermute | solution.py:60
  200.9 2.4 back.11
  216.8 2.9 norm_back.3
  224.7 4.5 grads.3
  236.6 4.8 %across_slope.1 = (bf16[1024,1024]{1,0:T(8,128)(2,1)}, bf16[1024,1024]{1,0:T(8,128)(2,1)S(1)}, bf16[1024,1024]{1,0:T(8,128)(2,1)S(1)}) custom-call(bf16[512,1024]{1,0:T(8,128)(2,1)S(1)} %get-tuple-element.239.refs_0_, bf16[512,1024]{1,0:T(8,128)(2,1)S(1)} %collective-permute-done.31.refs_1_, bf16[2,256,1024]{2,1,0:T(8,128)(2,1)S(1)} %copy-done, ...), custom_call_target="tpu_custom_call" | custom-call | flops 1 | bytes 1 | tf_op jit(solution)/shard_map/across_slope/pallas_call | solution.py:446
  241.4 4.2 back.13.refs_0_
  247.0 5.4 %back.12 = bf16[512,1024]{1,0:T(8,128)(2,1)} custom-call(bf16[1024,1024]{1,0:T(8,128)(2,1)S(1)} %get-tuple-element.243.refs_1_.refs_0_, bf16[1024,1024]{1,0:T(8,128)(2,1)S(1)} %get-tuple-element.244.refs_2_.refs_1_, bf16[2,256,1024]{2,1,0:T(8,128)(2,1)} %pad_maximum_fusion.3.refs_2_, bf16[2,256,1024]{2,1,0:T(8,128)(2,1)} %collective-permute-done.11.refs_3_, ...), custom_call_target="tpu_custom_call" | custom-call | flops 1 | bytes 1 | tf_op jit(solution)/shard_map/back/pallas_call | solution.py:446
  252.4 4.6 grads.4
  271.3 3.9 norm_back.4
  278.4 2.6 across_plain.3
  281.1 10.3 %attend_back.3 = bf16[2,512,768]{2,1,0:T(8,128)(2,1)S(1)} custom-call(s32[1]{0:T(128)} %bitcast.1.c_ref, s32[1024,1]{1,0:T(8,128)S(1)} %copy-done.2, bf16[2,512,768]{2,1,0:T(8,128)(2,1)S(1)} %bitcast.353, bf16[2,512,256]{2,1,0:T(8,128)(2,1)S(1)} %copy-done.4, bf16[2,512,256]{2,1,0:T(8,128)(2,1)S(1)} %bitcast.359, f32[2,1024,128]{2,1,0:T(8,128)S(1)} %copy-done.36), custom_call_target="tpu_custom_call" | custom-call | flops 1 | bytes 1 | tf_op jit(solution)/shard_map/attend_back/pallas_call | solution.py:405
  291.5 10.7 %attend_back.2 = bf16[2,512,768]{2,1,0:T(8,128)(2,1)S(1)} custom-call(s32[1]{0:T(128)} %bitcast.1.c_ref, s32[1024,1]{1,0:T(8,128)S(1)} %copy-done.2, bf16[2,512,768]{2,1,0:T(8,128)(2,1)S(1)} %bitcast.351, bf16[2,512,256]{2,1,0:T(8,128)(2,1)S(1)} %copy-done.6, bf16[2,512,256]{2,1,0:T(8,128)(2,1)S(1)} %bitcast.358, f32[2,1024,128]{2,1,0:T(8,128)S(1)} %copy-done.34), custom_call_target="tpu_custom_call" | custom-call | flops 1 | bytes 1 | tf_op jit(solution)/shard_map/attend_back/pallas_call | solution.py:405
  302.2 3.2 back.14
  305.4 4.6 grads.5
  322.1 3.0 back.15.refs_0_
  325.2 3.7 norm_back.5
  334.4 4.7 %all-to-all-start.4 = ((bf16[4,256,512]{2,1,0:T(8,128)(2,1)}), bf16[4,256,512]{2,1,0:T(8,128)(2,1)}, u32[]{:S(2)}, u32[]{:S(2)}) async-start(bf16[4,256,512]{2,1,0:T(8,128)(2,1)} %pad_maximum_fusion.6), calls=%async_computation.4 | async-start | bytes 2097152 | tf_op jit(solution)/shard_map/all_to_all | solution.py:79
  343.8 9.0 %collective-permute-done.46 = bf16[2,256,1024]{2,1,0:T(8,128)(2,1)} collective-permute-done((bf16[2,256,1024]{2,1,0:T(8,128)(2,1)}, bf16[2,256,1024]{2,1,0:T(8,128)(2,1)}, u32[]{:S(2)}, u32[]{:S(2)}) %collective-permute-start.46) | collective-permute-done | bytes 1048608 | tf_op jit(solution)/shard_map/ppermute | solution.py:60
  352.9 2.9 collective-permute-done.47
  368.2 4.8 %all-to-all-start.5 = ((bf16[4,256,512]{2,1,0:T(8,128)(2,1)}), bf16[4,256,512]{2,1,0:T(8,128)(2,1)}, u32[]{:S(2)}, u32[]{:S(2)}) async-start(bf16[4,256,512]{2,1,0:T(8,128)(2,1)} %pad_maximum_fusion.5), calls=%async_computation.5 | async-start | bytes 2097152 | tf_op jit(solution)/shard_map/all_to_all | solution.py:79
  377.4 2.8 collective-permute-done.53
  389.8 3.6 collective-permute-start.57
  395.6 5.7 %all-to-all-done.5 = bf16[4,256,512]{2,1,0:T(8,128)(2,1)} async-done(((bf16[4,256,512]{2,1,0:T(8,128)(2,1)}), bf16[4,256,512]{2,1,0:T(8,128)(2,1)}, u32[]{:S(2)}, u32[]{:S(2)}) %all-to-all-start.5) | async-done | bytes 1048608 | tf_op jit(solution)/shard_map/all_to_all | solution.py:79
  401.2 3.5 all-to-all-start.6
  408.9 2.4 collective-permute-start.60
  416.3 9.5 %collective-permute-done.59 = bf16[32,1152]{1,0:T(8,128)(2,1)S(1)} collective-permute-done((bf16[32,1152]{1,0:T(8,128)(2,1)S(1)}, bf16[32,1152]{1,0:T(8,128)(2,1)S(1)}, u32[]{:S(2)}, u32[]{:S(2)}) %collective-permute-start.59) | collective-permute-done | bytes 73760 | tf_op jit(solution)/shard_map/ppermute | solution.py:76
  425.8 7.0 %collective-permute-done.60 = bf16[32,1152]{1,0:T(8,128)(2,1)S(1)} collective-permute-done((bf16[32,1152]{1,0:T(8,128)(2,1)S(1)}, bf16[32,1152]{1,0:T(8,128)(2,1)S(1)}, u32[]{:S(2)}, u32[]{:S(2)}) %collective-permute-start.60) | collective-permute-done | bytes 73760 | tf_op jit(solution)/shard_map/ppermute | solution.py:76
  454.8 2.4 collective-permute-done.68
  461.4 6.2 %adam.1 = (f32[3,128,256]{2,1,0:T(8,128)}, f32[3,128,256]{2,1,0:T(8,128)}, f32[3,128,256]{2,1,0:T(8,128)}, bf16[3,128,256]{2,1,0:T(8,128)(2,1)}, f32[256,128]{1,...) custom-call(f32[1]{0:T(128)} %bitcast.143.scale_ref, ...), custom_call_target="tpu_custom_call" | custom-call | flops 1 | bytes 1 | tf_op jit(solution)/shard_map/adam/pallas_call | solution.py:849
  (442 shorter events, 188.1 us)
Async XLA Ops:
  18.2 30.1 %all-to-all-start = ((bf16[4,256,512]{2,1,0:T(8,128)(2,1)}), bf16[4,256,512]{2,1,0:T(8,128)(2,1)S(1)}, u32[]{:S(2)}, u32[]{:S(2)}) async-start(bf16[4,256,512]{2,1,0:T(8,128)(2,1)} %broadcast_in_dim.56), calls=%async_computation | async-start | bytes 2097152 | tf_op jit(solution)/shard_map/all_to_all | solution.py:79
  49.4 29.6 %all-to-all-start.1 = ((bf16[4,256,512]{2,1,0:T(8,128)(2,1)}), bf16[4,256,512]{2,1,0:T(8,128)(2,1)}, u32[]{:S(2)}, u32[]{:S(2)}) async-start(bf16[4,256,512]{2,1,0:T(8,128)(2,1)} %broadcast_in_dim.94), calls=%async_computation.1 | async-start | bytes 2097152 | tf_op jit(solution)/shard_map/all_to_all | solution.py:79
  54.2 38.2 %collective-permute-start.5 = (bf16[2,256,1024]{2,1,0:T(8,128)(2,1)S(1)}, bf16[2,256,1024]{2,1,0:T(8,128)(2,1)S(1)}, u32[]{:S(2)}, u32[]{:S(2)}) collective-permute-start(bf16[2,256,1024]{2,1,0:T(8,128)(2,1)S(1)} %pad_maximum_fusion.2.refs_2_), channel_id=1, source_target_pairs={{0,8},{4,12},{8,0},{12,4},{16,24},{20,28},{24,16},{28,20},{1,9},{5... | collective-permute-start | bytes 3145736 | tf_op jit(solution)/shard_map/ppermute | solution.py:60
  55.8 36.6 %collective-permute-start.6 = (bf16[2,256,1024]{2,1,0:T(8,128)(2,1)S(1)}, bf16[2,256,1024]{2,1,0:T(8,128)(2,1)S(1)}, u32[]{:S(2)}, u32[]{:S(2)}) collective-permute-start(bf16[2,256,1024]{2,1,0:T(8,128)(2,1)S(1)} %pad_maximum_fusion.2.refs_2_), channel_id=1, source_target_pairs={{16,0},{20,4},{24,8},{28,12},{0,16},{4,20},{8,24},{12,28},{17,1},{... | collective-permute-start | bytes 3145736 | tf_op jit(solution)/shard_map/ppermute | solution.py:64
  60.8 27.0 %collective-permute-start.7 = (bf16[128,1152]{1,0:T(8,128)(2,1)S(1)}, bf16[128,1152]{1,0:T(8,128)(2,1)}, u32[]{:S(2)}, u32[]{:S(2)}) collective-permute-start(bf16[128,1152]{1,0:T(8,128)(2,1)S(1)} %bitcast.354), channel_id=1, source_target_pairs={{8,0},{12,4},{0,8},{4,12},{24,16},{28,20},{16,24},{20,28},{9,1},{1... | collective-permute-start | bytes 884744 | tf_op jit(solution)/shard_map/ppermute | solution.py:83
  61.3 30.9 %collective-permute-start.8 = (bf16[128,1152]{1,0:T(8,128)(2,1)S(1)}, bf16[128,1152]{1,0:T(8,128)(2,1)}, u32[]{:S(2)}, u32[]{:S(2)}) collective-permute-start(bf16[128,1152]{1,0:T(8,128)(2,1)S(1)} %bitcast.355), channel_id=1, source_target_pairs={{24,0},{28,4},{16,8},{20,12},{8,16},{12,20},{0,24},{4,28},{25,1},{... | collective-permute-start | bytes 884744 | tf_op jit(solution)/shard_map/ppermute | solution.py:83
  62.8 29.6 %collective-permute-start.9 = (bf16[128,1152]{1,0:T(8,128)(2,1)S(1)}, bf16[128,1152]{1,0:T(8,128)(2,1)}, u32[]{:S(2)}, u32[]{:S(2)}) collective-permute-start(bf16[128,1152]{1,0:T(8,128)(2,1)S(1)} %bitcast.356), channel_id=1, source_target_pairs={{16,0},{20,4},{24,8},{28,12},{0,16},{4,20},{8,24},{12,28},{17,1},{... | collective-permute-start | bytes 884744 | tf_op jit(solution)/shard_map/ppermute | solution.py:83
  81.0 29.5 %all-to-all-start.2 = ((bf16[4,256,512]{2,1,0:T(8,128)(2,1)}), bf16[4,256,512]{2,1,0:T(8,128)(2,1)}, u32[]{:S(2)}, u32[]{:S(2)}) async-start(bf16[4,256,512]{2,1,0:T(8,128)(2,1)} %broadcast_in_dim.93), calls=%async_computation.2 | async-start | bytes 2097152 | tf_op jit(solution)/shard_map/all_to_all | solution.py:79
  96.9 38.1 %collective-permute-start.11 = (bf16[2,256,1024]{2,1,0:T(8,128)(2,1)}, bf16[2,256,1024]{2,1,0:T(8,128)(2,1)}, u32[]{:S(2)}, u32[]{:S(2)}) collective-permute-start(bf16[2,256,1024]{2,1,0:T(8,128)(2,1)} %pad_maximum_fusion.3.refs_2_), channel_id=1, source_target_pairs={{0,8},{4,12},{8,0},{12,4},{16,24},{20,28},{24,16},{28,20},{1,9},{5... | collective-permute-start | bytes 3145736 | tf_op jit(solution)/shard_map/ppermute | solution.py:60
  98.2 36.8 %collective-permute-start.12 = (bf16[2,256,1024]{2,1,0:T(8,128)(2,1)}, bf16[2,256,1024]{2,1,0:T(8,128)(2,1)}, u32[]{:S(2)}, u32[]{:S(2)}) collective-permute-start(bf16[2,256,1024]{2,1,0:T(8,128)(2,1)} %pad_maximum_fusion.3.refs_2_), channel_id=1, source_target_pairs={{16,0},{20,4},{24,8},{28,12},{0,16},{4,20},{8,24},{12,28},{17,1},{... | collective-permute-start | bytes 3145736 | tf_op jit(solution)/shard_map/ppermute | solution.py:64
  103.1 31.9 %collective-permute-start.15 = (bf16[512,1024]{1,0:T(8,128)(2,1)}, bf16[512,1024]{1,0:T(8,128)(2,1)}, u32[]{:S(2)}, u32[]{:S(2)}) collective-permute-start(bf16[512,1024]{1,0:T(8,128)(2,1)} %get-tuple-element.199.refs_0_), channel_id=1, source_target_pairs={{0,4},{4,0},{8,12},{12,8},{16,20},{20,16},{24,28},{28,24},{1,5},{5... | collective-permute-start | bytes 3145736 | tf_op jit(solution)/shard_map/ppermute | solution.py:57
  103.9 30.1 %collective-permute-start.13 = (bf16[256,1024]{1,0:T(8,128)(2,1)}, bf16[256,1024]{1,0:T(8,128)(2,1)}, u32[]{:S(2)}, u32[]{:S(2)}) collective-permute-start(bf16[256,1024]{1,0:T(8,128)(2,1)} %slice_bitcast_fusion.5), channel_id=1, source_target_pairs={{0,8},{4,12},{8,0},{12,4},{16,24},{20,28},{24,16},{28,20},{1,9},{5... | collective-permute-start | bytes 1572872 | tf_op jit(solution)/shard_map/ppermute | solution.py:60
  106.3 28.7 %collective-permute-start.14 = (bf16[256,1024]{1,0:T(8,128)(2,1)}, bf16[256,1024]{1,0:T(8,128)(2,1)}, u32[]{:S(2)}, u32[]{:S(2)}) collective-permute-start(bf16[256,1024]{1,0:T(8,128)(2,1)} %slice_bitcast_fusion.4), channel_id=1, source_target_pairs={{16,0},{20,4},{24,8},{28,12},{0,16},{4,20},{8,24},{12,28},{17,1},{... | collective-permute-start | bytes 1572872 | tf_op jit(solution)/shard_map/ppermute | solution.py:64
  111.3 23.7 %all-to-all-start.3 = ((bf16[4,32,1152]{2,1,0:T(8,128)(2,1)}), bf16[4,32,1152]{2,1,0:T(8,128)(2,1)S(1)}, u32[]{:S(2)}, u32[]{:S(2)}) async-start(bf16[4,32,1152]{2,1,0:T(8,128)(2,1)} %broadcast_in_dim.95), calls=%async_computation.3 | async-start | bytes 589824 | tf_op jit(solution)/shard_map/all_to_all | solution.py:79
  135.0 36.5 %collective-permute-start.16 = (bf16[2,256,1024]{2,1,0:T(8,128)(2,1)}, bf16[2,256,1024]{2,1,0:T(8,128)(2,1)S(1)}, u32[]{:S(2)}, u32[]{:S(2)}) collective-permute-start(bf16[2,256,1024]{2,1,0:T(8,128)(2,1)} %pad_maximum_fusion.4.refs_2_), channel_id=1, source_target_pairs={{0,8},{4,12},{8,0},{12,4},{16,24},{20,28},{24,16},{28,20},{1,9},{5... | collective-permute-start | bytes 3145736 | tf_op jit(solution)/shard_map/ppermute | solution.py:60
  135.9 35.6 %collective-permute-start.17 = (bf16[2,256,1024]{2,1,0:T(8,128)(2,1)}, bf16[2,256,1024]{2,1,0:T(8,128)(2,1)S(1)}, u32[]{:S(2)}, u32[]{:S(2)}) collective-permute-start(bf16[2,256,1024]{2,1,0:T(8,128)(2,1)} %pad_maximum_fusion.4.refs_2_), channel_id=1, source_target_pairs={{16,0},{20,4},{24,8},{28,12},{0,16},{4,20},{8,24},{12,28},{17,1},{... | collective-permute-start | bytes 3145736 | tf_op jit(solution)/shard_map/ppermute | solution.py:64
  138.5 32.5 %collective-permute-start.18 = (bf16[256,1024]{1,0:T(8,128)(2,1)S(1)}, bf16[256,1024]{1,0:T(8,128)(2,1)S(1)}, u32[]{:S(2)}, u32[]{:S(2)}) collective-permute-start(bf16[256,1024]{1,0:T(8,128)(2,1)S(1)} %slice_bitcast_fusion.3), channel_id=1, source_target_pairs={{0,8},{4,12},{8,0},{12,4},{16,24},{20,28},{24,16},{28,20},{1,9},{5... | collective-permute-start | bytes 1572872 | tf_op jit(solution)/shard_map/ppermute | solution.py:60
  140.1 31.3 %collective-permute-start.19 = (bf16[256,1024]{1,0:T(8,128)(2,1)S(1)}, bf16[256,1024]{1,0:T(8,128)(2,1)S(1)}, u32[]{:S(2)}, u32[]{:S(2)}) collective-permute-start(bf16[256,1024]{1,0:T(8,128)(2,1)S(1)} %slice_bitcast_fusion.2), channel_id=1, source_target_pairs={{16,0},{20,4},{24,8},{28,12},{0,16},{4,20},{8,24},{12,28},{17,1},{... | collective-permute-start | bytes 1572872 | tf_op jit(solution)/shard_map/ppermute | solution.py:64
  176.7 21.7 %collective-permute-start.23 = (bf16[256,1024]{1,0:T(8,128)(2,1)S(1)}, bf16[256,1024]{1,0:T(8,128)(2,1)S(1)}, u32[]{:S(2)}, u32[]{:S(2)}) collective-permute-start(bf16[256,1024]{1,0:T(8,128)(2,1)S(1)} %slice_bitcast_fusion.1), channel_id=1, source_target_pairs={{0,8},{4,12},{8,0},{12,4},{16,24},{20,28},{24,16},{28,20},{1,9},{5... | collective-permute-start | bytes 1572872 | tf_op jit(solution)/shard_map/ppermute | solution.py:60
  178.0 20.3 %collective-permute-start.24 = (bf16[256,1024]{1,0:T(8,128)(2,1)S(1)}, bf16[256,1024]{1,0:T(8,128)(2,1)S(1)}, u32[]{:S(2)}, u32[]{:S(2)}) collective-permute-start(bf16[256,1024]{1,0:T(8,128)(2,1)S(1)} %slice_bitcast_fusion), channel_id=1, source_target_pairs={{16,0},{20,4},{24,8},{28,12},{0,16},{4,20},{8,24},{12,28},{17,1},{... | collective-permute-start | bytes 1572872 | tf_op jit(solution)/shard_map/ppermute | solution.py:64
  179.0 18.3 %collective-permute-start.21 = (bf16[2,64,1152]{2,1,0:T(8,128)(2,1)S(1)}, bf16[2,64,1152]{2,1,0:T(8,128)(2,1)S(1)}, u32[]{:S(2)}, u32[]{:S(2)}) collective-permute-start(bf16[2,64,1152]{2,1,0:T(8,128)(2,1)S(1)} %pad_maximum_fusion.13), channel_id=1, source_target_pairs={{0,8},{4,12},{8,0},{12,4},{16,24},{20,28},{24,16},{28,20},{1,9},{5... | collective-permute-start | bytes 884744 | tf_op jit(solution)/shard_map/ppermute | solution.py:60
  180.4 17.9 %collective-permute-start.22 = (bf16[2,64,1152]{2,1,0:T(8,128)(2,1)S(1)}, bf16[2,64,1152]{2,1,0:T(8,128)(2,1)S(1)}, u32[]{:S(2)}, u32[]{:S(2)}) collective-permute-start(bf16[2,64,1152]{2,1,0:T(8,128)(2,1)S(1)} %pad_maximum_fusion.13), channel_id=1, source_target_pairs={{16,0},{20,4},{24,8},{28,12},{0,16},{4,20},{8,24},{12,28},{17,1},{... | collective-permute-start | bytes 884744 | tf_op jit(solution)/shard_map/ppermute | solution.py:64
  232.4 27.8 %collective-permute-start.34 = (bf16[2,256,1024]{2,1,0:T(8,128)(2,1)S(1)}, bf16[2,256,1024]{2,1,0:T(8,128)(2,1)}, u32[]{:S(2)}, u32[]{:S(2)}) collective-permute-start(bf16[2,256,1024]{2,1,0:T(8,128)(2,1)S(1)} %slice.514), channel_id=1, source_target_pairs={{0,8},{4,12},{8,0},{12,4},{16,24},{20,28},{24,16},{28,20},{1,9},{5... | collective-permute-start | bytes 3145736 | tf_op jit(solution)/shard_map/ppermute | solution.py:60
  233.2 27.1 %collective-permute-start.35 = (bf16[2,256,1024]{2,1,0:T(8,128)(2,1)S(1)}, bf16[2,256,1024]{2,1,0:T(8,128)(2,1)}, u32[]{:S(2)}, u32[]{:S(2)}) collective-permute-start(bf16[2,256,1024]{2,1,0:T(8,128)(2,1)S(1)} %slice.515), channel_id=1, source_target_pairs={{0,16},{4,20},{8,24},{12,28},{16,0},{20,4},{24,8},{28,12},{1,17},{... | collective-permute-start | bytes 3145736 | tf_op jit(solution)/shard_map/ppermute | solution.py:68
  234.8 25.4 %collective-permute-start.36 = (bf16[64,1152]{1,0:T(8,128)(2,1)S(1)}, bf16[64,1152]{1,0:T(8,128)(2,1)S(1)}, u32[]{:S(2)}, u32[]{:S(2)}) collective-permute-start(bf16[64,1152]{1,0:T(8,128)(2,1)S(1)} %get-tuple-element.336), channel_id=1, source_target_pairs={{0,16},{4,20},{8,24},{12,28},{16,0},{20,4},{24,8},{28,12},{1,17},{... | collective-permute-start | bytes 442376 | tf_op jit(solution)/shard_map/ppermute | solution.py:68
  235.4 24.9 %collective-permute-start.37 = (bf16[64,1152]{1,0:T(8,128)(2,1)S(1)}, bf16[64,1152]{1,0:T(8,128)(2,1)S(1)}, u32[]{:S(2)}, u32[]{:S(2)}) collective-permute-start(bf16[64,1152]{1,0:T(8,128)(2,1)S(1)} %get-tuple-element.335), channel_id=1, source_target_pairs={{0,8},{4,12},{8,0},{12,4},{16,24},{20,28},{24,16},{28,20},{1,9},{5... | collective-permute-start | bytes 442376 | tf_op jit(solution)/shard_map/ppermute | solution.py:60
  263.0 49.6 %collective-permute-start.41 = (bf16[256,1024]{1,0:T(8,128)(2,1)S(1)}, bf16[256,1024]{1,0:T(8,128)(2,1)S(1)}, u32[]{:S(2)}, u32[]{:S(2)}) collective-permute-start(bf16[256,1024]{1,0:T(8,128)(2,1)S(1)} %fusion.12), channel_id=1, source_target_pairs={{0,8},{4,12},{8,0},{12,4},{16,24},{20,28},{24,16},{28,20},{1,9},{5... | collective-permute-start | bytes 1572872 | tf_op jit(solution)/shard_map/ppermute | solution.py:60
  264.2 48.4 %collective-permute-start.38 = (bf16[2,256,1024]{2,1,0:T(8,128)(2,1)}, bf16[2,256,1024]{2,1,0:T(8,128)(2,1)S(1)}, u32[]{:S(2)}, u32[]{:S(2)}) collective-permute-start(bf16[2,256,1024]{2,1,0:T(8,128)(2,1)} %slice.521), channel_id=1, source_target_pairs={{0,8},{4,12},{8,0},{12,4},{16,24},{20,28},{24,16},{28,20},{1,9},{5... | collective-permute-start | bytes 3145736 | tf_op jit(solution)/shard_map/ppermute | solution.py:60
  265.1 47.5 %collective-permute-start.39 = (bf16[2,256,1024]{2,1,0:T(8,128)(2,1)}, bf16[2,256,1024]{2,1,0:T(8,128)(2,1)S(1)}, u32[]{:S(2)}, u32[]{:S(2)}) collective-permute-start(bf16[2,256,1024]{2,1,0:T(8,128)(2,1)} %slice.522), channel_id=1, source_target_pairs={{0,16},{4,20},{8,24},{12,28},{16,0},{20,4},{24,8},{28,12},{1,17},{... | collective-permute-start | bytes 3145736 | tf_op jit(solution)/shard_map/ppermute | solution.py:68
  276.5 36.0 %collective-permute-start.40 = (bf16[256,1024]{1,0:T(8,128)(2,1)S(1)}, bf16[256,1024]{1,0:T(8,128)(2,1)S(1)}, u32[]{:S(2)}, u32[]{:S(2)}) collective-permute-start(bf16[256,1024]{1,0:T(8,128)(2,1)S(1)} %fusion.11), channel_id=1, source_target_pairs={{0,16},{4,20},{8,24},{12,28},{16,0},{20,4},{24,8},{28,12},{1,17},{... | collective-permute-start | bytes 1572872 | tf_op jit(solution)/shard_map/ppermute | solution.py:68
  316.0 27.8 %collective-permute-start.49 = (bf16[256,1024]{1,0:T(8,128)(2,1)}, bf16[256,1024]{1,0:T(8,128)(2,1)}, u32[]{:S(2)}, u32[]{:S(2)}) collective-permute-start(bf16[256,1024]{1,0:T(8,128)(2,1)} %fusion.14), channel_id=1, source_target_pairs={{0,8},{4,12},{8,0},{12,4},{16,24},{20,28},{24,16},{28,20},{1,9},{5... | collective-permute-start | bytes 1572872 | tf_op jit(solution)/shard_map/ppermute | solution.py:60
  319.2 24.7 %collective-permute-start.48 = (bf16[256,1024]{1,0:T(8,128)(2,1)}, bf16[256,1024]{1,0:T(8,128)(2,1)}, u32[]{:S(2)}, u32[]{:S(2)}) collective-permute-start(bf16[256,1024]{1,0:T(8,128)(2,1)} %fusion.13), channel_id=1, source_target_pairs={{0,16},{4,20},{8,24},{12,28},{16,0},{20,4},{24,8},{28,12},{1,17},{... | collective-permute-start | bytes 1572872 | tf_op jit(solution)/shard_map/ppermute | solution.py:68
  320.1 32.8 %collective-permute-start.46 = (bf16[2,256,1024]{2,1,0:T(8,128)(2,1)}, bf16[2,256,1024]{2,1,0:T(8,128)(2,1)}, u32[]{:S(2)}, u32[]{:S(2)}) collective-permute-start(bf16[2,256,1024]{2,1,0:T(8,128)(2,1)} %slice.529), channel_id=1, source_target_pairs={{0,8},{4,12},{8,0},{12,4},{16,24},{20,28},{24,16},{28,20},{1,9},{5... | collective-permute-start | bytes 3145736 | tf_op jit(solution)/shard_map/ppermute | solution.py:60
  321.5 34.3 %collective-permute-start.47 = (bf16[2,256,1024]{2,1,0:T(8,128)(2,1)}, bf16[2,256,1024]{2,1,0:T(8,128)(2,1)}, u32[]{:S(2)}, u32[]{:S(2)}) collective-permute-start(bf16[2,256,1024]{2,1,0:T(8,128)(2,1)} %slice.530), channel_id=1, source_target_pairs={{0,16},{4,20},{8,24},{12,28},{16,0},{20,4},{24,8},{28,12},{1,17},{... | collective-permute-start | bytes 3145736 | tf_op jit(solution)/shard_map/ppermute | solution.py:68
  334.4 33.8 %all-to-all-start.4 = ((bf16[4,256,512]{2,1,0:T(8,128)(2,1)}), bf16[4,256,512]{2,1,0:T(8,128)(2,1)}, u32[]{:S(2)}, u32[]{:S(2)}) async-start(bf16[4,256,512]{2,1,0:T(8,128)(2,1)} %pad_maximum_fusion.6), calls=%async_computation.4 | async-start | bytes 2097152 | tf_op jit(solution)/shard_map/all_to_all | solution.py:79
  357.8 22.4 %collective-permute-start.51 = (bf16[256,1024]{1,0:T(8,128)(2,1)}, bf16[256,1024]{1,0:T(8,128)(2,1)}, u32[]{:S(2)}, u32[]{:S(2)}) collective-permute-start(bf16[256,1024]{1,0:T(8,128)(2,1)} %fusion.16), channel_id=1, source_target_pairs={{0,8},{4,12},{8,0},{12,4},{16,24},{20,28},{24,16},{28,20},{1,9},{5... | collective-permute-start | bytes 1572872 | tf_op jit(solution)/shard_map/ppermute | solution.py:60
  360.9 19.3 %collective-permute-start.50 = (bf16[256,1024]{1,0:T(8,128)(2,1)}, bf16[256,1024]{1,0:T(8,128)(2,1)}, u32[]{:S(2)}, u32[]{:S(2)}) collective-permute-start(bf16[256,1024]{1,0:T(8,128)(2,1)} %fusion.15), channel_id=1, source_target_pairs={{0,16},{4,20},{8,24},{12,28},{16,0},{20,4},{24,8},{28,12},{1,17},{... | collective-permute-start | bytes 1572872 | tf_op jit(solution)/shard_map/ppermute | solution.py:68
  362.3 15.1 %collective-permute-start.52 = (bf16[2,64,1152]{2,1,0:T(8,128)(2,1)}, bf16[2,64,1152]{2,1,0:T(8,128)(2,1)}, u32[]{:S(2)}, u32[]{:S(2)}) collective-permute-start(bf16[2,64,1152]{2,1,0:T(8,128)(2,1)} %get-tuple-element.279), channel_id=1, source_target_pairs={{0,8},{4,12},{8,0},{12,4},{16,24},{20,28},{24,16},{28,20},{1,9},{5... | collective-permute-start | bytes 884744 | tf_op jit(solution)/shard_map/ppermute | solution.py:60
  362.9 17.3 %collective-permute-start.53 = (bf16[2,64,1152]{2,1,0:T(8,128)(2,1)}, bf16[2,64,1152]{2,1,0:T(8,128)(2,1)}, u32[]{:S(2)}, u32[]{:S(2)}) collective-permute-start(bf16[2,64,1152]{2,1,0:T(8,128)(2,1)} %get-tuple-element.280), channel_id=1, source_target_pairs={{0,16},{4,20},{8,24},{12,28},{16,0},{20,4},{24,8},{28,12},{1,17},{... | collective-permute-start | bytes 884744 | tf_op jit(solution)/shard_map/ppermute | solution.py:68
  368.2 33.0 %all-to-all-start.5 = ((bf16[4,256,512]{2,1,0:T(8,128)(2,1)}), bf16[4,256,512]{2,1,0:T(8,128)(2,1)}, u32[]{:S(2)}, u32[]{:S(2)}) async-start(bf16[4,256,512]{2,1,0:T(8,128)(2,1)} %pad_maximum_fusion.5), calls=%async_computation.5 | async-start | bytes 2097152 | tf_op jit(solution)/shard_map/all_to_all | solution.py:79
  375.2 85.3 %collective-permute-start.71 = (f32[128,512]{1,0:T(8,128)}, f32[128,512]{1,0:T(8,128)S(1)}, u32[]{:S(2)}, u32[]{:S(2)}) collective-permute-start(f32[128,512]{1,0:T(8,128)} %get-tuple-element.372), channel_id=1, source_target_pairs={{0,4},{4,0},{8,12},{12,8},{16,20},{20,16},{24,28},{28,24},{1,5},{5... | collective-permute-start | bytes 786440 | tf_op jit(solution)/shard_map/ppermute | solution.py:57
  389.8 15.1 %collective-permute-start.57 = (bf16[32,1152]{1,0:T(8,128)(2,1)S(1)}, bf16[32,1152]{1,0:T(8,128)(2,1)S(1)}, u32[]{:S(2)}, u32[]{:S(2)}) collective-permute-start(bf16[32,1152]{1,0:T(8,128)(2,1)S(1)} %get-tuple-element.399), channel_id=1, source_target_pairs={{0,3},{1,0},{2,1},{3,2},{4,7},{5,4},{6,5},{7,6},{8,11},{9,8},{10,9... | collective-permute-start | bytes 221192 | tf_op jit(solution)/shard_map/ppermute | solution.py:76
  401.2 33.0 %all-to-all-start.6 = ((bf16[4,256,512]{2,1,0:T(8,128)(2,1)}), bf16[4,256,512]{2,1,0:T(8,128)(2,1)S(1)}, u32[]{:S(2)}, u32[]{:S(2)}) async-start(bf16[4,256,512]{2,1,0:T(8,128)(2,1)} %maximum_maximum_fusion), calls=%async_computation.6 | async-start | bytes 2097152 | tf_op jit(solution)/shard_map/all_to_all | solution.py:79
  406.9 18.9 %collective-permute-start.59 = (bf16[32,1152]{1,0:T(8,128)(2,1)S(1)}, bf16[32,1152]{1,0:T(8,128)(2,1)S(1)}, u32[]{:S(2)}, u32[]{:S(2)}) collective-permute-start(bf16[32,1152]{1,0:T(8,128)(2,1)S(1)} %get-tuple-element.397), channel_id=1, source_target_pairs={{0,1},{1,2},{2,3},{3,0},{4,5},{5,6},{6,7},{7,4},{8,9},{9,10},{10,1... | collective-permute-start | bytes 221192 | tf_op jit(solution)/shard_map/ppermute | solution.py:76
  408.9 23.9 %collective-permute-start.60 = (bf16[32,1152]{1,0:T(8,128)(2,1)S(1)}, bf16[32,1152]{1,0:T(8,128)(2,1)S(1)}, u32[]{:S(2)}, u32[]{:S(2)}) collective-permute-start(bf16[32,1152]{1,0:T(8,128)(2,1)S(1)} %get-tuple-element.396), channel_id=1, source_target_pairs={{0,2},{1,3},{2,0},{3,1},{4,6},{5,7},{6,4},{7,5},{8,10},{9,11},{10,... | collective-permute-start | bytes 221192 | tf_op jit(solution)/shard_map/ppermute | solution.py:76
  411.3 21.5 %collective-permute-start.61 = (bf16[32,1152]{1,0:T(8,128)(2,1)S(1)}, bf16[32,1152]{1,0:T(8,128)(2,1)S(1)}, u32[]{:S(2)}, u32[]{:S(2)}) collective-permute-start(bf16[32,1152]{1,0:T(8,128)(2,1)S(1)} %get-tuple-element.395), channel_id=1, source_target_pairs={{0,3},{1,0},{2,1},{3,2},{4,7},{5,4},{6,5},{7,6},{8,11},{9,8},{10,9... | collective-permute-start | bytes 221192 | tf_op jit(solution)/shard_map/ppermute | solution.py:76
  414.9 45.6 %collective-permute-start.70 = (f32[128,512]{1,0:T(8,128)S(1)}, f32[128,512]{1,0:T(8,128)S(1)}, u32[]{:S(2)}, u32[]{:S(2)}) collective-permute-start(f32[128,512]{1,0:T(8,128)S(1)} %get-tuple-element.374), channel_id=1, source_target_pairs={{0,4},{4,0},{8,12},{12,8},{16,20},{20,16},{24,28},{28,24},{1,5},{5... | collective-permute-start | bytes 786440 | tf_op jit(solution)/shard_map/ppermute | solution.py:57
  438.5 22.0 %collective-permute-start.69 = (f32[128,512]{1,0:T(8,128)S(1)}, f32[128,512]{1,0:T(8,128)S(1)}, u32[]{:S(2)}, u32[]{:S(2)}) collective-permute-start(f32[128,512]{1,0:T(8,128)S(1)} %get-tuple-element.376), channel_id=1, source_target_pairs={{0,4},{4,0},{8,12},{12,8},{16,20},{20,16},{24,28},{28,24},{1,5},{5... | collective-permute-start | bytes 786440 | tf_op jit(solution)/shard_map/ppermute | solution.py:57
  (93 other events, 602.1 us)
